TPU v7x, 32 devices: a whole 2x2x4 slice. The times are simulated.
32 devices in a mesh: grp: 4 (over z), mem: 8 (over y, x, core).
Axes of the slice: x: 2, y: 2, z: 4, core: 2. Of those that a mesh axis runs over, the one named last changes fastest.
Arguments:
- forcing: float32 [3, 256, 4096], P(None, ('grp', 'mem')), may hold values from -6 to 6
- viscosity: float32 [256, 4096], P(('grp', 'mem')), may hold values from 0.1 to 10
- refinement: int32 [256], P(('grp', 'mem')), may hold values from 0 to 1
- face_owner: int32 [1024, 1], P(('grp', 'mem')), may hold values from 0 to 7; in each aligned block of 32 rows (0 to 31, 32 to 63, ...) at most 8 rows name the same one
- face_block: int32 [256, 4], P(('grp', 'mem')), may hold values from 0 to 7
- plane_block: int32 [256, 2], P(('grp', 'mem')), may hold values from 0 to 7
- hanging: int32 [256, 6], P(('grp', 'mem')), may hold values 0 or 1
- coarse_solver: float32 [4, 192, 192], P('grp', 'mem'), may hold values from -0.4375 to 0.4375
Outputs:
- velocity: float32 [3, 256, 4096], P(None, ('grp', 'mem'))
- residual: float32 [3, 256, 4096], P(None, ('grp', 'mem'))
Inputs may be any that keep to these rules, and one draw needn't show every extreme that they name: `face_owner`: among the 32 rows of one device no member appears more than 8 times, and some member appears exactly 8 times.
All inputs are finite; a program needn't handle non-finite values. No bound on the sum of `hanging` on one device may be relied on, other than what follows from the above.
Results may differ from a plain program's by a relative error of at most 0.0001.
Values sent between devices are 32-bit elements; how exact they have to be, the bound alone decides.
No kernel may reach another device: no remote copies, remote signals or barrier semaphores. Data moves between devices by JAX's collectives and lax.ppermute only.
A program may use at most 64 MiB of HBM per device.

v0:
```python
import functools
import math

import jax
import jax.numpy as jnp
from jax import lax
from jax.experimental import pallas as pl
from jax.experimental.pallas import tpu as pltpu
from jax.sharding import PartitionSpec as P

EDGE = 16
DEG = 3
CELLS = 4096
MASS_TERM = 1.0
LOWER_BOUND = 0.25
UPPER_BOUND = 2.0
THETA = 0.5 * (UPPER_BOUND + LOWER_BOUND)
DELTA = 0.5 * (UPPER_BOUND - LOWER_BOUND)
SIGMA = THETA / DELTA

LANES = 128
BLK = 8
TILES = CELLS // LANES
F32 = jnp.float32
VMEM = pl.BlockSpec(memory_space=pltpu.VMEM)
SMEM = pl.BlockSpec(memory_space=pltpu.SMEM)
PARAMS = pltpu.CompilerParams(vmem_limit_bytes=28 * 1024 * 1024)


def lane_id():
    return lax.broadcasted_iota(jnp.int32, (BLK, LANES), 1)


def sub_id():
    return lax.broadcasted_iota(jnp.int32, (BLK, LANES), 0)


def roll(v, shift):
    shift = shift % LANES
    return v if shift == 0 else pltpu.roll(v, shift, 1)


def tile(m):
    return slice(m * LANES, (m + 1) * LANES)


def pack_faces(values, lane):
    k, g = lane & 15, lane >> 4
    faces = [[], [], [], []]
    for p in range(2):
        low = high = None
        for t in range(16):
            moved = roll(values[16 * p + t], t)
            low = moved if t == 0 else jnp.where(k == t, moved, low)
            high = moved if t == 0 else jnp.where(k == (15 + t) % 16, moved, high)
        faces[0].append(low)
        faces[1].append(roll(high, -15))
        low = high = None
        for t in range(8):
            i = 8 * p + t
            first = roll(values[2 * i], 16 * t)
            last = roll(values[2 * i + 1], 16 * t + 16)
            low = first if t == 0 else jnp.where(g == t, first, low)
            high = last if t == 0 else jnp.where(g == t, last, high)
        faces[2].append(low)
        faces[3].append(high)
    return faces


def mean_squares(v, lane, bit):
    for n in (bit, 16):
        v = v + jnp.where((lane & n) == 0, roll(v, -n), roll(v, n))
    return v * 0.25


def unpack_k(low, high, lane, m):
    t = m % 16
    return jnp.where((lane & 15) == 0, roll(low[m // 16], -t), roll(high[m // 16], 15 - t))


def unpack_j(low, high, m):
    i = m // 2
    if m % 2 == 0:
        return roll(low[i // 8], -16 * (i % 8))
    return roll(high[i // 8], 112 - 16 * (i % 8))


def gather_ghosts(starts, stride, near, first, second, meta, plane_block, hanging, ghosts, planes, lane, rows):
    even = meta[0] == 1
    has_lower, has_upper = meta[1] == 1, meta[2] == 1
    for n in range(rows):
        span = slice(n * BLK, (n + 1) * BLK)
        a, b = first[span, :], second[span, :]
        planes[span, :] = jnp.where(has_lower, jnp.where(even, b, a), 0.0)
        span_up = slice((rows + n) * BLK, (rows + n + 1) * BLK)
        planes[span_up, :] = jnp.where(has_upper, jnp.where(even, a, b), 0.0)
    for b in range(BLK):
        for d in range(4):
            row = near[pl.ds(starts(b, d), rows, stride=stride), :]
            ghosts[pl.ds(d * rows * BLK + b, rows, stride=BLK), :] = row
        for d in range(2):
            row = planes[pl.ds(d * rows * BLK + plane_block[b, d], rows, stride=BLK), :]
            ghosts[pl.ds((4 + d) * rows * BLK + b, rows, stride=BLK), :] = row
    result = []
    for d in range(6):
        hang = jnp.broadcast_to(hanging[:, d : d + 1], (BLK, LANES)) == 1
        tiles = []
        for n in range(rows):
            v = ghosts[(d * rows + n) * BLK : (d * rows + n + 1) * BLK, :]
            tiles.append(jnp.where(hang, mean_squares(v, lane, 2 if d < 2 else 1), v))
        result.append(tiles)
    return result


def emit_planes(low, high, even, first, second):
    for n in range(len(low)):
        span = slice(n * BLK, (n + 1) * BLK)
        first[span, :] = jnp.where(even, high[n], low[n])
        second[span, :] = jnp.where(even, low[n], high[n])


def emit_faces(values, chosen, meta, payload, first, second, faces, lane, members, cap):
    low, high = [], []
    for c in range(3):
        packed = pack_faces(values[c], lane)
        for f in range(4):
            for p in range(2):
                at = (f * 6 + c * 2 + p) * BLK
                faces[at : at + BLK, :] = packed[f][p]
        low += values[c][:2]
        high += values[c][-2:]
    emit_planes(low, high, meta[0] == 1, first, second)
    for n in range(members * cap):
        member, slot = divmod(n, cap)
        row = faces[pl.ds(chosen[n], 6, stride=BLK), :]
        payload[pl.ds(member * 6 * cap + slot, 6, stride=cap), :] = row


def prepare_kernel(
    members, groups, cap, viscosity, refinement, face_owner, face_block, coarse_rows,
    eff, payload, first, second, meta, starts, wants, faces, count,
):
    lane, sub = lane_id(), sub_id()
    group, member = lax.axis_index("grp"), lax.axis_index("mem")
    even = group % 2 == 0
    meta[0] = jnp.where(even, 1, 0)
    meta[1] = jnp.where(group > 0, 1, 0)
    meta[2] = jnp.where(group < groups - 1, 1, 0)
    meta[3] = member
    meta[4] = group
    level = jnp.zeros((BLK, LANES), jnp.int32)
    for b in range(BLK):
        level = jnp.where(sub == b, refinement[b], level)
    scale = jnp.exp2(-level.astype(F32))
    values = []
    for m in range(TILES):
        v = viscosity[:, tile(m)] * scale
        eff[:, tile(m)] = v
        values.append(v)
    packed = pack_faces(values, lane)
    per = 64 + BLK + 24
    for f in range(4):
        for p in range(2):
            at = (f * 2 + p) * BLK
            for n in range(members):
                payload[n * per + at : n * per + at + BLK, :] = packed[f][p]
    emit_planes(values[:2], values[-2:], even, first, second)
    columns = BLK * 3
    wide = lax.broadcasted_iota(jnp.int32, (24, LANES), 1)
    for n in range(members):
        payload[n * per + 64 : n * per + 72, :] = jnp.zeros((BLK, LANES), F32)
        at, off = divmod(n * columns, LANES)
        have = coarse_rows[:, tile(at)]
        part = have if off == 0 else pltpu.roll(have, LANES - off, 1)
        if off + columns > LANES:
            more = pltpu.roll(coarse_rows[:, tile(at + 1)], LANES - off, 1)
            part = jnp.where(wide < LANES - off, part, more)
        payload[n * per + 72 : n * per + per, :] = jnp.where(wide < columns, part, 0.0)
        count[n] = 0
    for b in range(BLK):
        for d in range(4):
            owner = face_owner[b * 4 + d, 0]
            slot = count[owner]
            count[owner] = slot + 1
            starts[b * 4 + d] = owner * 6 * cap + slot
            want = (d ^ 1) * 6 * BLK + face_block[b, d]
            payload[pl.ds(owner * per + 64 + slot, 1), :] = jnp.full((1, LANES), want, jnp.int32).astype(F32)
            wants[b * 4 + d] = owner * per + (d ^ 1) * 2 * BLK + face_block[b, d]


def weights_kernel(
    members, cap, near, from_first, from_second, eff, forcing, meta, wants, plane_block, hanging, chosen,
    step, payload, first, second, wi, gk, gj, gi, diagonal, inverse, faces, ghosts, planes,
):
    lane = lane_id()
    k, g = lane & 15, lane >> 4
    ghost = gather_ghosts(
        lambda b, d: wants[b * 4 + d], BLK, near, from_first, from_second, meta, plane_block, hanging,
        ghosts, planes, lane, 2,
    )
    values = [eff[:, tile(m)] for m in range(TILES)]
    start = [[], [], []]
    for m in range(TILES):
        i, h = divmod(m, 2)
        e = values[m]
        side_k = unpack_k(ghost[0], ghost[1], lane, m)
        side_j = unpack_j(ghost[2], ghost[3], m)
        ends_j = (g == 0) if h == 0 else (g == 7)
        n0 = jnp.where(k == 0, side_k, roll(e, 1))
        n1 = jnp.where(k == 15, side_k, roll(e, -1))
        n2 = jnp.where(g == 0, side_j if h == 0 else roll(values[m - 1], 16), roll(e, 16))
        n3 = jnp.where(g == 7, side_j if h == 1 else roll(values[m + 1], -16), roll(e, -16))
        n4 = ghost[4][h] if i == 0 else values[m - 2]
        n5 = ghost[5][h] if i == EDGE - 1 else values[m + 2]
        w = [0.5 * (e + n) for n in (n0, n1, n2, n3, n4, n5)]
        diag = MASS_TERM * e
        for d in range(6):
            diag = diag + w[d]
        inv = 1.0 / diag
        diagonal[:, tile(m)] = diag
        inverse[:, tile(m)] = inv
        wi[0, :, tile(m)] = jnp.where(k == 0, 0.0, w[0])
        wi[1, :, tile(m)] = jnp.where(k == 15, 0.0, w[1])
        wi[2, :, tile(m)] = jnp.where(ends_j, 0.0, w[2]) if h == 0 else w[2]
        wi[3, :, tile(m)] = jnp.where(ends_j, 0.0, w[3]) if h == 1 else w[3]
        wi[4, :, tile(m)] = w[4]
        gk[:, tile(m)] = jnp.where(k == 0, w[0], jnp.where(k == 15, w[1], 0.0))
        gj[:, tile(m)] = jnp.where(ends_j, w[2 + h], 0.0)
        if i == 0:
            gi[:, tile(h)] = w[4]
        if i == EDGE - 1:
            gi[:, tile(2 + h)] = w[5]
        scale = inv * (1.0 / THETA)
        for c in range(3):
            s = forcing[c, :, tile(m)] * scale
            step[c, :, tile(m)] = s
            start[c].append(s)
    emit_faces(start, chosen, meta, payload, first, second, faces, lane, members, cap)


def inside_kernel(has_x, has_lift, *refs):
    refs = list(refs)
    residual, step, wi, diagonal = refs[:4]
    refs = refs[4:]
    x = refs.pop(0) if has_x else None
    lift = refs.pop(0) if has_lift else None
    new_residual = refs.pop(0)
    new_x = refs.pop(0) if has_x else None
    g = lane_id() >> 4
    for c in range(3):
        up = None if not has_lift else lift[c * BLK : (c + 1) * BLK, :]
        for m in range(TILES):
            i, h = divmod(m, 2)
            s = step[c, :, tile(m)]
            n2, n3 = roll(s, 16), roll(s, -16)
            if h == 1:
                n2 = jnp.where(g == 0, roll(step[c, :, tile(m - 1)], 16), n2)
            else:
                n3 = jnp.where(g == 7, roll(step[c, :, tile(m + 1)], -16), n3)
            acc = residual[c, :, tile(m)] - diagonal[:, tile(m)] * s
            acc = acc + wi[0, :, tile(m)] * roll(s, 1)
            acc = acc + wi[1, :, tile(m)] * roll(s, -1)
            acc = acc + wi[2, :, tile(m)] * n2
            acc = acc + wi[3, :, tile(m)] * n3
            if i > 0:
                acc = acc + wi[4, :, tile(m)] * step[c, :, tile(m - 2)]
            if i < EDGE - 1:
                acc = acc + wi[4, :, tile(m + 2)] * step[c, :, tile(m + 2)]
            new_residual[c, :, tile(m)] = acc
            if has_x:
                total = x[c, :, tile(m)] + s
                if has_lift:
                    total = total + up
                new_x[c, :, tile(m)] = total


def add_ghosts(c, m, value, ghost, gk, gj, gi, lane):
    i, h = divmod(m, 2)
    pair = slice(2 * c, 2 * c + 2)
    value = value + gk[:, tile(m)] * unpack_k(ghost[0][pair], ghost[1][pair], lane, m)
    value = value + gj[:, tile(m)] * unpack_j(ghost[2][pair], ghost[3][pair], m)
    if i == 0:
        value = value + gi[:, tile(h)] * ghost[4][2 * c + h]
    if i == EDGE - 1:
        value = value + gi[:, tile(2 + h)] * ghost[5][2 * c + h]
    return value


def outside_kernel(
    members, cap, old, new, near, from_first, from_second, residual, step, inverse, gk, gj, gi,
    meta, starts, plane_block, hanging, chosen,
    new_residual, new_step, payload, first, second, faces, ghosts, planes,
):
    lane = lane_id()
    ghost = gather_ghosts(
        lambda b, d: starts[b * 4 + d], cap, near, from_first, from_second, meta, plane_block, hanging,
        ghosts, planes, lane, 6,
    )
    values = [[], [], []]
    for c in range(3):
        for m in range(TILES):
            r = add_ghosts(c, m, residual[c, :, tile(m)], ghost, gk, gj, gi, lane)
            new_residual[c, :, tile(m)] = r
            s = old * step[c, :, tile(m)] + new * (r * inverse[:, tile(m)])
            new_step[c, :, tile(m)] = s
            values[c].append(s)
    emit_faces(values, chosen, meta, payload, first, second, faces, lane, members, cap)


def last_kernel(
    cap, near, from_first, from_second, residual, gk, gj, gi, meta, starts, plane_block, hanging,
    new_residual, ghosts, planes,
):
    lane = lane_id()
    ghost = gather_ghosts(
        lambda b, d: starts[b * 4 + d], cap, near, from_first, from_second, meta, plane_block, hanging,
        ghosts, planes, lane, 6,
    )
    for c in range(3):
        for m in range(TILES):
            new_residual[c, :, tile(m)] = add_ghosts(c, m, residual[c, :, tile(m)], ghost, gk, gj, gi, lane)


def coarse_kernel(
    members, devices, cap, near, from_first, from_second, residual, gk, gj, gi, meta, starts, plane_block, hanging,
    coarse, new_residual, payload, ghosts, planes,
):
    lane, sub = lane_id(), sub_id()
    ghost = gather_ghosts(
        lambda b, d: starts[b * 4 + d], cap, near, from_first, from_second, meta, plane_block, hanging,
        ghosts, planes, lane, 6,
    )
    placed = jnp.zeros((BLK, LANES), F32)
    for c in range(3):
        sums = [None] * 4
        for m in range(TILES):
            r = add_ghosts(c, m, residual[c, :, tile(m)], ghost, gk, gj, gi, lane)
            new_residual[c, :, tile(m)] = r
            sums[m % 4] = r if sums[m % 4] is None else sums[m % 4] + r
        total = (sums[0] + sums[1]) + (sums[2] + sums[3])
        total = jnp.broadcast_to(jnp.sum(total, axis=1, keepdims=True), (BLK, LANES))
        placed = jnp.where(lane == 3 * sub + c, total, placed)
    own = jnp.sum(placed, axis=0, keepdims=True) * (1.0 / math.sqrt(CELLS))
    own = jnp.broadcast_to(own, (BLK, LANES))
    unknowns = members * BLK * 3
    wide = -(-unknowns // LANES)
    rows = [jnp.zeros((BLK, LANES), F32) for _ in range(wide)]
    per = 64 + BLK + 24
    for n in range(members):
        for v in range(3):
            at = n * per + 72 + v * BLK
            part = jnp.sum(coarse[at : at + BLK, :] * own, axis=1, keepdims=True)
            part = jnp.broadcast_to(part, (BLK, LANES))
            place = n * 24 + v * BLK
            for t in range(place // LANES, (place + BLK - 1) // LANES + 1):
                rows[t] = jnp.where(lane + t * LANES == place + sub, part, rows[t])
    out = jnp.zeros((BLK, LANES), F32)
    for t in range(wide):
        out = jnp.where(sub == t, jnp.sum(rows[t], axis=0, keepdims=True), out)
    for n in range(devices):
        payload[n * BLK : (n + 1) * BLK, :] = out


def lift_kernel(
    members, cap, arrived, residual, eff, inverse, gk, gj, gi, meta, face_owner, face_block, plane_block, chosen,
    new_residual, step, lift, payload, first, second, faces,
):
    lane, sub = lane_id(), sub_id()
    k = lane & 15
    wide = -(-members * BLK * 3 // LANES)
    group, member = meta[4], meta[3]
    base = [
        jnp.where(meta[1] == 1, group - 1, group), group, jnp.where(meta[2] == 1, group + 1, group)
    ]
    known = []
    for n in range(3):
        total = jnp.zeros((BLK, LANES), F32)
        for p in range(members):
            at = pl.multiple_of((base[n] * members + p) * BLK, BLK)
            total = total + arrived[pl.ds(at, BLK), :]
        if n != 1:
            total = jnp.where(meta[1 if n == 0 else 2] == 1, total, 0.0)
        known.append([jnp.broadcast_to(total[t : t + 1, :], (BLK, LANES)) for t in range(wide)])

    def look_up(table, block):
        index = jnp.zeros((BLK, LANES), jnp.int32)
        for b in range(BLK):
            index = jnp.where(sub == b, 3 * block(b), index)
        found = []
        for c in range(3):
            total = jnp.zeros((BLK, LANES), F32)
            for t in range(wide):
                total = total + jnp.where(lane + t * LANES == index + c, table[t], 0.0)
            found.append(jnp.broadcast_to(jnp.sum(total, axis=1, keepdims=True), (BLK, LANES)))
        return found

    own = look_up(known[1], lambda b: member * BLK + b)
    side = [look_up(known[1], lambda b, d=d: face_owner[b * 4 + d, 0] * BLK + face_block[b, d]) for d in range(4)]
    below = look_up(known[0], lambda b: member * BLK + plane_block[b, 0])
    above = look_up(known[2], lambda b: member * BLK + plane_block[b, 1])
    values = [[], [], []]
    for c in range(3):
        lift[c * BLK : (c + 1) * BLK, :] = own[c]
        drop_k = own[c] - jnp.where(k == 0, side[0][c], side[1][c])
        drop_j = [own[c] - side[2][c], own[c] - side[3][c]]
        drop_i = [own[c] - below[c], own[c] - above[c]]
        for m in range(TILES):
            i, h = divmod(m, 2)
            applied = (MASS_TERM * eff[:, tile(m)]) * own[c]
            applied = applied + gk[:, tile(m)] * drop_k + gj[:, tile(m)] * drop_j[h]
            if i == 0:
                applied = applied + gi[:, tile(h)] * drop_i[0]
            if i == EDGE - 1:
                applied = applied + gi[:, tile(2 + h)] * drop_i[1]
            r = residual[c, :, tile(m)] - applied
            new_residual[c, :, tile(m)] = r
            s = r * (inverse[:, tile(m)] * (1.0 / THETA))
            step[c, :, tile(m)] = s
            values[c].append(s)
    emit_faces(values, chosen, meta, payload, first, second, faces, lane, members, cap)


def local(
    forcing, viscosity, refinement, face_owner, face_block, plane_block, hanging, coarse_solver
):
    groups, members = lax.axis_size("grp"), lax.axis_size("mem")
    cap = 8 * BLK // members
    devices = groups * members
    field = jax.ShapeDtypeStruct(forcing.shape, F32)
    scalar_field = jax.ShapeDtypeStruct(viscosity.shape, F32)

    def array(*shape):
        return jax.ShapeDtypeStruct(shape, F32)

    def ints(n):
        return jax.ShapeDtypeStruct((n,), jnp.int32)

    def scratch(*shape):
        return pltpu.VMEM(shape, F32)

    def call(body, in_specs, out_shape, out_specs, scratch_shapes, name, flops=2_000_000, moved=2_000_000):
        return pl.pallas_call(
            body,
            out_shape=out_shape,
            in_specs=in_specs,
            out_specs=out_specs,
            scratch_shapes=scratch_shapes,
            compiler_params=PARAMS,
            cost_estimate=pl.CostEstimate(flops=flops, bytes_accessed=moved, transcendentals=0),
            name=name,
        )

    first_route = [(q * members + m, (q ^ 1) * members + m) for q in range(groups) for m in range(members)]
    second_route = []
    for q in range(groups):
        for m in range(members):
            if q == 0 or q == groups - 1:
                second_route.append((q * members + m, q * members + (m ^ 1)))
            else:
                second_route.append((q * members + m, (q + 1 if q % 2 else q - 1) * members + m))

    def exchange(payload, first, second):
        near = payload.reshape(members, -1, LANES)
        near = lax.all_to_all(near, "mem", split_axis=0, concat_axis=0, tiled=True)
        first = lax.ppermute(first, ("grp", "mem"), first_route)
        second = lax.ppermute(second, ("grp", "mem"), second_route)
        return near.reshape(-1, LANES), first, second

    per = 64 + BLK + 24
    solver_rows = jnp.pad(coarse_solver[0], ((0, 0), (0, -coarse_solver.shape[2] % LANES)))
    eff, payload, first, second, meta, starts, wants = call(
        functools.partial(prepare_kernel, members, groups, cap),
        [VMEM, SMEM, SMEM, SMEM, VMEM],
        [scalar_field, array(members * per, LANES), array(16, LANES), array(16, LANES), ints(8), ints(32), ints(32)],
        [VMEM] * 4 + [SMEM] * 3,
        [scratch(4 * 16, LANES), pltpu.SMEM((members,), jnp.int32)],
        "prepare",
    )(viscosity, refinement, face_owner, face_block, solver_rows)
    arrived, from_first, from_second = exchange(payload, first, second)
    chosen = arrived.reshape(members, per, LANES)[:, 64 : 64 + cap, 0].astype(jnp.int32).reshape(-1)

    payload_out = [array(members * 6 * cap, LANES), array(48, LANES), array(48, LANES)]
    face_scratch = scratch(4 * 48, LANES)
    ghost_scratch = [scratch(6 * 48, LANES), scratch(2 * 48, LANES)]

    step, payload, first, second, wi, gk, gj, gi, diagonal, inverse = call(
        functools.partial(weights_kernel, members, cap),
        [VMEM] * 5 + [SMEM] * 3 + [VMEM, SMEM],
        [field] + payload_out
        + [array(5, BLK, CELLS), scalar_field, scalar_field, array(BLK, 4 * LANES), scalar_field, scalar_field],
        [VMEM] * 10,
        [face_scratch, scratch(6 * 16, LANES), scratch(2 * 16, LANES)],
        "weights",
    )(arrived, from_first, from_second, eff, forcing, meta, wants, plane_block, hanging, chosen)

    def inside(residual, step, x=None, lift=None):
        operands = [residual, step, wi, diagonal] + [a for a in (x, lift) if a is not None]
        out = [field] + ([field] if x is not None else [])
        result = call(
            functools.partial(inside_kernel, x is not None, lift is not None),
            [VMEM] * len(operands), out, [VMEM] * len(out), [], "inside",
        )(*operands)
        return result if x is not None else (result[0], step)

    def outside(arrived, from_first, from_second, residual, step, old, new):
        return call(
            functools.partial(outside_kernel, members, cap, old, new),
            [VMEM] * 9 + [SMEM] * 3 + [VMEM, SMEM],
            [field, field] + payload_out,
            [VMEM] * 5,
            [face_scratch] + ghost_scratch,
            "outside",
        )(arrived, from_first, from_second, residual, step, inverse, gk, gj, gi, meta, starts, plane_block, hanging, chosen)

    rho = 1.0 / SIGMA
    factors = []
    for _ in range(DEG - 1):
        rho_next = 1.0 / (2.0 * SIGMA - rho)
        factors.append((rho_next * rho, 2.0 * rho_next / DELTA))
        rho = rho_next

    def steps(residual, step, payload, first, second, x, lift):
        for old, new in factors:
            arrived, from_first, from_second = exchange(payload, first, second)
            residual, x = inside(residual, step, x, lift)
            lift = None
            residual, step, payload, first, second = outside(
                arrived, from_first, from_second, residual, step, old, new
            )
        arrived, from_first, from_second = exchange(payload, first, second)
        residual, x = inside(residual, step, x, lift)
        return arrived, from_first, from_second, residual, x

    coarse_table = arrived
    arrived, from_first, from_second, residual, x = steps(forcing, step, payload, first, second, None, None)
    residual, payload = call(
        functools.partial(coarse_kernel, members, devices, cap),
        [VMEM] * 7 + [SMEM] * 3 + [VMEM, VMEM],
        [field, array(devices * BLK, LANES)],
        [VMEM] * 2,
        ghost_scratch,
        "coarse",
    )(arrived, from_first, from_second, residual, gk, gj, gi, meta, starts, plane_block, hanging, coarse_table)
    sums = payload.reshape(devices, BLK, LANES)
    sums = lax.all_to_all(sums, ("grp", "mem"), split_axis=0, concat_axis=0, tiled=True).reshape(-1, LANES)
    residual, step, lift, payload, first, second = call(
        functools.partial(lift_kernel, members, cap),
        [VMEM] * 7 + [SMEM] * 5,
        [field, field, array(3 * BLK, LANES)] + payload_out,
        [VMEM] * 6,
        [face_scratch],
        "lift",
    )(sums, residual, eff, inverse, gk, gj, gi, meta, face_owner, face_block, plane_block, chosen)
    arrived, from_first, from_second, residual, x = steps(residual, step, payload, first, second, x, lift)
    residual = call(
        functools.partial(last_kernel, cap),
        [VMEM] * 7 + [SMEM] * 3 + [VMEM],
        [field],
        [VMEM],
        ghost_scratch,
        "last",
    )(arrived, from_first, from_second, residual, gk, gj, gi, meta, starts, plane_block, hanging)[0]
    return x, residual


def solution(mesh):
    in_specs = (
        P(None, ("grp", "mem"), None),
        P(("grp", "mem"), None),
        P(("grp", "mem")),
        P(("grp", "mem"), None),
        P(("grp", "mem"), None),
        P(("grp", "mem"), None),
        P(("grp", "mem"), None),
        P("grp", "mem", None),
    )
    out_specs = (P(None, ("grp", "mem"), None), P(None, ("grp", "mem"), None))
    return jax.shard_map(local, mesh=mesh, in_specs=in_specs, out_specs=out_specs, check_vma=False)
```

profile of v0, /device:TPU:0, one launch (start us, length us, event | category | flops | bytes accessed | tf_op | source)
XLA Modules:
  0.0 118.1 jit_solution(15717291871550259105)
XLA Ops:
  3.7 1.9 %prepare.1 = (f32[8,4096]{1,0:T(8,128)S(1)}, f32[768,128]{1,0:T(8,128)}, f32[16,128]{1,0:T(8,128)S(1)}, f32[16,128]{1,0:T(8,128)S(1)}, s32[8]{0:T(128)S(1)}, /*index=5*/s32[32]{0:T(128)S(1)}, s32[32]{0:T(128)S(1)}) custom-call(f32[8,4096]{1,0:T(8,128)S(1)} %copy-done.18, s32[8]{0:T(128)S(1)} %copy-done.19, s32[32,1]{1,0:T(8,128)S(1)} %copy.36.face_owner, ...), custom_call_target="tpu_custom_call" | custom-call | flops 2000000 | bytes 2000000 | tf_op jit(solution)/shard_map/prepare/pallas_call | solution.py:471
  5.6 5.3 %all-to-all-start = ((f32[8,96,128]{2,1,0:T(8,128)}), f32[8,96,128]{2,1,0:T(8,128)S(1)}, u32[]{:S(2)}, u32[]{:S(2)}) async-start(f32[8,96,128]{2,1,0:T(8,128)} %bitcast.1), calls=%async_computation | async-start | bytes 786432 | tf_op jit(solution)/shard_map/all_to_all | solution.py:464
  12.8 6.5 %all-to-all-done = f32[8,96,128]{2,1,0:T(8,128)S(1)} async-done(((f32[8,96,128]{2,1,0:T(8,128)}), f32[8,96,128]{2,1,0:T(8,128)S(1)}, u32[]{:S(2)}, u32[]{:S(2)}) %all-to-all-start) | async-done | bytes 393248 | tf_op jit(solution)/shard_map/all_to_all | solution.py:464
  20.2 2.3 %weights.1 = (f32[3,8,4096]{2,1,0:T(8,128)S(1)}, f32[384,128]{1,0:T(8,128)}, f32[48,128]{1,0:T(8,128)S(1)}, f32[48,128]{1,0:T(8,128)S(1)}, f32[5,8,4096]{2,1,0:T...) custom-call(f32[768,128]{1,0:T(8,128)S(1)} %bitcast.17, ...), custom_call_target="tpu_custom_call" | custom-call | flops 2000000 | bytes 2000000 | tf_op jit(solution)/shard_map/weights/pallas_call | solution.py:486
  22.5 3.4 %all-to-all-start.1 = ((f32[8,48,128]{2,1,0:T(8,128)}), f32[8,48,128]{2,1,0:T(8,128)S(1)}, u32[]{:S(2)}, u32[]{:S(2)}) async-start(f32[8,48,128]{2,1,0:T(8,128)} %bitcast.3), calls=%async_computation.1 | async-start | bytes 393216 | tf_op jit(solution)/shard_map/all_to_all | solution.py:464
  29.8 2.3 %all-to-all-done.1 = f32[8,48,128]{2,1,0:T(8,128)S(1)} async-done(((f32[8,48,128]{2,1,0:T(8,128)}), f32[8,48,128]{2,1,0:T(8,128)S(1)}, u32[]{:S(2)}, u32[]{:S(2)}) %all-to-all-start.1) | async-done | bytes 196640 | tf_op jit(solution)/shard_map/all_to_all | solution.py:464
  32.1 3.6 %outside.4 = (f32[3,8,4096]{2,1,0:T(8,128)S(1)}, f32[3,8,4096]{2,1,0:T(8,128)S(1)}, f32[384,128]{1,0:T(8,128)}, f32[48,128]{1,0:T(8,128)S(1)}, f32[48,128]{1,0:T(8,128)S(1)}) custom-call(f32[384,128]{1,0:T(8,128)S(1)} %bitcast.22, f32[48,128]{1,0:T(8,128)S(1)} %collective-permute-done.2.from_first, f32[48,128]{1,0:T(8,128)S(1)} %collective-permute-done.3.from_second, ...), custom_call_target="tpu_custom_call" | custom-call | flops 2000000 | bytes 2000000 | tf_op jit(solution)/shard_map/outside/pallas_call | solution.py:506
  36.4 3.4 %all-to-all-start.2 = ((f32[8,48,128]{2,1,0:T(8,128)}), f32[8,48,128]{2,1,0:T(8,128)S(1)}, u32[]{:S(2)}, u32[]{:S(2)}) async-start(f32[8,48,128]{2,1,0:T(8,128)} %bitcast.5), calls=%async_computation.2 | async-start | bytes 393216 | tf_op jit(solution)/shard_map/all_to_all | solution.py:464
  43.9 2.1 %all-to-all-done.2 = f32[8,48,128]{2,1,0:T(8,128)S(1)} async-done(((f32[8,48,128]{2,1,0:T(8,128)}), f32[8,48,128]{2,1,0:T(8,128)S(1)}, u32[]{:S(2)}, u32[]{:S(2)}) %all-to-all-start.2) | async-done | bytes 196640 | tf_op jit(solution)/shard_map/all_to_all | solution.py:464
  46.0 3.6 %outside.5 = (f32[3,8,4096]{2,1,0:T(8,128)S(1)}, f32[3,8,4096]{2,1,0:T(8,128)S(1)}, f32[384,128]{1,0:T(8,128)}, f32[48,128]{1,0:T(8,128)S(1)}, f32[48,128]{1,0:T(8,128)S(1)}) custom-call(f32[384,128]{1,0:T(8,128)S(1)} %bitcast.21, f32[48,128]{1,0:T(8,128)S(1)} %collective-permute-done.4.from_first, f32[48,128]{1,0:T(8,128)S(1)} %collective-permute-done.5.from_second, ...), custom_call_target="tpu_custom_call" | custom-call | flops 2000000 | bytes 2000000 | tf_op jit(solution)/shard_map/outside/pallas_call | solution.py:506
  51.1 3.5 %all-to-all-start.3 = ((f32[8,48,128]{2,1,0:T(8,128)}), f32[8,48,128]{2,1,0:T(8,128)S(1)}, u32[]{:S(2)}, u32[]{:S(2)}) async-start(f32[8,48,128]{2,1,0:T(8,128)} %bitcast.7), calls=%async_computation.3 | async-start | bytes 393216 | tf_op jit(solution)/shard_map/all_to_all | solution.py:464
  60.8 2.6 %coarse.1 = (f32[3,8,4096]{2,1,0:T(8,128)S(1)}, f32[256,128]{1,0:T(8,128)S(1)}) custom-call(f32[384,128]{1,0:T(8,128)S(1)} %bitcast.24, f32[48,128]{1,0:T(8,128)S(1)} %collective-permute-done.6.from_first, f32[48,128]{1,0:T(8,128)S(1)} %collective-permute-done.7.from_second, f32[3,8,4096]{2,1,0:T(8,128)S(1)} %get-tuple-element.86.residual, ...), custom_call_target="tpu_custom_call" | custom-call | flops 2000000 | bytes 2000000 | tf_op jit(solution)/shard_map/coarse/pallas_call | solution.py:536
  63.5 12.5 %all_to_all.40 = f32[32,8,128]{2,1,0:T(8,128)S(1)} all-to-all(f32[32,8,128]{2,1,0:T(8,128)S(1)} %bitcast.27), channel_id=1, replica_groups=mesh['grp'=4,'mem'=8] {'grp','mem'}, dimensions={0} | all-to-all | bytes 262144 | tf_op jit(solution)/shard_map/all_to_all | solution.py:545
  76.0 2.2 %lift.1 = (f32[3,8,4096]{2,1,0:T(8,128)S(1)}, f32[3,8,4096]{2,1,0:T(8,128)S(1)}, f32[24,128]{1,0:T(8,128)S(1)}, f32[384,128]{1,0:T(8,128)}, f32[48,128]{1,0:T(8,128)S(1)}, /*index=5*/f32[48,128]{1,0:T(8,128)S(1)}) custom-call(f32[256,128]{1,0:T(8,128)S(1)} %bitcast.25, f32[3,8,4096]{2,1,0:T(8,128)S(1)} %get-tuple-element.88.residual, ...), custom_call_target="tpu_custom_call" | custom-call | flops 2000000 | bytes 2000000 | tf_op jit(solution)/shard_map/lift/pallas_call | solution.py:546
  78.2 3.4 %all-to-all-start.5 = ((f32[8,48,128]{2,1,0:T(8,128)}), f32[8,48,128]{2,1,0:T(8,128)S(1)}, u32[]{:S(2)}, u32[]{:S(2)}) async-start(f32[8,48,128]{2,1,0:T(8,128)} %bitcast.11), calls=%async_computation.5 | async-start | bytes 393216 | tf_op jit(solution)/shard_map/all_to_all | solution.py:464
  85.5 2.3 %all-to-all-done.5 = f32[8,48,128]{2,1,0:T(8,128)S(1)} async-done(((f32[8,48,128]{2,1,0:T(8,128)}), f32[8,48,128]{2,1,0:T(8,128)S(1)}, u32[]{:S(2)}, u32[]{:S(2)}) %all-to-all-start.5) | async-done | bytes 196640 | tf_op jit(solution)/shard_map/all_to_all | solution.py:464
  87.8 3.6 %outside.6 = (f32[3,8,4096]{2,1,0:T(8,128)S(1)}, f32[3,8,4096]{2,1,0:T(8,128)S(1)}, f32[384,128]{1,0:T(8,128)}, f32[48,128]{1,0:T(8,128)}, f32[48,128]{1,0:T(8,128)S(1)}) custom-call(f32[384,128]{1,0:T(8,128)S(1)} %bitcast.20, f32[48,128]{1,0:T(8,128)S(1)} %collective-permute-done.8.from_first, f32[48,128]{1,0:T(8,128)S(1)} %collective-permute-done.9.from_second, ...), custom_call_target="tpu_custom_call" | custom-call | flops 2000000 | bytes 2000000 | tf_op jit(solution)/shard_map/outside/pallas_call | solution.py:506
  91.4 3.5 %all-to-all-start.6 = ((f32[8,48,128]{2,1,0:T(8,128)}), f32[8,48,128]{2,1,0:T(8,128)S(1)}, u32[]{:S(2)}, u32[]{:S(2)}) async-start(f32[8,48,128]{2,1,0:T(8,128)} %bitcast.13), calls=%async_computation.6 | async-start | bytes 393216 | tf_op jit(solution)/shard_map/all_to_all | solution.py:464
  96.3 2.7 %collective-permute-done.10.from_first = f32[48,128]{1,0:T(8,128)S(1)} collective-permute-done((f32[48,128]{1,0:T(8,128)}, f32[48,128]{1,0:T(8,128)S(1)}, u32[]{:S(2)}, u32[]{:S(2)}) %collective-permute-start.10) | collective-permute-done | bytes 24608 | tf_op jit(solution)/shard_map/ppermute | solution.py:465
  99.0 2.1 %all-to-all-done.6 = f32[8,48,128]{2,1,0:T(8,128)S(1)} async-done(((f32[8,48,128]{2,1,0:T(8,128)}), f32[8,48,128]{2,1,0:T(8,128)S(1)}, u32[]{:S(2)}, u32[]{:S(2)}) %all-to-all-start.6) | async-done | bytes 196640 | tf_op jit(solution)/shard_map/all_to_all | solution.py:464
  101.1 2.9 %outside.7 = (f32[3,8,4096]{2,1,0:T(8,128)S(1)}, f32[3,8,4096]{2,1,0:T(8,128)S(1)}, f32[384,128]{1,0:T(8,128)S(1)}, f32[48,128]{1,0:T(8,128)S(1)}, f32[48,128]{1,0:T(8,128)S(1)}) custom-call(f32[384,128]{1,0:T(8,128)S(1)} %bitcast.19, f32[48,128]{1,0:T(8,128)S(1)} %collective-permute-done.10.from_first, f32[48,128]{1,0:T(8,128)S(1)} %collective-permute-done.11.from_second, ...), custom_call_target="tpu_custom_call" | custom-call | flops 2000000 | bytes 2000000 | tf_op jit(solution)/shard_map/outside/pallas_call | solution.py:506
  105.3 3.5 %all-to-all-start.7 = ((f32[8,48,128]{2,1,0:T(8,128)}), f32[8,48,128]{2,1,0:T(8,128)S(1)}, u32[]{:S(2)}, u32[]{:S(2)}) async-start(f32[8,48,128]{2,1,0:T(8,128)} %bitcast.26), calls=%async_computation.7 | async-start | bytes 393216 | tf_op jit(solution)/shard_map/all_to_all | solution.py:464
  112.8 2.3 %all-to-all-done.7 = f32[8,48,128]{2,1,0:T(8,128)S(1)} async-done(((f32[8,48,128]{2,1,0:T(8,128)}), f32[8,48,128]{2,1,0:T(8,128)S(1)}, u32[]{:S(2)}, u32[]{:S(2)}) %all-to-all-start.7) | async-done | bytes 196640 | tf_op jit(solution)/shard_map/all_to_all | solution.py:464
  115.0 3.1 %last.1 = f32[3,8,4096]{2,1,0:T(8,128)} custom-call(f32[384,128]{1,0:T(8,128)S(1)} %bitcast.23, f32[48,128]{1,0:T(8,128)S(1)} %collective-permute-done.12.from_first, f32[48,128]{1,0:T(8,128)S(1)} %collective-permute-done.13.from_second, f32[3,8,4096]{2,1,0:T(8,128)S(1)} %get-tuple-element.111.residual, f32[8,4096]{1,0:T(8,128)S(1)} %get-tuple-element.70.gk, ...), custom_call_target="tpu_custom_call" | custom-call | flops 2000000 | bytes 2000000 | tf_op jit(solution)/shard_map/last/pallas_call | solution.py:555
  (88 shorter events, 32.7 us)
Async XLA Ops:
  5.6 14.0 %copy-start = (f32[3,8,4096]{2,1,0:T(8,128)S(1)}, f32[3,8,4096]{2,1,0:T(8,128)}, u32[]{:S(2)}) copy-start(f32[3,8,4096]{2,1,0:T(8,128)} %refs_0_.1) | copy-start | bytes 1179652
  5.6 13.7 %all-to-all-start = ((f32[8,96,128]{2,1,0:T(8,128)}), f32[8,96,128]{2,1,0:T(8,128)S(1)}, u32[]{:S(2)}, u32[]{:S(2)}) async-start(f32[8,96,128]{2,1,0:T(8,128)} %bitcast.1), calls=%async_computation | async-start | bytes 786432 | tf_op jit(solution)/shard_map/all_to_all | solution.py:464
  10.9 8.6 %collective-permute-start = (f32[16,128]{1,0:T(8,128)S(1)}, f32[16,128]{1,0:T(8,128)S(1)}, u32[]{:S(2)}, u32[]{:S(2)}) collective-permute-start(f32[16,128]{1,0:T(8,128)S(1)} %get-tuple-element.58), channel_id=1, source_target_pairs={{0,8},{1,9},{2,10},{3,11},{4,12},{5,13},{6,14},{7,15},{8,0},{9,1},... | collective-permute-start | bytes 24584 | tf_op jit(solution)/shard_map/ppermute | solution.py:465
  12.6 7.0 %collective-permute-start.1 = (f32[16,128]{1,0:T(8,128)S(1)}, f32[16,128]{1,0:T(8,128)S(1)}, u32[]{:S(2)}, u32[]{:S(2)}) collective-permute-start(f32[16,128]{1,0:T(8,128)S(1)} %get-tuple-element.59), channel_id=1, source_target_pairs={{0,1},{1,0},{2,3},{3,2},{4,5},{5,4},{6,7},{7,6},{8,16},{9,17},{10,... | collective-permute-start | bytes 24584 | tf_op jit(solution)/shard_map/ppermute | solution.py:466
  12.8 63.2 %copy-start.11 = (s32[8,2]{1,0:T(8,128)}, s32[8,2]{1,0:T(8,128)S(1)}, u32[]{:S(2)}) copy-start(s32[8,2]{1,0:T(8,128)S(1)} %copy.38.plane_block) | copy-start | bytes 196
  22.5 9.6 %all-to-all-start.1 = ((f32[8,48,128]{2,1,0:T(8,128)}), f32[8,48,128]{2,1,0:T(8,128)S(1)}, u32[]{:S(2)}, u32[]{:S(2)}) async-start(f32[8,48,128]{2,1,0:T(8,128)} %bitcast.3), calls=%async_computation.1 | async-start | bytes 393216 | tf_op jit(solution)/shard_map/all_to_all | solution.py:464
  25.9 3.9 %collective-permute-start.2 = (f32[48,128]{1,0:T(8,128)S(1)}, f32[48,128]{1,0:T(8,128)S(1)}, u32[]{:S(2)}, u32[]{:S(2)}) collective-permute-start(f32[48,128]{1,0:T(8,128)S(1)} %get-tuple-element.64), channel_id=1, source_target_pairs={{0,8},{1,9},{2,10},{3,11},{4,12},{5,13},{6,14},{7,15},{8,0},{9,1},... | collective-permute-start | bytes 73736 | tf_op jit(solution)/shard_map/ppermute | solution.py:465
  27.6 2.3 %collective-permute-start.3 = (f32[48,128]{1,0:T(8,128)S(1)}, f32[48,128]{1,0:T(8,128)S(1)}, u32[]{:S(2)}, u32[]{:S(2)}) collective-permute-start(f32[48,128]{1,0:T(8,128)S(1)} %get-tuple-element.65), channel_id=1, source_target_pairs={{0,1},{1,0},{2,3},{3,2},{4,5},{5,4},{6,7},{7,6},{8,16},{9,17},{10,... | collective-permute-start | bytes 73736 | tf_op jit(solution)/shard_map/ppermute | solution.py:466
  36.4 9.6 %all-to-all-start.2 = ((f32[8,48,128]{2,1,0:T(8,128)}), f32[8,48,128]{2,1,0:T(8,128)S(1)}, u32[]{:S(2)}, u32[]{:S(2)}) async-start(f32[8,48,128]{2,1,0:T(8,128)} %bitcast.5), calls=%async_computation.2 | async-start | bytes 393216 | tf_op jit(solution)/shard_map/all_to_all | solution.py:464
  39.8 4.1 %collective-permute-start.4 = (f32[48,128]{1,0:T(8,128)S(1)}, f32[48,128]{1,0:T(8,128)S(1)}, u32[]{:S(2)}, u32[]{:S(2)}) collective-permute-start(f32[48,128]{1,0:T(8,128)S(1)} %get-tuple-element.75), channel_id=1, source_target_pairs={{0,8},{1,9},{2,10},{3,11},{4,12},{5,13},{6,14},{7,15},{8,0},{9,1},... | collective-permute-start | bytes 73736 | tf_op jit(solution)/shard_map/ppermute | solution.py:465
  41.5 2.4 %collective-permute-start.5 = (f32[48,128]{1,0:T(8,128)S(1)}, f32[48,128]{1,0:T(8,128)S(1)}, u32[]{:S(2)}, u32[]{:S(2)}) collective-permute-start(f32[48,128]{1,0:T(8,128)S(1)} %get-tuple-element.76), channel_id=1, source_target_pairs={{0,1},{1,0},{2,3},{3,2},{4,5},{5,4},{6,7},{7,6},{8,16},{9,17},{10,... | collective-permute-start | bytes 73736 | tf_op jit(solution)/shard_map/ppermute | solution.py:466
  51.1 5.5 %copy-start.4 = (f32[3,8,4096]{2,1,0:T(8,128)S(1)}, f32[3,8,4096]{2,1,0:T(8,128)}, u32[]{:S(2)}) copy-start(f32[3,8,4096]{2,1,0:T(8,128)} %copy-done.3) | copy-start | bytes 1179652
  51.1 9.7 %all-to-all-start.3 = ((f32[8,48,128]{2,1,0:T(8,128)}), f32[8,48,128]{2,1,0:T(8,128)S(1)}, u32[]{:S(2)}, u32[]{:S(2)}) async-start(f32[8,48,128]{2,1,0:T(8,128)} %bitcast.7), calls=%async_computation.3 | async-start | bytes 393216 | tf_op jit(solution)/shard_map/all_to_all | solution.py:464
  54.6 4.5 %collective-permute-start.6 = (f32[48,128]{1,0:T(8,128)S(1)}, f32[48,128]{1,0:T(8,128)S(1)}, u32[]{:S(2)}, u32[]{:S(2)}) collective-permute-start(f32[48,128]{1,0:T(8,128)S(1)} %get-tuple-element.81), channel_id=1, source_target_pairs={{0,8},{1,9},{2,10},{3,11},{4,12},{5,13},{6,14},{7,15},{8,0},{9,1},... | collective-permute-start | bytes 73736 | tf_op jit(solution)/shard_map/ppermute | solution.py:465
  56.3 2.8 %collective-permute-start.7 = (f32[48,128]{1,0:T(8,128)S(1)}, f32[48,128]{1,0:T(8,128)S(1)}, u32[]{:S(2)}, u32[]{:S(2)}) collective-permute-start(f32[48,128]{1,0:T(8,128)S(1)} %get-tuple-element.82), channel_id=1, source_target_pairs={{0,1},{1,0},{2,3},{3,2},{4,5},{5,4},{6,7},{7,6},{8,16},{9,17},{10,... | collective-permute-start | bytes 73736 | tf_op jit(solution)/shard_map/ppermute | solution.py:466
  78.2 9.6 %all-to-all-start.5 = ((f32[8,48,128]{2,1,0:T(8,128)}), f32[8,48,128]{2,1,0:T(8,128)S(1)}, u32[]{:S(2)}, u32[]{:S(2)}) async-start(f32[8,48,128]{2,1,0:T(8,128)} %bitcast.11), calls=%async_computation.5 | async-start | bytes 393216 | tf_op jit(solution)/shard_map/all_to_all | solution.py:464
  81.6 3.9 %collective-permute-start.8 = (f32[48,128]{1,0:T(8,128)S(1)}, f32[48,128]{1,0:T(8,128)S(1)}, u32[]{:S(2)}, u32[]{:S(2)}) collective-permute-start(f32[48,128]{1,0:T(8,128)S(1)} %get-tuple-element.90), channel_id=1, source_target_pairs={{0,8},{1,9},{2,10},{3,11},{4,12},{5,13},{6,14},{7,15},{8,0},{9,1},... | collective-permute-start | bytes 73736 | tf_op jit(solution)/shard_map/ppermute | solution.py:465
  82.3 3.2 %collective-permute-start.9 = (f32[48,128]{1,0:T(8,128)S(1)}, f32[48,128]{1,0:T(8,128)S(1)}, u32[]{:S(2)}, u32[]{:S(2)}) collective-permute-start(f32[48,128]{1,0:T(8,128)S(1)} %get-tuple-element.91), channel_id=1, source_target_pairs={{0,1},{1,0},{2,3},{3,2},{4,5},{5,4},{6,7},{7,6},{8,16},{9,17},{10,... | collective-permute-start | bytes 73736 | tf_op jit(solution)/shard_map/ppermute | solution.py:466
  91.4 9.7 %all-to-all-start.6 = ((f32[8,48,128]{2,1,0:T(8,128)}), f32[8,48,128]{2,1,0:T(8,128)S(1)}, u32[]{:S(2)}, u32[]{:S(2)}) async-start(f32[8,48,128]{2,1,0:T(8,128)} %bitcast.13), calls=%async_computation.6 | async-start | bytes 393216 | tf_op jit(solution)/shard_map/all_to_all | solution.py:464
  94.9 4.1 %collective-permute-start.10 = (f32[48,128]{1,0:T(8,128)}, f32[48,128]{1,0:T(8,128)S(1)}, u32[]{:S(2)}, u32[]{:S(2)}) collective-permute-start(f32[48,128]{1,0:T(8,128)} %get-tuple-element.98), channel_id=1, source_target_pairs={{0,8},{1,9},{2,10},{3,11},{4,12},{5,13},{6,14},{7,15},{8,0},{9,1},... | collective-permute-start | bytes 73736 | tf_op jit(solution)/shard_map/ppermute | solution.py:465
  95.6 3.4 %collective-permute-start.11 = (f32[48,128]{1,0:T(8,128)S(1)}, f32[48,128]{1,0:T(8,128)S(1)}, u32[]{:S(2)}, u32[]{:S(2)}) collective-permute-start(f32[48,128]{1,0:T(8,128)S(1)} %get-tuple-element.99), channel_id=1, source_target_pairs={{0,1},{1,0},{2,3},{3,2},{4,5},{5,4},{6,7},{7,6},{8,16},{9,17},{10,... | collective-permute-start | bytes 73736 | tf_op jit(solution)/shard_map/ppermute | solution.py:466
  105.3 9.7 %all-to-all-start.7 = ((f32[8,48,128]{2,1,0:T(8,128)}), f32[8,48,128]{2,1,0:T(8,128)S(1)}, u32[]{:S(2)}, u32[]{:S(2)}) async-start(f32[8,48,128]{2,1,0:T(8,128)} %bitcast.26), calls=%async_computation.7 | async-start | bytes 393216 | tf_op jit(solution)/shard_map/all_to_all | solution.py:464
  108.9 3.9 %collective-permute-start.12 = (f32[48,128]{1,0:T(8,128)S(1)}, f32[48,128]{1,0:T(8,128)S(1)}, u32[]{:S(2)}, u32[]{:S(2)}) collective-permute-start(f32[48,128]{1,0:T(8,128)S(1)} %copy-done.21), channel_id=1, source_target_pairs={{0,8},{1,9},{2,10},{3,11},{4,12},{5,13},{6,14},{7,15},{8,0},{9,1},... | collective-permute-start | bytes 73736 | tf_op jit(solution)/shard_map/ppermute | solution.py:465
  109.6 3.2 %collective-permute-start.13 = (f32[48,128]{1,0:T(8,128)S(1)}, f32[48,128]{1,0:T(8,128)S(1)}, u32[]{:S(2)}, u32[]{:S(2)}) collective-permute-start(f32[48,128]{1,0:T(8,128)S(1)} %get-tuple-element.110), channel_id=1, source_target_pairs={{0,1},{1,0},{2,3},{3,2},{4,5},{5,4},{6,7},{7,6},{8,16},{9,17},{10,... | collective-permute-start | bytes 73736 | tf_op jit(solution)/shard_map/ppermute | solution.py:466
  (21 other events, 43.0 us)
where the time goes:
time: 119 us; the launch traced here: 118 us
  starting transfers between devices  35.5 us (30%)
  Pallas kernels  30.1 us (25%)
  waiting for transfers between devices  27 us (23%)
  blocking collectives  12.5 us (11%)
  local copies, waits for them, and re-layouts  11.9 us (10%)
    all_to_all x7, starting transfers between devices, exchange(): near = lax.all_to_all(near, 'mem', split_axis=0, concat_axis=0, tiled=True)  26.1 us
    all_to_all x7, waiting for transfers between devices, exchange(): near = lax.all_to_all(near, 'mem', split_axis=0, concat_axis=0, tiled=True)  19 us
    pallas_call x4, Pallas kernels, outside(): call(functools.partial(outside_kernel, members, cap, old, new), [VMEM] *...  13.8 us
    all_to_all x1, blocking collectives, local(): lax.all_to_all(sums, ('grp', 'mem'), split_axis=0, concat_axis=0, tiled=T...  12.5 us
    unnamed x51, local copies, waits for them, and re-layouts  11.8 us
    ppermute x7, starting transfers between devices, exchange(): first = lax.ppermute(first, ('grp', 'mem'), first_route)  8.78 us
    ppermute x7, waiting for transfers between devices, exchange(): first = lax.ppermute(first, ('grp', 'mem'), first_route)  7.94 us
    pallas_call x6, Pallas kernels, inside(): call(functools.partial(inside_kernel, x is not None, lift is not None), [...  4.23 us
  transfers between devices with their start and end apart: 21, of which 11 were waited for; matrix products, arithmetic and copies ran while one was open for 0% of the time, Pallas kernels for 4%

commit v1 on v0

v1 whole, which is shorter than its diff:
```python
import functools
import math

import jax
import jax.numpy as jnp
from jax import lax
from jax.experimental import pallas as pl
from jax.experimental.pallas import tpu as pltpu
from jax.sharding import PartitionSpec as P

EDGE = 16
DEG = 3
CELLS = 4096
MASS_TERM = 1.0
LOWER_BOUND = 0.25
UPPER_BOUND = 2.0
THETA = 0.5 * (UPPER_BOUND + LOWER_BOUND)
DELTA = 0.5 * (UPPER_BOUND - LOWER_BOUND)
SIGMA = THETA / DELTA

LANES = 128
BLK = 8
TILES = CELLS // LANES
F32 = jnp.float32
VMEM = pl.BlockSpec(memory_space=pltpu.VMEM)
HBM = pl.BlockSpec(memory_space=pltpu.HBM)
PARAMS = pltpu.CompilerParams(vmem_limit_bytes=8 * 1024 * 1024)


def lane_id():
    return lax.broadcasted_iota(jnp.int32, (BLK, LANES), 1)


def sub_id():
    return lax.broadcasted_iota(jnp.int32, (BLK, LANES), 0)


def roll(v, shift):
    shift = shift % LANES
    return v if shift == 0 else pltpu.roll(v, shift, 1)


def tile(m):
    return slice(m * LANES, (m + 1) * LANES)


def pack_faces(values, lane):
    k, g = lane & 15, lane >> 4
    faces = [[], [], [], []]
    for p in range(2):
        low = high = None
        for t in range(16):
            moved = roll(values[16 * p + t], t)
            low = moved if t == 0 else jnp.where(k == t, moved, low)
            high = moved if t == 0 else jnp.where(k == (15 + t) % 16, moved, high)
        faces[0].append(low)
        faces[1].append(roll(high, -15))
        low = high = None
        for t in range(8):
            i = 8 * p + t
            first = roll(values[2 * i], 16 * t)
            last = roll(values[2 * i + 1], 16 * t + 16)
            low = first if t == 0 else jnp.where(g == t, first, low)
            high = last if t == 0 else jnp.where(g == t, last, high)
        faces[2].append(low)
        faces[3].append(high)
    return faces


def unpack_k(low, high, lane, m):
    t = m % 16
    return jnp.where((lane & 15) == 0, roll(low[m // 16], -t), roll(high[m // 16], 15 - t))


def unpack_j(low, high, m):
    i = m // 2
    if m % 2 == 0:
        return roll(low[i // 8], -16 * (i % 8))
    return roll(high[i // 8], 112 - 16 * (i % 8))


def pick(values, index):
    return jnp.take_along_axis(values, index, axis=0, mode="promise_in_bounds")


def lane_sum(v):
    return jnp.sum(v, axis=1, keepdims=True)


def splat(column):
    return jnp.broadcast_to(column, (BLK, LANES))


class Table:
    OWNER, SLOT, BLOCK, PLANE, EVEN, LOWER, UPPER, HANG = 0, 4, 8, 12, 14, 15, 16, 17
    SIZE = 23

    def __init__(self, ref):
        self.ref = ref

    def __call__(self, n):
        return self.ref[n * BLK : (n + 1) * BLK, :]


def gather_ghosts(near_tile, members, first, second, table, ghosts, lane, rows):
    even = table(Table.EVEN) == 1
    for d in range(6):
        for n in range(rows):
            if d < 4:
                v = None
                for m in range(members):
                    source, index = near_tile(m, d, n)
                    found = pick(source, index)
                    v = found if m == 0 else jnp.where(table(Table.OWNER + d) == m, found, v)
            else:
                a, b = first[n * BLK : (n + 1) * BLK, :], second[n * BLK : (n + 1) * BLK, :]
                v = jnp.where(even, b, a) if d == 4 else jnp.where(even, a, b)
                inside = table(Table.LOWER if d == 4 else Table.UPPER) == 1
                v = jnp.where(inside, pick(v, table(Table.PLANE + d - 4)), 0.0)
            at = (d * rows + n) * BLK
            ghosts[0, at : at + BLK, :] = v
    for stage in range(2):
        for d in range(6):
            bit = 16 if stage else (2 if d < 2 else 1)
            low = (lane & bit) == 0
            for n in range(rows):
                at = (d * rows + n) * BLK
                v = ghosts[stage, at : at + BLK, :]
                ghosts[stage + 1, at : at + BLK, :] = v + jnp.where(low, roll(v, -bit), roll(v, bit))
    result = []
    for d in range(6):
        hang = table(Table.HANG + d) == 1
        tiles = []
        for n in range(rows):
            at = (d * rows + n) * BLK
            tiles.append(jnp.where(hang, ghosts[2, at : at + BLK, :] * 0.25, ghosts[0, at : at + BLK, :]))
        result.append(tiles)
    return result


def step_ghosts(members, cap, near, first, second, table, ghosts, lane):
    def near_tile(m, d, n):
        start = n * cap
        at = start // BLK * BLK
        return near[m, at : at + BLK, :], table(Table.SLOT + d) + (start - at)

    return gather_ghosts(near_tile, members, first, second, table, ghosts, lane, 6)


def emit_planes(low, high, even, at, first, second):
    for n in range(2):
        span = slice((at + n) * BLK, (at + n + 1) * BLK)
        first[span, :] = jnp.where(even, high[n], low[n])
        second[span, :] = jnp.where(even, low[n], high[n])


def emit_channel(c, values, chosen, table, payload, first, second, staged, sems, lane, members, cap):
    packed = pack_faces(values, lane)
    emit_planes(values[:2], values[-2:], table(Table.EVEN) == 1, 2 * c, first, second)
    sub = sub_id()
    for m in range(members):
        want = chosen[m * BLK : (m + 1) * BLK, :]
        face, block = want >> 3, want & 7
        for u in range(2 * cap // BLK):
            out = None
            for p in range(2):
                if not u * BLK <= p * cap < (u + 1) * BLK:
                    continue
                v = None
                for f in range(4):
                    found = pick(packed[f][p], block)
                    v = found if f == 0 else jnp.where(face == f, found, v)
                out = v if out is None else jnp.where(sub < p * cap - u * BLK, out, v)
            at = c * 2 * cap + u * BLK
            staged[m, at : at + BLK, :] = out
    part = pl.ds(c * 2 * cap, 2 * cap)
    pltpu.make_async_copy(staged.at[:, part, :], payload.at[:, part, :], sems.at[c]).start()


def emit_wait(payload, staged, sems, cap):
    for c in range(3):
        part = pl.ds(c * 2 * cap, 2 * cap)
        pltpu.make_async_copy(staged.at[:, part, :], payload.at[:, part, :], sems.at[c]).wait()


def prepare_kernel(
    members, groups, cap, viscosity_hbm, refinement_hbm, owner_hbm, block_hbm, plane_hbm, hanging_hbm, coarse_rows,
    eff, payload, first, second, tables,
    viscosity, refinement, face_owner, face_block, plane_block, hanging, staged, sems, out_sem,
):
    copies = [
        pltpu.make_async_copy(source, target, sems.at[n])
        for n, (source, target) in enumerate(
            [
                (viscosity_hbm, viscosity), (refinement_hbm, refinement), (owner_hbm, face_owner),
                (block_hbm, face_block), (plane_hbm, plane_block), (hanging_hbm, hanging),
            ]
        )
    ]
    for copy in copies:
        copy.start()
    lane, sub = lane_id(), sub_id()
    group = lax.axis_index("grp")
    even = group % 2 == 0
    for copy in copies:
        copy.wait()

    def iotas(width):
        return (
            lax.broadcasted_iota(jnp.int32, (BLK, width), 1), lax.broadcasted_iota(jnp.int32, (BLK, width), 0)
        )

    lane8, sub8 = iotas(BLK)
    lane32, sub32 = iotas(4 * BLK)
    lane64, sub64 = iotas(members * cap)

    def column(row):
        wide = jnp.broadcast_to(row.astype(F32), (BLK, BLK))
        return lane_sum(jnp.where(lane8 == sub8, wide, 0.0))

    def put(n, value):
        tables[n * BLK : (n + 1) * BLK, :] = splat(value).astype(jnp.int32)

    scale = jnp.exp2(-splat(column(refinement[...])))
    values = []
    for m in range(TILES):
        v = viscosity[:, tile(m)] * scale
        eff[:, tile(m)] = v
        values.append(v)
    packed = pack_faces(values, lane)
    emit_planes(values[:2], values[-2:], even, 0, first, second)

    row = jnp.broadcast_to(face_owner[...].astype(F32), (BLK, 4 * BLK))
    wanted = jnp.zeros((BLK, members * cap), F32)
    for d in range(4):
        place = 4 * sub32 + d
        owner = lane_sum(jnp.where(lane32 == place, row, 0.0))
        slot = lane_sum(jnp.where((lane32 < place) & (row == owner), 1.0, 0.0))
        block = column(face_block[d : d + 1, :])
        put(Table.OWNER + d, owner)
        put(Table.SLOT + d, slot)
        put(Table.BLOCK + d, block)
        target = jnp.broadcast_to(owner * cap + slot, (BLK, members * cap))
        want = jnp.broadcast_to(block + (d ^ 1) * BLK, (BLK, members * cap))
        wanted = wanted + jnp.where(lane64.astype(F32) == target, want, 0.0)
    wanted = jnp.broadcast_to(jnp.sum(wanted, axis=0, keepdims=True), (BLK, members * cap))
    for d in range(2):
        put(Table.PLANE + d, column(plane_block[d : d + 1, :]))
    for n, flag in ((Table.EVEN, even), (Table.LOWER, group > 0), (Table.UPPER, group < groups - 1)):
        tables[n * BLK : (n + 1) * BLK, :] = jnp.full((BLK, LANES), jnp.where(flag, 1, 0), jnp.int32)
    for d in range(6):
        put(Table.HANG + d, hanging[:, d : d + 1])

    columns = BLK * 3
    for n in range(members):
        for f in range(4):
            for p in range(2):
                at = (f * 2 + p) * BLK
                staged[n, at : at + BLK, :] = packed[f][p]
        request = lane_sum(jnp.where(lane64 == n * cap + sub64 % cap, wanted, 0.0))
        last = splat(request)
        at, off = divmod(n * columns, LANES)
        for v in range(3):
            rows = slice(v * BLK, (v + 1) * BLK)
            part = roll(coarse_rows[rows, tile(at)], v * columns - off)
            if off + columns > LANES:
                more = roll(coarse_rows[rows, tile(at + 1)], v * columns - off)
                part = jnp.where(lane < v * columns + LANES - off, part, more)
            last = jnp.where((lane >= v * columns) & (lane < (v + 1) * columns), part, last)
        staged[n, 8 * BLK : 9 * BLK, :] = last
    copy = pltpu.make_async_copy(staged, payload, out_sem)
    copy.start()
    copy.wait()


def weights_kernel(
    members, cap, near, from_first, from_second, eff, forcing, tables,
    step, payload, first, second, wi, gk, gj, gi, diagonal, inverse, chosen, coarse, ghosts, staged, sems,
):
    lane = lane_id()
    k, g = lane & 15, lane >> 4
    table = Table(tables)
    for n in range(members):
        last = near[n, 8 * BLK : 9 * BLK, :]
        coarse[n * BLK : (n + 1) * BLK, :] = last
        chosen[n * BLK : (n + 1) * BLK, :] = splat(last[:, LANES - 1 :]).astype(jnp.int32)

    def near_tile(m, d, n):
        at = ((d ^ 1) * 2 + n) * BLK
        return near[m, at : at + BLK, :], table(Table.BLOCK + d)

    ghost = gather_ghosts(near_tile, members, from_first, from_second, table, ghosts, lane, 2)
    values = [eff[:, tile(m)] for m in range(TILES)]
    start = [[], [], []]
    for m in range(TILES):
        i, h = divmod(m, 2)
        e = values[m]
        side_k = unpack_k(ghost[0], ghost[1], lane, m)
        side_j = unpack_j(ghost[2], ghost[3], m)
        ends_j = (g == 0) if h == 0 else (g == 7)
        n0 = jnp.where(k == 0, side_k, roll(e, 1))
        n1 = jnp.where(k == 15, side_k, roll(e, -1))
        n2 = jnp.where(g == 0, side_j if h == 0 else roll(values[m - 1], 16), roll(e, 16))
        n3 = jnp.where(g == 7, side_j if h == 1 else roll(values[m + 1], -16), roll(e, -16))
        n4 = ghost[4][h] if i == 0 else values[m - 2]
        n5 = ghost[5][h] if i == EDGE - 1 else values[m + 2]
        w = [0.5 * (e + n) for n in (n0, n1, n2, n3, n4, n5)]
        diag = MASS_TERM * e
        for d in range(6):
            diag = diag + w[d]
        inv = 1.0 / diag
        diagonal[:, tile(m)] = diag
        inverse[:, tile(m)] = inv
        wi[0, :, tile(m)] = jnp.where(k == 0, 0.0, w[0])
        wi[1, :, tile(m)] = jnp.where(k == 15, 0.0, w[1])
        wi[2, :, tile(m)] = jnp.where(ends_j, 0.0, w[2]) if h == 0 else w[2]
        wi[3, :, tile(m)] = jnp.where(ends_j, 0.0, w[3]) if h == 1 else w[3]
        wi[4, :, tile(m)] = w[4]
        gk[:, tile(m)] = jnp.where(k == 0, w[0], jnp.where(k == 15, w[1], 0.0))
        gj[:, tile(m)] = jnp.where(ends_j, w[2 + h], 0.0)
        if i == 0:
            gi[:, tile(h)] = w[4]
        if i == EDGE - 1:
            gi[:, tile(2 + h)] = w[5]
        scale = inv * (1.0 / THETA)
        for c in range(3):
            s = forcing[c, :, tile(m)] * scale
            step[c, :, tile(m)] = s
            start[c].append(s)
    for c in range(3):
        emit_channel(c, start[c], chosen, table, payload, first, second, staged, sems, lane, members, cap)
    emit_wait(payload, staged, sems, cap)


def inside_kernel(has_x, has_lift, *refs):
    refs = list(refs)
    residual, step, wi, diagonal = refs[:4]
    refs = refs[4:]
    x = refs.pop(0) if has_x else None
    lift = refs.pop(0) if has_lift else None
    new_residual = refs.pop(0)
    new_x = refs.pop(0) if has_x else None
    g = lane_id() >> 4
    for c in range(3):
        up = None if not has_lift else lift[c * BLK : (c + 1) * BLK, :]
        for m in range(TILES):
            i, h = divmod(m, 2)
            s = step[c, :, tile(m)]
            n2, n3 = roll(s, 16), roll(s, -16)
            if h == 1:
                n2 = jnp.where(g == 0, roll(step[c, :, tile(m - 1)], 16), n2)
            else:
                n3 = jnp.where(g == 7, roll(step[c, :, tile(m + 1)], -16), n3)
            acc = residual[c, :, tile(m)] - diagonal[:, tile(m)] * s
            acc = acc + wi[0, :, tile(m)] * roll(s, 1)
            acc = acc + wi[1, :, tile(m)] * roll(s, -1)
            acc = acc + wi[2, :, tile(m)] * n2
            acc = acc + wi[3, :, tile(m)] * n3
            if i > 0:
                acc = acc + wi[4, :, tile(m)] * step[c, :, tile(m - 2)]
            if i < EDGE - 1:
                acc = acc + wi[4, :, tile(m + 2)] * step[c, :, tile(m + 2)]
            new_residual[c, :, tile(m)] = acc
            if has_x:
                total = x[c, :, tile(m)] + s
                if has_lift:
                    total = total + up
                new_x[c, :, tile(m)] = total


def add_ghosts(c, m, value, ghost, gk, gj, gi, lane):
    i, h = divmod(m, 2)
    pair = slice(2 * c, 2 * c + 2)
    value = value + gk[:, tile(m)] * unpack_k(ghost[0][pair], ghost[1][pair], lane, m)
    value = value + gj[:, tile(m)] * unpack_j(ghost[2][pair], ghost[3][pair], m)
    if i == 0:
        value = value + gi[:, tile(h)] * ghost[4][2 * c + h]
    if i == EDGE - 1:
        value = value + gi[:, tile(2 + h)] * ghost[5][2 * c + h]
    return value


def outside_kernel(
    members, cap, old, new, near, from_first, from_second, residual, step, inverse, gk, gj, gi, tables, chosen,
    new_residual, new_step, payload, first, second, ghosts, staged, sems,
):
    lane = lane_id()
    table = Table(tables)
    ghost = step_ghosts(members, cap, near, from_first, from_second, table, ghosts, lane)
    for c in range(3):
        values = []
        for m in range(TILES):
            r = add_ghosts(c, m, residual[c, :, tile(m)], ghost, gk, gj, gi, lane)
            new_residual[c, :, tile(m)] = r
            s = old * step[c, :, tile(m)] + new * (r * inverse[:, tile(m)])
            new_step[c, :, tile(m)] = s
            values.append(s)
        emit_channel(c, values, chosen, table, payload, first, second, staged, sems, lane, members, cap)
    emit_wait(payload, staged, sems, cap)


def last_kernel(
    members, cap, near, from_first, from_second, residual, gk, gj, gi, tables, new_residual, ghosts, staged, sems,
):
    lane = lane_id()
    ghost = step_ghosts(members, cap, near, from_first, from_second, Table(tables), ghosts, lane)
    copies = []
    for c in range(3):
        for m in range(TILES):
            staged[c, :, tile(m)] = add_ghosts(c, m, residual[c, :, tile(m)], ghost, gk, gj, gi, lane)
        copies.append(pltpu.make_async_copy(staged.at[c], new_residual.at[c], sems.at[c]))
        copies[c].start()
    for copy in copies:
        copy.wait()


def coarse_kernel(
    members, devices, cap, near, from_first, from_second, residual, gk, gj, gi, tables, coarse,
    new_residual, payload, ghosts,
):
    lane, sub = lane_id(), sub_id()
    ghost = step_ghosts(members, cap, near, from_first, from_second, Table(tables), ghosts, lane)
    placed = jnp.zeros((BLK, LANES), F32)
    for c in range(3):
        sums = [None] * 4
        for m in range(TILES):
            r = add_ghosts(c, m, residual[c, :, tile(m)], ghost, gk, gj, gi, lane)
            new_residual[c, :, tile(m)] = r
            sums[m % 4] = r if sums[m % 4] is None else sums[m % 4] + r
        total = splat(lane_sum((sums[0] + sums[1]) + (sums[2] + sums[3])))
        placed = jnp.where(lane == 3 * sub + c, total, placed)
    own = jnp.sum(placed, axis=0, keepdims=True) * (1.0 / math.sqrt(CELLS))
    own = jnp.broadcast_to(own, (BLK, LANES))
    columns = BLK * 3
    wide = -(-members * columns // LANES)
    rows = [jnp.zeros((BLK, LANES), F32) for _ in range(wide)]
    for n in range(members):
        for v in range(3):
            have = jnp.where(lane < columns, roll(coarse[n * BLK : (n + 1) * BLK, :], -v * columns), 0.0)
            part = splat(lane_sum(have * own))
            place = n * columns + v * BLK
            for t in range(place // LANES, (place + BLK - 1) // LANES + 1):
                rows[t] = jnp.where(lane + t * LANES == place + sub, part, rows[t])
    out = jnp.zeros((BLK, LANES), F32)
    for t in range(wide):
        out = jnp.where(sub == t, jnp.sum(rows[t], axis=0, keepdims=True), out)
    for n in range(devices):
        payload[n * BLK : (n + 1) * BLK, :] = out


def lift_kernel(
    members, groups, cap, arrived, residual, eff, inverse, gk, gj, gi, tables, chosen,
    new_residual, step, lift, payload, first, second, staged, sems,
):
    lane, sub = lane_id(), sub_id()
    k = lane & 15
    table = Table(tables)
    wide = -(-members * BLK * 3 // LANES)
    group, member = lax.axis_index("grp"), lax.axis_index("mem")
    base = [jnp.maximum(group - 1, 0), group, jnp.minimum(group + 1, groups - 1)]
    known = []
    for n in range(3):
        total = jnp.zeros((BLK, LANES), F32)
        for p in range(members):
            at = pl.multiple_of((base[n] * members + p) * BLK, BLK)
            total = total + arrived[pl.ds(at, BLK), :]
        if n != 1:
            total = jnp.where(table(Table.LOWER if n == 0 else Table.UPPER) == 1, total, 0.0)
        known.append([jnp.broadcast_to(total[t : t + 1, :], (BLK, LANES)) for t in range(wide)])

    def look_up(values, block):
        found = []
        for c in range(3):
            total = jnp.zeros((BLK, LANES), F32)
            for t in range(wide):
                total = total + jnp.where(lane + t * LANES == 3 * block + c, values[t], 0.0)
            found.append(splat(lane_sum(total)))
        return found

    own = look_up(known[1], member * BLK + sub)
    side = [look_up(known[1], table(Table.OWNER + d) * BLK + table(Table.BLOCK + d)) for d in range(4)]
    below = look_up(known[0], member * BLK + table(Table.PLANE))
    above = look_up(known[2], member * BLK + table(Table.PLANE + 1))
    for c in range(3):
        values = []
        lift[c * BLK : (c + 1) * BLK, :] = own[c]
        drop_k = own[c] - jnp.where(k == 0, side[0][c], side[1][c])
        drop_j = [own[c] - side[2][c], own[c] - side[3][c]]
        drop_i = [own[c] - below[c], own[c] - above[c]]
        for m in range(TILES):
            i, h = divmod(m, 2)
            applied = (MASS_TERM * eff[:, tile(m)]) * own[c]
            applied = applied + gk[:, tile(m)] * drop_k + gj[:, tile(m)] * drop_j[h]
            if i == 0:
                applied = applied + gi[:, tile(h)] * drop_i[0]
            if i == EDGE - 1:
                applied = applied + gi[:, tile(2 + h)] * drop_i[1]
            r = residual[c, :, tile(m)] - applied
            new_residual[c, :, tile(m)] = r
            s = r * (inverse[:, tile(m)] * (1.0 / THETA))
            step[c, :, tile(m)] = s
            values.append(s)
        emit_channel(c, values, chosen, table, payload, first, second, staged, sems, lane, members, cap)
    emit_wait(payload, staged, sems, cap)


def local(
    forcing, viscosity, refinement, face_owner, face_block, plane_block, hanging, coarse_solver
):
    groups, members = lax.axis_size("grp"), lax.axis_size("mem")
    cap = 8 * BLK // members
    devices = groups * members
    field = jax.ShapeDtypeStruct(forcing.shape, F32)
    scalar_field = jax.ShapeDtypeStruct(viscosity.shape, F32)

    def array(*shape):
        return jax.ShapeDtypeStruct(shape, F32)

    def ints(*shape):
        return jax.ShapeDtypeStruct(shape, jnp.int32)

    def scratch(*shape):
        return pltpu.VMEM(shape, F32)

    def call(body, in_specs, out_shape, out_specs, scratch_shapes, name):
        return pl.pallas_call(
            body,
            out_shape=out_shape,
            in_specs=in_specs,
            out_specs=out_specs,
            scratch_shapes=scratch_shapes,
            compiler_params=PARAMS,
            cost_estimate=pl.CostEstimate(flops=2_000_000, bytes_accessed=2_000_000, transcendentals=0),
            name=name,
        )

    first_route = [(q * members + m, (q ^ 1) * members + m) for q in range(groups) for m in range(members)]
    second_route = []
    for q in range(groups):
        for m in range(members):
            if q == 0 or q == groups - 1:
                second_route.append((q * members + m, q * members + (m ^ 1)))
            else:
                second_route.append((q * members + m, (q + 1 if q % 2 else q - 1) * members + m))

    def exchange(payload, first, second):
        near = lax.all_to_all(payload, "mem", split_axis=0, concat_axis=0, tiled=True)
        first = lax.ppermute(first, ("grp", "mem"), first_route)
        second = lax.ppermute(second, ("grp", "mem"), second_route)
        return near, first, second

    per = 9 * BLK
    solver_rows = jnp.pad(coarse_solver[0], ((0, 0), (0, -coarse_solver.shape[2] % LANES)))
    eff, payload, first, second, tables = call(
        functools.partial(prepare_kernel, members, groups, cap),
        [HBM] * 6 + [VMEM],
        [scalar_field, array(members, per, LANES), array(16, LANES), array(16, LANES), ints(Table.SIZE * BLK, LANES)],
        [VMEM, HBM, VMEM, VMEM, VMEM],
        [
            scratch(BLK, CELLS), pltpu.VMEM((1, BLK), jnp.int32), pltpu.VMEM((1, 4 * BLK), jnp.int32),
            pltpu.VMEM((4, BLK), jnp.int32), pltpu.VMEM((2, BLK), jnp.int32), pltpu.VMEM((BLK, 6), jnp.int32),
            scratch(members, per, LANES), pltpu.SemaphoreType.DMA((6,)), pltpu.SemaphoreType.DMA,
        ],
        "prepare",
    )(viscosity, refinement.reshape(1, BLK), face_owner.T, face_block.T, plane_block.T, hanging, solver_rows)
    arrived, from_first, from_second = exchange(payload, first, second)

    payload_out = [array(members, 6 * cap, LANES), array(48, LANES), array(48, LANES)]
    payload_specs = [HBM, VMEM, VMEM]
    ghost_scratch = [scratch(3, 6 * 48, LANES)]
    emit_scratch = [scratch(members, 6 * cap, LANES), pltpu.SemaphoreType.DMA((3,))]

    step, payload, first, second, wi, gk, gj, gi, diagonal, inverse, chosen, coarse = call(
        functools.partial(weights_kernel, members, cap),
        [VMEM] * 6,
        [field] + payload_out
        + [array(5, BLK, CELLS), scalar_field, scalar_field, array(BLK, 4 * LANES), scalar_field, scalar_field]
        + [ints(members * BLK, LANES), array(members * BLK, LANES)],
        [VMEM] + payload_specs + [VMEM] * 8,
        [scratch(3, 6 * 16, LANES)] + emit_scratch,
        "weights",
    )(arrived, from_first, from_second, eff, forcing, tables)

    def inside(residual, step, x=None, lift=None):
        operands = [residual, step, wi, diagonal] + [a for a in (x, lift) if a is not None]
        out = [field] + ([field] if x is not None else [])
        result = call(
            functools.partial(inside_kernel, x is not None, lift is not None),
            [VMEM] * len(operands), out, [VMEM] * len(out), [], "inside",
        )(*operands)
        return result if x is not None else (result[0], step)

    def outside(arrived, from_first, from_second, residual, step, old, new):
        return call(
            functools.partial(outside_kernel, members, cap, old, new),
            [VMEM] * 11,
            [field, field] + payload_out,
            [VMEM, VMEM] + payload_specs,
            ghost_scratch + emit_scratch,
            "outside",
        )(arrived, from_first, from_second, residual, step, inverse, gk, gj, gi, tables, chosen)

    rho = 1.0 / SIGMA
    factors = []
    for _ in range(DEG - 1):
        rho_next = 1.0 / (2.0 * SIGMA - rho)
        factors.append((rho_next * rho, 2.0 * rho_next / DELTA))
        rho = rho_next

    def steps(residual, step, payload, first, second, x, lift):
        for old, new in factors:
            arrived, from_first, from_second = exchange(payload, first, second)
            residual, x = inside(residual, step, x, lift)
            lift = None
            residual, step, payload, first, second = outside(
                arrived, from_first, from_second, residual, step, old, new
            )
        arrived, from_first, from_second = exchange(payload, first, second)
        residual, x = inside(residual, step, x, lift)
        return arrived, from_first, from_second, residual, x

    arrived, from_first, from_second, residual, x = steps(forcing, step, payload, first, second, None, None)
    residual, payload = call(
        functools.partial(coarse_kernel, members, devices, cap),
        [VMEM] * 9,
        [field, array(devices * BLK, LANES)],
        [VMEM] * 2,
        ghost_scratch,
        "coarse",
    )(arrived, from_first, from_second, residual, gk, gj, gi, tables, coarse)
    sums = payload.reshape(devices, BLK, LANES)
    sums = lax.all_to_all(sums, ("grp", "mem"), split_axis=0, concat_axis=0, tiled=True).reshape(-1, LANES)
    residual, step, lift, payload, first, second = call(
        functools.partial(lift_kernel, members, groups, cap),
        [VMEM] * 9,
        [field, field, array(3 * BLK, LANES)] + payload_out,
        [VMEM] * 3 + payload_specs,
        emit_scratch,
        "lift",
    )(sums, residual, eff, inverse, gk, gj, gi, tables, chosen)
    arrived, from_first, from_second, residual, x = steps(residual, step, payload, first, second, x, lift)
    residual = call(
        functools.partial(last_kernel, members, cap),
        [VMEM] * 8,
        [field],
        [HBM],
        ghost_scratch + [scratch(3, BLK, CELLS), pltpu.SemaphoreType.DMA((3,))],
        "last",
    )(arrived, from_first, from_second, residual, gk, gj, gi, tables)[0]
    return x, residual


def solution(mesh):
    in_specs = (
        P(None, ("grp", "mem"), None),
        P(("grp", "mem"), None),
        P(("grp", "mem")),
        P(("grp", "mem"), None),
        P(("grp", "mem"), None),
        P(("grp", "mem"), None),
        P(("grp", "mem"), None),
        P("grp", "mem", None),
    )
    out_specs = (P(None, ("grp", "mem"), None), P(None, ("grp", "mem"), None))
    return jax.shard_map(local, mesh=mesh, in_specs=in_specs, out_specs=out_specs, check_vma=False)
```

time: 119 us -> 104 us (0.87)
  Pallas kernels: 30.1 us -> 18.2 us
  waiting for transfers between devices: 27 us -> 24.8 us
    pallas_call x4, Pallas kernels: 13.8 us -> 6.92 us  [outside(): call(functools.partial(outside_kernel, members, cap, old, new), [VMEM] *...]
    pallas_call x5, Pallas kernels: 12.1 us -> 6.88 us  [the longest x1 1.59 us: local(): call(functools.partial(coarse_kernel, members, devices, cap), [VMEM] * 9,...]
    all_to_all x7, waiting for transfers between devices: 19 us -> 16.4 us  [exchange(): lax.all_to_all(payload, 'mem', split_axis=0, concat_axis=0, tiled=True)]
    unnamed x51 -> x42, local copies, waits for them, and re-layouts: 11.8 us -> 10.1 us
  transfers between devices with their start and end apart: 21 -> 21, of which waited for: 11 -> 12; matrix products, arithmetic and copies ran while one was open for 0% -> 0% of each run, Pallas kernels for 4% -> 4%
where the time goes in v1:
time: 104 us; the launch traced here: 103 us
  starting transfers between devices  35.4 us (34%)
  waiting for transfers between devices  24.8 us (24%)
  Pallas kernels  18.2 us (18%)
  blocking collectives  12.5 us (12%)
  local copies, waits for them, and re-layouts  10.9 us (10%)
    all_to_all x7, starting transfers between devices, exchange(): lax.all_to_all(payload, 'mem', split_axis=0, concat_axis=0, tiled=True)  25.9 us
    all_to_all x7, waiting for transfers between devices, exchange(): lax.all_to_all(payload, 'mem', split_axis=0, concat_axis=0, tiled=True)  16.4 us
    all_to_all x1, blocking collectives, local(): lax.all_to_all(sums, ('grp', 'mem'), split_axis=0, concat_axis=0, tiled=T...  12.5 us
    unnamed x42, local copies, waits for them, and re-layouts  10.1 us
    ppermute x7, starting transfers between devices, exchange(): first = lax.ppermute(first, ('grp', 'mem'), first_route)  8.71 us
    ppermute x7, waiting for transfers between devices, exchange(): first = lax.ppermute(first, ('grp', 'mem'), first_route)  8.43 us
    pallas_call x4, Pallas kernels, outside(): call(functools.partial(outside_kernel, members, cap, old, new), [VMEM] *...  6.92 us
    pallas_call x6, Pallas kernels, inside(): call(functools.partial(inside_kernel, x is not None, lift is not None), [...  4.44 us
  transfers between devices with their start and end apart: 21, of which 12 were waited for; matrix products, arithmetic and copies ran while one was open for 0% of the time, Pallas kernels for 4%

profile of v1, /device:TPU:0, one launch (start us, length us, event | category | flops | bytes accessed | tf_op | source)
XLA Modules:
  0.0 102.9 jit_solution(2441835616318193019)
XLA Ops:
  3.9 5.2 %all-to-all-start = ((f32[8,72,128]{2,1,0:T(8,128)}), f32[8,72,128]{2,1,0:T(8,128)S(1)}, u32[]{:S(2)}, u32[]{:S(2)}) async-start(f32[8,72,128]{2,1,0:T(8,128)} %get-tuple-element.57), calls=%async_computation | async-start | bytes 589824 | tf_op jit(solution)/shard_map/all_to_all | solution.py:547
  10.9 1.8 %collective-permute-done.from_first = f32[16,128]{1,0:T(8,128)S(1)} collective-permute-done((f32[16,128]{1,0:T(8,128)S(1)}, f32[16,128]{1,0:T(8,128)S(1)}, u32[]{:S(2)}, u32[]{:S(2)}) %collective-permute-start) | collective-permute-done | bytes 8224 | tf_op jit(solution)/shard_map/ppermute | solution.py:548
  12.7 3.6 %all-to-all-done.near = f32[8,72,128]{2,1,0:T(8,128)S(1)} async-done(((f32[8,72,128]{2,1,0:T(8,128)}), f32[8,72,128]{2,1,0:T(8,128)S(1)}, u32[]{:S(2)}, u32[]{:S(2)}) %all-to-all-start) | async-done | bytes 294944 | tf_op jit(solution)/shard_map/all_to_all | solution.py:547
  17.9 3.4 %all-to-all-start.1 = ((f32[8,48,128]{2,1,0:T(8,128)}), f32[8,48,128]{2,1,0:T(8,128)S(1)}, u32[]{:S(2)}, u32[]{:S(2)}) async-start(f32[8,48,128]{2,1,0:T(8,128)} %get-tuple-element.62), calls=%async_computation.1 | async-start | bytes 393216 | tf_op jit(solution)/shard_map/all_to_all | solution.py:547
  21.3 1.6 %collective-permute-start.2 = (f32[48,128]{1,0:T(8,128)S(1)}, f32[48,128]{1,0:T(8,128)S(1)}, u32[]{:S(2)}, u32[]{:S(2)}) collective-permute-start(f32[48,128]{1,0:T(8,128)S(1)} %get-tuple-element.63), channel_id=1, source_target_pairs={{0,8},{1,9},{2,10},{3,11},{4,12},{5,13},{6,14},{7,15},{8,0},{9,1},... | collective-permute-start | bytes 73736 | tf_op jit(solution)/shard_map/ppermute | solution.py:548
  25.2 2.3 %all-to-all-done.1.near = f32[8,48,128]{2,1,0:T(8,128)S(1)} async-done(((f32[8,48,128]{2,1,0:T(8,128)}), f32[8,48,128]{2,1,0:T(8,128)S(1)}, u32[]{:S(2)}, u32[]{:S(2)}) %all-to-all-start.1) | async-done | bytes 196640 | tf_op jit(solution)/shard_map/all_to_all | solution.py:547
  27.5 1.7 %outside.4 = (f32[3,8,4096]{2,1,0:T(8,128)S(1)}, f32[3,8,4096]{2,1,0:T(8,128)S(1)}, f32[8,48,128]{2,1,0:T(8,128)}, f32[48,128]{1,0:T(8,128)S(1)}, f32[48,128]{1,0:T(8,128)S(1)}) custom-call(f32[8,48,128]{2,1,0:T(8,128)S(1)} %all-to-all-done.1.near, f32[48,128]{1,0:T(8,128)S(1)} %collective-permute-done.2.from_first, ...), custom_call_target="tpu_custom_call" | custom-call | flops 2000000 | bytes 2000000 | tf_op jit(solution)/shard_map/outside/pallas_call | solution.py:594
  29.9 3.4 %all-to-all-start.2 = ((f32[8,48,128]{2,1,0:T(8,128)}), f32[8,48,128]{2,1,0:T(8,128)S(1)}, u32[]{:S(2)}, u32[]{:S(2)}) async-start(f32[8,48,128]{2,1,0:T(8,128)} %get-tuple-element.73), calls=%async_computation.2 | async-start | bytes 393216 | tf_op jit(solution)/shard_map/all_to_all | solution.py:547
  33.4 1.6 %collective-permute-start.4 = (f32[48,128]{1,0:T(8,128)S(1)}, f32[48,128]{1,0:T(8,128)S(1)}, u32[]{:S(2)}, u32[]{:S(2)}) collective-permute-start(f32[48,128]{1,0:T(8,128)S(1)} %get-tuple-element.74), channel_id=1, source_target_pairs={{0,8},{1,9},{2,10},{3,11},{4,12},{5,13},{6,14},{7,15},{8,0},{9,1},... | collective-permute-start | bytes 73736 | tf_op jit(solution)/shard_map/ppermute | solution.py:548
  37.4 2.1 %all-to-all-done.2.near = f32[8,48,128]{2,1,0:T(8,128)S(1)} async-done(((f32[8,48,128]{2,1,0:T(8,128)}), f32[8,48,128]{2,1,0:T(8,128)S(1)}, u32[]{:S(2)}, u32[]{:S(2)}) %all-to-all-start.2) | async-done | bytes 196640 | tf_op jit(solution)/shard_map/all_to_all | solution.py:547
  39.5 1.7 %outside.5 = (f32[3,8,4096]{2,1,0:T(8,128)S(1)}, f32[3,8,4096]{2,1,0:T(8,128)S(1)}, f32[8,48,128]{2,1,0:T(8,128)}, f32[48,128]{1,0:T(8,128)S(1)}, f32[48,128]{1,0:T(8,128)S(1)}) custom-call(f32[8,48,128]{2,1,0:T(8,128)S(1)} %all-to-all-done.2.near, f32[48,128]{1,0:T(8,128)S(1)} %collective-permute-done.4.from_first, ...), custom_call_target="tpu_custom_call" | custom-call | flops 2000000 | bytes 2000000 | tf_op jit(solution)/shard_map/outside/pallas_call | solution.py:594
  42.7 3.5 %all-to-all-start.3 = ((f32[8,48,128]{2,1,0:T(8,128)}), f32[8,48,128]{2,1,0:T(8,128)S(1)}, u32[]{:S(2)}, u32[]{:S(2)}) async-start(f32[8,48,128]{2,1,0:T(8,128)} %get-tuple-element.79), calls=%async_computation.3 | async-start | bytes 393216 | tf_op jit(solution)/shard_map/all_to_all | solution.py:547
  46.3 1.7 %collective-permute-start.6 = (f32[48,128]{1,0:T(8,128)S(1)}, f32[48,128]{1,0:T(8,128)S(1)}, u32[]{:S(2)}, u32[]{:S(2)}) collective-permute-start(f32[48,128]{1,0:T(8,128)S(1)} %get-tuple-element.80), channel_id=1, source_target_pairs={{0,8},{1,9},{2,10},{3,11},{4,12},{5,13},{6,14},{7,15},{8,0},{9,1},... | collective-permute-start | bytes 73736 | tf_op jit(solution)/shard_map/ppermute | solution.py:548
  54.0 12.5 %all_to_all.40 = f32[32,8,128]{2,1,0:T(8,128)S(1)} all-to-all(f32[32,8,128]{2,1,0:T(8,128)S(1)} %bitcast.8), channel_id=1, replica_groups=mesh['grp'=4,'mem'=8] {'grp','mem'}, dimensions={0} | all-to-all | bytes 262144 | tf_op jit(solution)/shard_map/all_to_all | solution.py:632
  67.7 3.4 %all-to-all-start.5 = ((f32[8,48,128]{2,1,0:T(8,128)}), f32[8,48,128]{2,1,0:T(8,128)S(1)}, u32[]{:S(2)}, u32[]{:S(2)}) async-start(f32[8,48,128]{2,1,0:T(8,128)} %get-tuple-element.89), calls=%async_computation.5 | async-start | bytes 393216 | tf_op jit(solution)/shard_map/all_to_all | solution.py:547
  73.2 1.7 %collective-permute-done.8.from_first = f32[48,128]{1,0:T(8,128)S(1)} collective-permute-done((f32[48,128]{1,0:T(8,128)S(1)}, f32[48,128]{1,0:T(8,128)S(1)}, u32[]{:S(2)}, u32[]{:S(2)}) %collective-permute-start.8) | collective-permute-done | bytes 24608 | tf_op jit(solution)/shard_map/ppermute | solution.py:548
  75.0 2.3 %all-to-all-done.5.near = f32[8,48,128]{2,1,0:T(8,128)S(1)} async-done(((f32[8,48,128]{2,1,0:T(8,128)}), f32[8,48,128]{2,1,0:T(8,128)S(1)}, u32[]{:S(2)}, u32[]{:S(2)}) %all-to-all-start.5) | async-done | bytes 196640 | tf_op jit(solution)/shard_map/all_to_all | solution.py:547
  77.3 1.7 %outside.6 = (f32[3,8,4096]{2,1,0:T(8,128)S(1)}, f32[3,8,4096]{2,1,0:T(8,128)S(1)}, f32[8,48,128]{2,1,0:T(8,128)}, f32[48,128]{1,0:T(8,128)S(1)}, f32[48,128]{1,0:T(8,128)S(1)}) custom-call(f32[8,48,128]{2,1,0:T(8,128)S(1)} %all-to-all-done.5.near, f32[48,128]{1,0:T(8,128)S(1)} %collective-permute-done.8.from_first, ...), custom_call_target="tpu_custom_call" | custom-call | flops 2000000 | bytes 2000000 | tf_op jit(solution)/shard_map/outside/pallas_call | solution.py:594
  79.8 3.5 %all-to-all-start.6 = ((f32[8,48,128]{2,1,0:T(8,128)}), f32[8,48,128]{2,1,0:T(8,128)S(1)}, u32[]{:S(2)}, u32[]{:S(2)}) async-start(f32[8,48,128]{2,1,0:T(8,128)} %get-tuple-element.97), calls=%async_computation.6 | async-start | bytes 393216 | tf_op jit(solution)/shard_map/all_to_all | solution.py:547
  87.2 2.3 %all-to-all-done.6.near = f32[8,48,128]{2,1,0:T(8,128)S(1)} async-done(((f32[8,48,128]{2,1,0:T(8,128)}), f32[8,48,128]{2,1,0:T(8,128)S(1)}, u32[]{:S(2)}, u32[]{:S(2)}) %all-to-all-start.6) | async-done | bytes 196640 | tf_op jit(solution)/shard_map/all_to_all | solution.py:547
  89.4 1.7 %outside.7 = (f32[3,8,4096]{2,1,0:T(8,128)S(1)}, f32[3,8,4096]{2,1,0:T(8,128)S(1)}, f32[8,48,128]{2,1,0:T(8,128)}, f32[48,128]{1,0:T(8,128)S(1)}, f32[48,128]{1,0:T(8,128)S(1)}) custom-call(f32[8,48,128]{2,1,0:T(8,128)S(1)} %all-to-all-done.6.near, f32[48,128]{1,0:T(8,128)S(1)} %collective-permute-done.10.from_first, ...), custom_call_target="tpu_custom_call" | custom-call | flops 2000000 | bytes 2000000 | tf_op jit(solution)/shard_map/outside/pallas_call | solution.py:594
  91.9 3.5 %all-to-all-start.7 = ((f32[8,48,128]{2,1,0:T(8,128)}), f32[8,48,128]{2,1,0:T(8,128)S(1)}, u32[]{:S(2)}, u32[]{:S(2)}) async-start(f32[8,48,128]{2,1,0:T(8,128)} %get-tuple-element.108), calls=%async_computation.7 | async-start | bytes 393216 | tf_op jit(solution)/shard_map/all_to_all | solution.py:547
  97.5 1.8 %collective-permute-done.12.from_first = f32[48,128]{1,0:T(8,128)S(1)} collective-permute-done((f32[48,128]{1,0:T(8,128)S(1)}, f32[48,128]{1,0:T(8,128)S(1)}, u32[]{:S(2)}, u32[]{:S(2)}) %collective-permute-start.12) | collective-permute-done | bytes 24608 | tf_op jit(solution)/shard_map/ppermute | solution.py:548
  99.4 2.3 %all-to-all-done.7.near = f32[8,48,128]{2,1,0:T(8,128)S(1)} async-done(((f32[8,48,128]{2,1,0:T(8,128)}), f32[8,48,128]{2,1,0:T(8,128)S(1)}, u32[]{:S(2)}, u32[]{:S(2)}) %all-to-all-start.7) | async-done | bytes 196640 | tf_op jit(solution)/shard_map/all_to_all | solution.py:547
  (77 shorter events, 31.3 us)
Async XLA Ops:
  1.5 14.9 %copy-start = (f32[3,8,4096]{2,1,0:T(8,128)S(1)}, f32[3,8,4096]{2,1,0:T(8,128)}, u32[]{:S(2)}) copy-start(f32[3,8,4096]{2,1,0:T(8,128)} %refs_0_.1) | copy-start | bytes 1179652
  3.9 12.5 %all-to-all-start = ((f32[8,72,128]{2,1,0:T(8,128)}), f32[8,72,128]{2,1,0:T(8,128)S(1)}, u32[]{:S(2)}, u32[]{:S(2)}) async-start(f32[8,72,128]{2,1,0:T(8,128)} %get-tuple-element.57), calls=%async_computation | async-start | bytes 589824 | tf_op jit(solution)/shard_map/all_to_all | solution.py:547
  9.1 3.7 %collective-permute-start = (f32[16,128]{1,0:T(8,128)S(1)}, f32[16,128]{1,0:T(8,128)S(1)}, u32[]{:S(2)}, u32[]{:S(2)}) collective-permute-start(f32[16,128]{1,0:T(8,128)S(1)} %get-tuple-element.58), channel_id=1, source_target_pairs={{0,8},{1,9},{2,10},{3,11},{4,12},{5,13},{6,14},{7,15},{8,0},{9,1},... | collective-permute-start | bytes 24584 | tf_op jit(solution)/shard_map/ppermute | solution.py:548
  10.6 2.1 %collective-permute-start.1 = (f32[16,128]{1,0:T(8,128)S(1)}, f32[16,128]{1,0:T(8,128)S(1)}, u32[]{:S(2)}, u32[]{:S(2)}) collective-permute-start(f32[16,128]{1,0:T(8,128)S(1)} %get-tuple-element.59), channel_id=1, source_target_pairs={{0,1},{1,0},{2,3},{3,2},{4,5},{5,4},{6,7},{7,6},{8,16},{9,17},{10,... | collective-permute-start | bytes 24584 | tf_op jit(solution)/shard_map/ppermute | solution.py:549
  17.9 9.6 %all-to-all-start.1 = ((f32[8,48,128]{2,1,0:T(8,128)}), f32[8,48,128]{2,1,0:T(8,128)S(1)}, u32[]{:S(2)}, u32[]{:S(2)}) async-start(f32[8,48,128]{2,1,0:T(8,128)} %get-tuple-element.62), calls=%async_computation.1 | async-start | bytes 393216 | tf_op jit(solution)/shard_map/all_to_all | solution.py:547
  21.3 3.9 %collective-permute-start.2 = (f32[48,128]{1,0:T(8,128)S(1)}, f32[48,128]{1,0:T(8,128)S(1)}, u32[]{:S(2)}, u32[]{:S(2)}) collective-permute-start(f32[48,128]{1,0:T(8,128)S(1)} %get-tuple-element.63), channel_id=1, source_target_pairs={{0,8},{1,9},{2,10},{3,11},{4,12},{5,13},{6,14},{7,15},{8,0},{9,1},... | collective-permute-start | bytes 73736 | tf_op jit(solution)/shard_map/ppermute | solution.py:548
  22.9 2.3 %collective-permute-start.3 = (f32[48,128]{1,0:T(8,128)S(1)}, f32[48,128]{1,0:T(8,128)S(1)}, u32[]{:S(2)}, u32[]{:S(2)}) collective-permute-start(f32[48,128]{1,0:T(8,128)S(1)} %get-tuple-element.64), channel_id=1, source_target_pairs={{0,1},{1,0},{2,3},{3,2},{4,5},{5,4},{6,7},{7,6},{8,16},{9,17},{10,... | collective-permute-start | bytes 73736 | tf_op jit(solution)/shard_map/ppermute | solution.py:549
  29.9 9.6 %all-to-all-start.2 = ((f32[8,48,128]{2,1,0:T(8,128)}), f32[8,48,128]{2,1,0:T(8,128)S(1)}, u32[]{:S(2)}, u32[]{:S(2)}) async-start(f32[8,48,128]{2,1,0:T(8,128)} %get-tuple-element.73), calls=%async_computation.2 | async-start | bytes 393216 | tf_op jit(solution)/shard_map/all_to_all | solution.py:547
  33.4 4.1 %collective-permute-start.4 = (f32[48,128]{1,0:T(8,128)S(1)}, f32[48,128]{1,0:T(8,128)S(1)}, u32[]{:S(2)}, u32[]{:S(2)}) collective-permute-start(f32[48,128]{1,0:T(8,128)S(1)} %get-tuple-element.74), channel_id=1, source_target_pairs={{0,8},{1,9},{2,10},{3,11},{4,12},{5,13},{6,14},{7,15},{8,0},{9,1},... | collective-permute-start | bytes 73736 | tf_op jit(solution)/shard_map/ppermute | solution.py:548
  35.0 2.5 %collective-permute-start.5 = (f32[48,128]{1,0:T(8,128)S(1)}, f32[48,128]{1,0:T(8,128)S(1)}, u32[]{:S(2)}, u32[]{:S(2)}) collective-permute-start(f32[48,128]{1,0:T(8,128)S(1)} %get-tuple-element.75), channel_id=1, source_target_pairs={{0,1},{1,0},{2,3},{3,2},{4,5},{5,4},{6,7},{7,6},{8,16},{9,17},{10,... | collective-permute-start | bytes 73736 | tf_op jit(solution)/shard_map/ppermute | solution.py:549
  42.7 5.5 %copy-start.4 = (f32[3,8,4096]{2,1,0:T(8,128)S(1)}, f32[3,8,4096]{2,1,0:T(8,128)}, u32[]{:S(2)}) copy-start(f32[3,8,4096]{2,1,0:T(8,128)} %copy-done.3) | copy-start | bytes 1179652
  42.7 9.7 %all-to-all-start.3 = ((f32[8,48,128]{2,1,0:T(8,128)}), f32[8,48,128]{2,1,0:T(8,128)S(1)}, u32[]{:S(2)}, u32[]{:S(2)}) async-start(f32[8,48,128]{2,1,0:T(8,128)} %get-tuple-element.79), calls=%async_computation.3 | async-start | bytes 393216 | tf_op jit(solution)/shard_map/all_to_all | solution.py:547
  46.3 4.5 %collective-permute-start.6 = (f32[48,128]{1,0:T(8,128)S(1)}, f32[48,128]{1,0:T(8,128)S(1)}, u32[]{:S(2)}, u32[]{:S(2)}) collective-permute-start(f32[48,128]{1,0:T(8,128)S(1)} %get-tuple-element.80), channel_id=1, source_target_pairs={{0,8},{1,9},{2,10},{3,11},{4,12},{5,13},{6,14},{7,15},{8,0},{9,1},... | collective-permute-start | bytes 73736 | tf_op jit(solution)/shard_map/ppermute | solution.py:548
  48.0 2.9 %collective-permute-start.7 = (f32[48,128]{1,0:T(8,128)S(1)}, f32[48,128]{1,0:T(8,128)S(1)}, u32[]{:S(2)}, u32[]{:S(2)}) collective-permute-start(f32[48,128]{1,0:T(8,128)S(1)} %get-tuple-element.81), channel_id=1, source_target_pairs={{0,1},{1,0},{2,3},{3,2},{4,5},{5,4},{6,7},{7,6},{8,16},{9,17},{10,... | collective-permute-start | bytes 73736 | tf_op jit(solution)/shard_map/ppermute | solution.py:549
  67.7 9.6 %all-to-all-start.5 = ((f32[8,48,128]{2,1,0:T(8,128)}), f32[8,48,128]{2,1,0:T(8,128)S(1)}, u32[]{:S(2)}, u32[]{:S(2)}) async-start(f32[8,48,128]{2,1,0:T(8,128)} %get-tuple-element.89), calls=%async_computation.5 | async-start | bytes 393216 | tf_op jit(solution)/shard_map/all_to_all | solution.py:547
  71.1 3.9 %collective-permute-start.8 = (f32[48,128]{1,0:T(8,128)S(1)}, f32[48,128]{1,0:T(8,128)S(1)}, u32[]{:S(2)}, u32[]{:S(2)}) collective-permute-start(f32[48,128]{1,0:T(8,128)S(1)} %get-tuple-element.90), channel_id=1, source_target_pairs={{0,8},{1,9},{2,10},{3,11},{4,12},{5,13},{6,14},{7,15},{8,0},{9,1},... | collective-permute-start | bytes 73736 | tf_op jit(solution)/shard_map/ppermute | solution.py:548
  71.8 3.2 %collective-permute-start.9 = (f32[48,128]{1,0:T(8,128)S(1)}, f32[48,128]{1,0:T(8,128)S(1)}, u32[]{:S(2)}, u32[]{:S(2)}) collective-permute-start(f32[48,128]{1,0:T(8,128)S(1)} %get-tuple-element.91), channel_id=1, source_target_pairs={{0,1},{1,0},{2,3},{3,2},{4,5},{5,4},{6,7},{7,6},{8,16},{9,17},{10,... | collective-permute-start | bytes 73736 | tf_op jit(solution)/shard_map/ppermute | solution.py:549
  79.8 4.3 %copy-start.2 = (f32[3,8,4096]{2,1,0:T(8,128)S(1)}, f32[3,8,4096]{2,1,0:T(8,128)}, u32[]{:S(2)}) copy-start(f32[3,8,4096]{2,1,0:T(8,128)} %copy-done.1) | copy-start | bytes 1179652
  79.8 9.7 %all-to-all-start.6 = ((f32[8,48,128]{2,1,0:T(8,128)}), f32[8,48,128]{2,1,0:T(8,128)S(1)}, u32[]{:S(2)}, u32[]{:S(2)}) async-start(f32[8,48,128]{2,1,0:T(8,128)} %get-tuple-element.97), calls=%async_computation.6 | async-start | bytes 393216 | tf_op jit(solution)/shard_map/all_to_all | solution.py:547
  83.3 3.9 %collective-permute-start.10 = (f32[48,128]{1,0:T(8,128)S(1)}, f32[48,128]{1,0:T(8,128)S(1)}, u32[]{:S(2)}, u32[]{:S(2)}) collective-permute-start(f32[48,128]{1,0:T(8,128)S(1)} %get-tuple-element.98), channel_id=1, source_target_pairs={{0,8},{1,9},{2,10},{3,11},{4,12},{5,13},{6,14},{7,15},{8,0},{9,1},... | collective-permute-start | bytes 73736 | tf_op jit(solution)/shard_map/ppermute | solution.py:548
  84.0 3.2 %collective-permute-start.11 = (f32[48,128]{1,0:T(8,128)S(1)}, f32[48,128]{1,0:T(8,128)S(1)}, u32[]{:S(2)}, u32[]{:S(2)}) collective-permute-start(f32[48,128]{1,0:T(8,128)S(1)} %get-tuple-element.99), channel_id=1, source_target_pairs={{0,1},{1,0},{2,3},{3,2},{4,5},{5,4},{6,7},{7,6},{8,16},{9,17},{10,... | collective-permute-start | bytes 73736 | tf_op jit(solution)/shard_map/ppermute | solution.py:549
  91.9 9.7 %all-to-all-start.7 = ((f32[8,48,128]{2,1,0:T(8,128)}), f32[8,48,128]{2,1,0:T(8,128)S(1)}, u32[]{:S(2)}, u32[]{:S(2)}) async-start(f32[8,48,128]{2,1,0:T(8,128)} %get-tuple-element.108), calls=%async_computation.7 | async-start | bytes 393216 | tf_op jit(solution)/shard_map/all_to_all | solution.py:547
  95.5 3.9 %collective-permute-start.12 = (f32[48,128]{1,0:T(8,128)S(1)}, f32[48,128]{1,0:T(8,128)S(1)}, u32[]{:S(2)}, u32[]{:S(2)}) collective-permute-start(f32[48,128]{1,0:T(8,128)S(1)} %get-tuple-element.109), channel_id=1, source_target_pairs={{0,8},{1,9},{2,10},{3,11},{4,12},{5,13},{6,14},{7,15},{8,0},{9,1},... | collective-permute-start | bytes 73736 | tf_op jit(solution)/shard_map/ppermute | solution.py:548
  96.2 3.2 %collective-permute-start.13 = (f32[48,128]{1,0:T(8,128)S(1)}, f32[48,128]{1,0:T(8,128)S(1)}, u32[]{:S(2)}, u32[]{:S(2)}) collective-permute-start(f32[48,128]{1,0:T(8,128)S(1)} %get-tuple-element.110), channel_id=1, source_target_pairs={{0,1},{1,0},{2,3},{3,2},{4,5},{5,4},{6,7},{7,6},{8,16},{9,17},{10,... | collective-permute-start | bytes 73736 | tf_op jit(solution)/shard_map/ppermute | solution.py:549
  (18 other events, 18.6 us)

commit v2 on v1

v2 whole, which is shorter than its diff:
```python
import functools
import math

import jax
import jax.numpy as jnp
from jax import lax
from jax.experimental import pallas as pl
from jax.experimental.pallas import tpu as pltpu
from jax.sharding import PartitionSpec as P

EDGE = 16
DEG = 3
CELLS = 4096
MASS_TERM = 1.0
LOWER_BOUND = 0.25
UPPER_BOUND = 2.0
THETA = 0.5 * (UPPER_BOUND + LOWER_BOUND)
DELTA = 0.5 * (UPPER_BOUND - LOWER_BOUND)
SIGMA = THETA / DELTA

LANES = 128
BLK = 8
TILES = CELLS // LANES
BATCHES = [range(m, m + 8) for m in range(0, TILES, 8)]
F32 = jnp.float32
R, S = 0, 3
VMEM = pl.BlockSpec(memory_space=pltpu.VMEM)
ANY = pl.BlockSpec(memory_space=pl.ANY)
HBM = pl.BlockSpec(memory_space=pltpu.HBM)
PARAMS = pltpu.CompilerParams(vmem_limit_bytes=8 * 1024 * 1024)


def lane_id():
    return lax.broadcasted_iota(jnp.int32, (BLK, LANES), 1)


def sub_id():
    return lax.broadcasted_iota(jnp.int32, (BLK, LANES), 0)


def roll(v, shift):
    shift = shift % LANES
    return v if shift == 0 else pltpu.roll(v, shift, 1)


def tile(m):
    return slice(m * LANES, (m + 1) * LANES)


def pack_faces(values, lane):
    k, g = lane & 15, lane >> 4
    faces = [[], [], [], []]
    for p in range(2):
        low = high = None
        for t in range(16):
            moved = roll(values[16 * p + t], t)
            low = moved if t == 0 else jnp.where(k == t, moved, low)
            high = moved if t == 0 else jnp.where(k == (15 + t) % 16, moved, high)
        faces[0].append(low)
        faces[1].append(roll(high, -15))
        low = high = None
        for t in range(8):
            i = 8 * p + t
            first = roll(values[2 * i], 16 * t)
            last = roll(values[2 * i + 1], 16 * t + 16)
            low = first if t == 0 else jnp.where(g == t, first, low)
            high = last if t == 0 else jnp.where(g == t, last, high)
        faces[2].append(low)
        faces[3].append(high)
    return faces


def unpack_k(low, high, lane, m):
    t = m % 16
    return jnp.where((lane & 15) == 0, roll(low[m // 16], -t), roll(high[m // 16], 15 - t))


def unpack_j(low, high, m):
    i = m // 2
    if m % 2 == 0:
        return roll(low[i // 8], -16 * (i % 8))
    return roll(high[i // 8], 112 - 16 * (i % 8))


def pick(values, index):
    return jnp.take_along_axis(values, index, axis=0, mode="promise_in_bounds")


def lane_sum(v):
    return jnp.sum(v, axis=1, keepdims=True)


def splat(column):
    return jnp.broadcast_to(column, (BLK, LANES))


class Table:
    OWNER, SLOT, BLOCK, PLANE, EVEN, LOWER, UPPER, HANG, APART = 0, 4, 8, 12, 14, 15, 16, 17, 23
    SIZE = 27

    def __init__(self, ref):
        self.ref = ref

    def __call__(self, n):
        return self.ref[n * BLK : (n + 1) * BLK, :]


def gather_ghosts(near_tile, members, who, first, second, table, ghosts, lane, rows, amend=None):
    even = table(Table.EVEN) == 1
    for d in range(6):
        for n in range(rows):
            if d < 4:
                v = None
                for m in range(members):
                    source, index = near_tile(m, d, n)
                    found = pick(source, index)
                    v = found if m == 0 else jnp.where(table(who + d) == m, found, v)
                if amend:
                    v = amend(d, n, v)
            else:
                a, b = first[n * BLK : (n + 1) * BLK, :], second[n * BLK : (n + 1) * BLK, :]
                v = jnp.where(even, b, a) if d == 4 else jnp.where(even, a, b)
                if amend:
                    v = amend(d, n, v)
                inside = table(Table.LOWER if d == 4 else Table.UPPER) == 1
                v = jnp.where(inside, pick(v, table(Table.PLANE + d - 4)), 0.0)
            at = (d * rows + n) * BLK
            ghosts[0, at : at + BLK, :] = v
    for stage in range(2):
        for d in range(6):
            bit = 16 if stage else (2 if d < 2 else 1)
            low = (lane & bit) == 0
            for n in range(rows):
                at = (d * rows + n) * BLK
                v = ghosts[stage, at : at + BLK, :]
                ghosts[stage + 1, at : at + BLK, :] = v + jnp.where(low, roll(v, -bit), roll(v, bit))
    result = []
    for d in range(6):
        hang = table(Table.HANG + d) == 1
        tiles = []
        for n in range(rows):
            at = (d * rows + n) * BLK
            tiles.append(jnp.where(hang, ghosts[2, at : at + BLK, :] * 0.25, ghosts[0, at : at + BLK, :]))
        result.append(tiles)
    return result


def sent_by(near, apart, rows):
    pair, bit = divmod(apart, 2)
    return near[bit][0, rows, :] if pair == 0 else near[1 + pair][bit, rows, :]


def step_ghosts(members, cap, near, first, second, table, ghosts, lane, amend=None):
    def near_tile(m, d, n):
        start = n * cap
        at = start // BLK * BLK
        return sent_by(near, m, slice(at, at + BLK)), table(Table.SLOT + d) + (start - at)

    return gather_ghosts(near_tile, members, Table.APART, first, second, table, ghosts, lane, 6, amend)


def look_up(rows, block, lane):
    found = []
    for c in range(3):
        total = jnp.zeros((BLK, LANES), F32)
        for t, values in enumerate(rows):
            total = total + jnp.where(lane + t * LANES == 3 * block + c, values, 0.0)
        found.append(splat(lane_sum(total)))
    return found


def rows_of(v, wide):
    return [jnp.broadcast_to(v[t : t + 1, :], (BLK, LANES)) for t in range(wide)]


def from_side(first, second, table, n, upper):
    a, b = first[n * BLK : (n + 1) * BLK, :], second[n * BLK : (n + 1) * BLK, :]
    even = table(Table.EVEN) == 1
    v = jnp.where(even, a, b) if upper else jnp.where(even, b, a)
    return jnp.where(table(Table.UPPER if upper else Table.LOWER) == 1, v, 0.0)


def emit_planes(low, high, even, at, first, second):
    for n in range(len(low)):
        span = slice((at + n) * BLK, (at + n + 1) * BLK)
        first[span, :] = jnp.where(even, high[n], low[n])
        second[span, :] = jnp.where(even, low[n], high[n])


def emit_channel(c, values, chosen, table, mine, other, first, second, lane, members, cap):
    packed = pack_faces(values, lane)
    emit_planes(values[:2], values[-2:], table(Table.EVEN) == 1, 2 * c, first, second)
    sub = sub_id()
    for m in range(members):
        want = chosen[m * BLK : (m + 1) * BLK, :]
        face, block = want >> 3, want & 7
        for u in range(2 * cap // BLK):
            out = None
            for p in range(2):
                if not u * BLK <= p * cap < (u + 1) * BLK:
                    continue
                v = None
                for f in range(4):
                    found = pick(packed[f][p], block)
                    v = found if f == 0 else jnp.where(face == f, found, v)
                out = v if out is None else jnp.where(sub < p * cap - u * BLK, out, v)
            at = c * 2 * cap + u * BLK
            (mine, other)[m % 2][m // 2, at : at + BLK, :] = out


def prepare_kernel(
    members, groups, cap, eff, owner_hbm, block_hbm, plane_hbm, hanging_hbm, coarse_rows,
    payload, first, second, tables,
    face_owner, face_block, plane_block, hanging, staged, sems, out_sem,
):
    copies = [
        pltpu.make_async_copy(source, target, sems.at[n])
        for n, (source, target) in enumerate(
            [
                (owner_hbm, face_owner), (block_hbm, face_block), (plane_hbm, plane_block), (hanging_hbm, hanging),
            ]
        )
    ]
    for copy in copies:
        copy.start()
    lane, sub = lane_id(), sub_id()
    group, member = lax.axis_index("grp"), lax.axis_index("mem")
    even = group % 2 == 0
    for copy in copies:
        copy.wait()

    def iotas(width):
        return (
            lax.broadcasted_iota(jnp.int32, (BLK, width), 1), lax.broadcasted_iota(jnp.int32, (BLK, width), 0)
        )

    lane8, sub8 = iotas(BLK)
    lane32, sub32 = iotas(4 * BLK)
    lane64, sub64 = iotas(members * cap)

    def column(row):
        wide = jnp.broadcast_to(row.astype(F32), (BLK, BLK))
        return lane_sum(jnp.where(lane8 == sub8, wide, 0.0))

    def put(n, value):
        tables[n * BLK : (n + 1) * BLK, :] = splat(value).astype(jnp.int32)

    values = [eff[:, tile(m)] for m in range(TILES)]
    packed = pack_faces(values, lane)
    emit_planes(values[:2], values[-2:], even, 0, first, second)

    row = jnp.broadcast_to(face_owner[...].astype(F32), (BLK, 4 * BLK))
    wanted = jnp.zeros((BLK, members * cap), F32)
    for d in range(4):
        place = 4 * sub32 + d
        owner = lane_sum(jnp.where(lane32 == place, row, 0.0))
        slot = lane_sum(jnp.where((lane32 < place) & (row == owner), 1.0, 0.0))
        block = column(face_block[d : d + 1, :])
        put(Table.OWNER + d, owner)
        at = (Table.APART + d) * BLK
        tables[at : at + BLK, :] = splat(owner).astype(jnp.int32) ^ jnp.full((BLK, LANES), member, jnp.int32)
        put(Table.SLOT + d, slot)
        put(Table.BLOCK + d, block)
        target = jnp.broadcast_to(owner * cap + slot, (BLK, members * cap))
        want = jnp.broadcast_to(block + (d ^ 1) * BLK, (BLK, members * cap))
        wanted = wanted + jnp.where(lane64.astype(F32) == target, want, 0.0)
    wanted = jnp.broadcast_to(jnp.sum(wanted, axis=0, keepdims=True), (BLK, members * cap))
    for d in range(2):
        put(Table.PLANE + d, column(plane_block[d : d + 1, :]))
    for n, flag in ((Table.EVEN, even), (Table.LOWER, group > 0), (Table.UPPER, group < groups - 1)):
        tables[n * BLK : (n + 1) * BLK, :] = jnp.full((BLK, LANES), jnp.where(flag, 1, 0), jnp.int32)
    for d in range(6):
        put(Table.HANG + d, hanging[:, d : d + 1])

    def coarse_tile(rows, at):
        have = coarse_rows[rows, at * LANES : min((at + 1) * LANES, coarse_rows.shape[1])]
        missing = LANES - have.shape[1]
        return have if missing == 0 else jnp.concatenate([have, jnp.zeros((BLK, missing), F32)], axis=1)

    columns = BLK * 3
    for n in range(members):
        for f in range(4):
            for p in range(2):
                at = (f * 2 + p) * BLK
                staged[n, at : at + BLK, :] = packed[f][p]
        request = lane_sum(jnp.where(lane64 == n * cap + sub64 % cap, wanted, 0.0))
        last = splat(request)
        at, off = divmod(n * columns, LANES)
        for v in range(3):
            rows = slice(v * BLK, (v + 1) * BLK)
            part = roll(coarse_tile(rows, at), v * columns - off)
            if off + columns > LANES:
                more = roll(coarse_tile(rows, at + 1), v * columns - off)
                part = jnp.where(lane < v * columns + LANES - off, part, more)
            last = jnp.where((lane >= v * columns) & (lane < (v + 1) * columns), part, last)
        staged[n, 8 * BLK : 9 * BLK, :] = last
    copy = pltpu.make_async_copy(staged, payload, out_sem)
    copy.start()
    copy.wait()


def weights_kernel(
    members, cap, near, from_first, from_second, eff, forcing, tables,
    state, mine, other, first, second, wi, gk, gj, gi, diagonal, inverse, chosen, coarse, ghosts,
):
    lane = lane_id()
    k, g = lane & 15, lane >> 4
    table = Table(tables)
    for n in range(members):
        last = near[n, 8 * BLK : 9 * BLK, :]
        coarse[n * BLK : (n + 1) * BLK, :] = last
        asked = near[lax.axis_index("mem") ^ n, 8 * BLK : 9 * BLK, :]
        chosen[n * BLK : (n + 1) * BLK, :] = splat(asked[:, LANES - 1 :]).astype(jnp.int32)

    def near_tile(m, d, n):
        at = ((d ^ 1) * 2 + n) * BLK
        return near[m, at : at + BLK, :], table(Table.BLOCK + d)

    ghost = gather_ghosts(near_tile, members, Table.OWNER, from_first, from_second, table, ghosts, lane, 2)
    values = [eff[:, tile(m)] for m in range(TILES)]
    start = [[], [], []]
    for m in range(TILES):
        i, h = divmod(m, 2)
        e = values[m]
        side_k = unpack_k(ghost[0], ghost[1], lane, m)
        side_j = unpack_j(ghost[2], ghost[3], m)
        ends_j = (g == 0) if h == 0 else (g == 7)
        n0 = jnp.where(k == 0, side_k, roll(e, 1))
        n1 = jnp.where(k == 15, side_k, roll(e, -1))
        n2 = jnp.where(g == 0, side_j if h == 0 else roll(values[m - 1], 16), roll(e, 16))
        n3 = jnp.where(g == 7, side_j if h == 1 else roll(values[m + 1], -16), roll(e, -16))
        n4 = ghost[4][h] if i == 0 else values[m - 2]
        n5 = ghost[5][h] if i == EDGE - 1 else values[m + 2]
        w = [0.5 * (e + n) for n in (n0, n1, n2, n3, n4, n5)]
        diag = MASS_TERM * e
        for d in range(6):
            diag = diag + w[d]
        inv = 1.0 / diag
        diagonal[:, tile(m)] = diag
        inverse[:, tile(m)] = inv
        wi[0, :, tile(m)] = jnp.where(k == 0, 0.0, w[0])
        wi[1, :, tile(m)] = jnp.where(k == 15, 0.0, w[1])
        wi[2, :, tile(m)] = jnp.where(ends_j, 0.0, w[2]) if h == 0 else w[2]
        wi[3, :, tile(m)] = jnp.where(ends_j, 0.0, w[3]) if h == 1 else w[3]
        wi[4, :, tile(m)] = w[4]
        gk[:, tile(m)] = jnp.where(k == 0, w[0], jnp.where(k == 15, w[1], 0.0))
        gj[:, tile(m)] = jnp.where(ends_j, w[2 + h], 0.0)
        if i == 0:
            gi[:, tile(h)] = w[4]
        if i == EDGE - 1:
            gi[:, tile(2 + h)] = w[5]
        scale = inv * (1.0 / THETA)
        for c in range(3):
            f = forcing[c, :, tile(m)]
            s = f * scale
            state[R + c, :, tile(m)] = f
            state[S + c, :, tile(m)] = s
            start[c].append(s)
    for c in range(3):
        emit_channel(c, start[c], chosen, table, mine, other, first, second, lane, members, cap)


def merge_kernel(mine, got, *pairs):
    for n, pair in enumerate(pairs):
        pair[0, :, :] = mine[n + 1, :, :]
        pair[1, :, :] = got[n + 1, :, :]


def inside_kernel(first_step, has_lift, final, *refs):
    refs = list(refs)
    state, wi, diagonal = refs[:3]
    refs = refs[3:]
    x = None if first_step else refs.pop(0)
    lift, fixed = None, {}
    if has_lift:
        lift = refs.pop(0)
        fixed = lift_inside(has_lift, refs[0], refs[1], state, *refs[2:5])
        refs = refs[5:]
    out, new_x = refs[:2]
    if final:
        staged, sems = refs[2:]
    g = lane_id() >> 4
    copies = []

    def get(row, m):
        return fixed[row, m] if (row, m) in fixed else state[row, :, tile(m)]

    for c in range(3):
        up = None if not has_lift else lift[c * BLK : (c + 1) * BLK, :]
        for m in range(TILES):
            i, h = divmod(m, 2)
            s = get(S + c, m)
            n2, n3 = roll(s, 16), roll(s, -16)
            if h == 1:
                n2 = jnp.where(g == 0, roll(get(S + c, m - 1), 16), n2)
            else:
                n3 = jnp.where(g == 7, roll(get(S + c, m + 1), -16), n3)
            acc = get(R + c, m) - diagonal[:, tile(m)] * s
            acc = acc + wi[0, :, tile(m)] * roll(s, 1)
            acc = acc + wi[1, :, tile(m)] * roll(s, -1)
            acc = acc + wi[2, :, tile(m)] * n2
            acc = acc + wi[3, :, tile(m)] * n3
            if i > 0:
                acc = acc + wi[4, :, tile(m)] * get(S + c, m - 2)
            if i < EDGE - 1:
                acc = acc + wi[4, :, tile(m + 2)] * get(S + c, m + 2)
            out[R + c, :, tile(m)] = acc
            total = s if first_step else x[c, :, tile(m)] + s
            if has_lift:
                total = total + up
            if final:
                staged[c, :, tile(m)] = total
            else:
                new_x[c, :, tile(m)] = total
        if final:
            copies.append(pltpu.make_async_copy(staged.at[c], new_x.at[c], sems.at[c]))
            copies[c].start()
    for row in range(S, S + 3):
        for m in range(TILES):
            out[row, :, tile(m)] = get(row, m)
    for copy in copies:
        copy.wait()


def add_ghosts(c, m, value, ghost, gk, gj, gi, lane):
    i, h = divmod(m, 2)
    pair = slice(2 * c, 2 * c + 2)
    value = value + gk[:, tile(m)] * unpack_k(ghost[0][pair], ghost[1][pair], lane, m)
    value = value + gj[:, tile(m)] * unpack_j(ghost[2][pair], ghost[3][pair], m)
    if i == 0:
        value = value + gi[:, tile(h)] * ghost[4][2 * c + h]
    if i == EDGE - 1:
        value = value + gi[:, tile(2 + h)] * ghost[5][2 * c + h]
    return value


def outside_kernel(members, cap, old, new, has_lift, near, from_first, from_second, state, *refs):
    inverse, gk, gj, gi, tables, chosen, x = refs[:7]
    out, mine, other, first, second, same_x, ghosts = refs[-7:]
    lane = lane_id()
    table = Table(tables)
    amend = lift_outside(members, cap, near, from_first, from_second, refs[7], tables) if has_lift else None
    ghost = step_ghosts(members, cap, near, from_first, from_second, table, ghosts, lane, amend)
    for c in range(3):
        values = []
        for batch in BATCHES:
            done = []
            for m in batch:
                r = add_ghosts(c, m, state[R + c, :, tile(m)], ghost, gk, gj, gi, lane)
                done.append((m, r, old * state[S + c, :, tile(m)] + new * (r * inverse[:, tile(m)])))
            for m, r, s in done:
                out[R + c, :, tile(m)] = r
                out[S + c, :, tile(m)] = s
                values.append(s)
        emit_channel(c, values, chosen, table, mine, other, first, second, lane, members, cap)


def last_kernel(
    members, cap, near, from_first, from_second, state, gk, gj, gi, tables, new_residual, ghosts, staged, sems,
):
    lane = lane_id()
    ghost = step_ghosts(members, cap, near, from_first, from_second, Table(tables), ghosts, lane)
    copies = []
    for c in range(3):
        for m in range(TILES):
            staged[c, :, tile(m)] = add_ghosts(c, m, state[R + c, :, tile(m)], ghost, gk, gj, gi, lane)
        copies.append(pltpu.make_async_copy(staged.at[c], new_residual.at[c], sems.at[c]))
        copies[c].start()
    for copy in copies:
        copy.wait()


def coarse_kernel(
    members, cap, near, from_first, from_second, state, gk, gj, gi, tables, coarse, x,
    out_state, payload, same_x, ghosts,
):
    lane, sub = lane_id(), sub_id()
    ghost = step_ghosts(members, cap, near, from_first, from_second, Table(tables), ghosts, lane)
    placed = jnp.zeros((BLK, LANES), F32)
    for c in range(3):
        sums = [None] * 4
        for batch in BATCHES:
            done = [(m, add_ghosts(c, m, state[R + c, :, tile(m)], ghost, gk, gj, gi, lane)) for m in batch]
            for m, r in done:
                out_state[R + c, :, tile(m)] = r
                sums[m % 4] = r if sums[m % 4] is None else sums[m % 4] + r
        total = splat(lane_sum((sums[0] + sums[1]) + (sums[2] + sums[3])))
        placed = jnp.where(lane == 3 * sub + c, total, placed)
    own = jnp.sum(placed, axis=0, keepdims=True) * (1.0 / math.sqrt(CELLS))
    own = jnp.broadcast_to(own, (BLK, LANES))
    columns = BLK * 3
    wide = -(-members * columns // LANES)
    rows = [jnp.zeros((BLK, LANES), F32) for _ in range(wide)]
    for n in range(members):
        for v in range(3):
            have = jnp.where(lane < columns, roll(coarse[n * BLK : (n + 1) * BLK, :], -v * columns), 0.0)
            part = splat(lane_sum(have * own))
            place = n * columns + v * BLK
            for t in range(place // LANES, (place + BLK - 1) // LANES + 1):
                rows[t] = jnp.where(lane + t * LANES == place + sub, part, rows[t])
    out = jnp.zeros((BLK, LANES), F32)
    for t in range(wide):
        out = jnp.where(sub == t, jnp.sum(rows[t], axis=0, keepdims=True), out)
    for n in range(members):
        payload[n, :, :] = out


def lift_kernel(
    members, cap, arrived, state, eff, inverse, gk, gj, gi, tables, chosen, x,
    out, lift, unknowns, mine, other, first, second, same_x,
):
    lane, sub = lane_id(), sub_id()
    k, g = lane & 15, lane >> 4
    table = Table(tables)
    wide = -(-members * BLK * 3 // LANES)
    member = lax.axis_index("mem")
    total = arrived[0, :, :]
    for n in range(1, members):
        total = total + arrived[n, :, :]
    unknowns[...] = total
    known = rows_of(total, wide)
    own = look_up(known, member * BLK + sub, lane)
    side = [look_up(known, table(Table.OWNER + d) * BLK + table(Table.BLOCK + d), lane) for d in range(4)]
    for c in range(3):
        values = []
        lift[c * BLK : (c + 1) * BLK, :] = own[c]
        drop_k = own[c] - jnp.where(k == 0, side[0][c], side[1][c])
        drop_j = [own[c] - side[2][c], own[c] - side[3][c]]
        for batch in BATCHES:
            done = []
            for m in batch:
                i, h = divmod(m, 2)
                applied = (MASS_TERM * eff[:, tile(m)]) * own[c]
                applied = applied + gk[:, tile(m)] * drop_k + gj[:, tile(m)] * drop_j[h]
                if i == 0:
                    applied = applied + gi[:, tile(h)] * own[c]
                if i == EDGE - 1:
                    applied = applied + gi[:, tile(2 + h)] * own[c]
                r = state[R + c, :, tile(m)] - applied
                done.append((m, r, r * (inverse[:, tile(m)] * (1.0 / THETA))))
            for m, r, s in done:
                out[R + c, :, tile(m)] = r
                out[S + c, :, tile(m)] = s
                values.append(s)
        emit_channel(c, values, chosen, table, mine, other, first, second, lane, members, cap)

    ends = end_weights(inverse, gi)
    planes = [table(Table.PLANE + d).astype(F32) for d in range(2)]
    emit_planes(ends[:2] + planes[:1], ends[2:] + planes[1:], table(Table.EVEN) == 1, 6, first, second)
    for ref in (first, second):
        ref[9 * BLK : 10 * BLK, :] = total
    edges = []
    for f in range(2):
        v = jnp.zeros((BLK, LANES), F32)
        for t, end in zip((0, 1, 14, 15), ends):
            v = jnp.where(k == t, roll(end, t - 15 * f), v)
        edges.append(v)
    edges.append(jnp.where(g == 0, ends[0], jnp.where(g == 7, roll(ends[2], 112), 0.0)))
    edges.append(jnp.where(g == 0, roll(ends[1], 16), jnp.where(g == 7, ends[3], 0.0)))
    edges = [jnp.where(lane == 18, planes[0], jnp.where(lane == 19, planes[1], v)) for v in edges]
    for m in range(members):
        want = chosen[m * BLK : (m + 1) * BLK, :]
        face, block = want >> 3, want & 7
        v = None
        for f in range(4):
            found = pick(edges[f], block)
            v = found if f == 0 else jnp.where(face == f, found, v)
        (mine, other)[m % 2][m // 2, 6 * cap : 6 * cap + BLK, :] = v


def end_weights(inverse, gi):
    return [
        gi[:, tile(n)] * (inverse[:, tile(m)] * (1.0 / THETA)) for n, m in enumerate((0, 1, TILES - 2, TILES - 1))
    ]


def lift_inside(members, from_first, from_second, state, inverse, gi, tables):
    lane = lane_id()
    table = Table(tables)
    wide = -(-members * BLK * 3 // LANES)
    member = lax.axis_index("mem")
    ends = end_weights(inverse, gi)
    fixed = {}
    for upper in range(2):
        rows = rows_of(from_side(from_first, from_second, table, 9, upper == 1), wide)
        beyond = look_up(rows, member * BLK + table(Table.PLANE + upper), lane)
        for c in range(3):
            for h in range(2):
                n, m = 2 * upper + h, upper * (TILES - 2) + h
                fixed[R + c, m] = state[R + c, :, tile(m)] + gi[:, tile(n)] * beyond[c]
                fixed[S + c, m] = state[S + c, :, tile(m)] + ends[n] * beyond[c]
    return fixed


def lift_outside(members, cap, near, from_first, from_second, unknowns, tables):
    lane = lane_id()
    k, g = lane & 15, lane >> 4
    table = Table(tables)
    wide = -(-members * BLK * 3 // LANES)
    member = lax.axis_index("mem")
    below, above = [
        rows_of(from_side(from_first, from_second, table, 9, upper), wide) for upper in (False, True)
    ]
    known = rows_of(unknowns[...], wide)
    parts = []
    for d in range(4):
        v = None
        for m in range(members):
            found = pick(sent_by(near, m, slice(6 * cap, 6 * cap + BLK)), table(Table.SLOT + d))
            v = found if m == 0 else jnp.where(table(Table.APART + d) == m, found, v)
        base = table(Table.OWNER + d) * BLK
        low = look_up(below, base + splat(v[:, 18:19]).astype(jnp.int32), lane)
        high = look_up(above, base + splat(v[:, 19:20]).astype(jnp.int32), lane)
        at_low, at_high = (k < 2, k > 13) if d < 2 else (g == 0, g == 7)
        weights = [jnp.where(at_low, v, 0.0), jnp.where(at_high, v, 0.0)]
        parts.append([weights[n % 2] * (low, high)[n % 2][n // 2] for n in range(6)])
    for upper in (False, True):
        index = from_side(from_first, from_second, table, 8, upper).astype(jnp.int32)
        own = look_up(known, member * BLK + index, lane)
        weights = [from_side(from_first, from_second, table, 6 + p, upper) for p in range(2)]
        parts.append([weights[n % 2] * own[n // 2] for n in range(6)])
    return lambda d, n, v: v + parts[d][n]


def local(
    forcing, viscosity, refinement, face_owner, face_block, plane_block, hanging, coarse_solver
):
    groups, members = lax.axis_size("grp"), lax.axis_size("mem")
    cap = 8 * BLK // members
    field = jax.ShapeDtypeStruct(forcing.shape, F32)
    scalar_field = jax.ShapeDtypeStruct(viscosity.shape, F32)
    states = jax.ShapeDtypeStruct((6, BLK, CELLS), F32)

    def array(*shape):
        return jax.ShapeDtypeStruct(shape, F32)

    def ints(*shape):
        return jax.ShapeDtypeStruct(shape, jnp.int32)

    def scratch(*shape):
        return pltpu.VMEM(shape, F32)

    def call(body, in_specs, out_shape, out_specs, scratch_shapes, name, aliases=None, moved=2_000_000):
        return pl.pallas_call(
            body,
            out_shape=out_shape,
            in_specs=in_specs,
            out_specs=out_specs,
            scratch_shapes=scratch_shapes,
            compiler_params=PARAMS,
            input_output_aliases=aliases or {},
            cost_estimate=pl.CostEstimate(flops=2_000_000, bytes_accessed=moved, transcendentals=0),
            name=name,
        )

    first_route = [(q * members + m, (q ^ 1) * members + m) for q in range(groups) for m in range(members)]
    second_route = []
    for q in range(groups):
        for m in range(members):
            if q == 0 or q == groups - 1:
                second_route.append((q * members + m, q * members + (m ^ 1)))
            else:
                second_route.append((q * members + m, (q + 1 if q % 2 else q - 1) * members + m))

    def exchange(payload, first, second):
        near = lax.all_to_all(payload, "mem", split_axis=0, concat_axis=0, tiled=True)
        first = lax.ppermute(first, ("grp", "mem"), first_route)
        second = lax.ppermute(second, ("grp", "mem"), second_route)
        return near, first, second

    def swap(a, bits):
        return lax.ppermute(a, "mem", [(m, m ^ bits) for m in range(members)])

    def spread(mine, other, first, second):
        first = lax.ppermute(first, ("grp", "mem"), first_route)
        second = lax.ppermute(second, ("grp", "mem"), second_route)
        got = swap(other, 1)
        pairs = members // 2 - 1
        sent = call(
            merge_kernel, [VMEM] * 2, [array(2, *mine.shape[1:])] * pairs, [VMEM] * pairs, [], "merge", moved=200_000
        )(mine, got)
        return [mine, got] + [swap(a, 2 * n + 2) for n, a in enumerate(sent)], first, second

    per = 9 * BLK
    eff = viscosity * jnp.exp2(-refinement.astype(F32))[:, None]
    payload, first, second, tables = call(
        functools.partial(prepare_kernel, members, groups, cap),
        [VMEM] + [HBM] * 4 + [VMEM],
        [array(members, per, LANES), array(16, LANES), array(16, LANES), ints(Table.SIZE * BLK, LANES)],
        [HBM, VMEM, VMEM, VMEM],
        [
            pltpu.VMEM((1, 4 * BLK), jnp.int32), pltpu.VMEM((4, BLK), jnp.int32), pltpu.VMEM((2, BLK), jnp.int32),
            pltpu.VMEM((BLK, 6), jnp.int32), scratch(members, per, LANES),
            pltpu.SemaphoreType.DMA((4,)), pltpu.SemaphoreType.DMA,
        ],
        "prepare",
        moved=0,
    )(eff, face_owner.T, face_block.T, plane_block.T, hanging, coarse_solver[0])
    arrived, from_first, from_second = exchange(payload, first, second)

    half = array(members // 2, 6 * cap, LANES)
    sent_out = [half, half, array(48, LANES), array(48, LANES)]
    near_refs = members // 2 + 1
    ghost_scratch = [scratch(3, 6 * 48, LANES)]

    def gathered(body, *fixed):
        return lambda *refs: body(*fixed, refs[:near_refs], *refs[near_refs:])

    state, mine, other, first, second, wi, gk, gj, gi, diagonal, inverse, chosen, coarse = call(
        functools.partial(weights_kernel, members, cap),
        [VMEM] * 6,
        [states] + sent_out
        + [array(5, BLK, CELLS), scalar_field, scalar_field, array(BLK, 4 * LANES), scalar_field, scalar_field]
        + [ints(members * BLK, LANES), array(members * BLK, LANES)],
        [VMEM] * 13,
        [scratch(3, 6 * 16, LANES)],
        "weights",
    )(arrived, from_first, from_second, eff, forcing, tables)

    field_scratch = [scratch(3, BLK, CELLS), pltpu.SemaphoreType.DMA((3,))]

    def inside(state, x=None, lift=(), final=False):
        operands = [state, wi, diagonal] + ([] if x is None else [x]) + list(lift)
        return call(
            functools.partial(inside_kernel, x is None, members if lift else 0, final),
            [VMEM] * len(operands),
            [states, field],
            [VMEM, HBM if final else VMEM],
            field_scratch * final,
            "inside",
            {0: 0} if x is None or final else {0: 0, 3: 1},
        )(*operands)

    def outside(near, from_first, from_second, state, x, old, new, unknowns=None):
        more = [] if unknowns is None else [unknowns]
        return call(
            gathered(outside_kernel, members, cap, old, new, unknowns is not None),
            [VMEM] * (near_refs + 9) + [ANY] + [VMEM] * len(more),
            [states] + sent_out + [field],
            [VMEM] * 5 + [ANY],
            ghost_scratch,
            "outside",
            {near_refs + 2: 0, near_refs + 9: 5},
        )(*near, from_first, from_second, state, inverse, gk, gj, gi, tables, chosen, x, *more)

    rho = 1.0 / SIGMA
    factors = []
    for _ in range(DEG - 1):
        rho_next = 1.0 / (2.0 * SIGMA - rho)
        factors.append((rho_next * rho, 2.0 * rho_next / DELTA))
        rho = rho_next

    def steps(state, sent, x, lift=None, unknowns=None):
        for n, (old, new) in enumerate(factors):
            near, from_first, from_second = spread(*sent)
            more = (lift, from_first, from_second, inverse, gi, tables) if n == 0 and lift is not None else ()
            state, x = inside(state, x, more)
            state, *sent, x = outside(
                near, from_first, from_second, state, x, old, new, unknowns if n == 0 else None
            )
        return state, x, spread(*sent)

    state, x, (near, from_first, from_second) = steps(state, (mine, other, first, second), None)
    state, x = inside(state, x)
    state, payload, x = call(
        gathered(coarse_kernel, members, cap),
        [VMEM] * (near_refs + 8) + [ANY],
        [states, array(members, BLK, LANES), field],
        [VMEM, VMEM, ANY],
        ghost_scratch,
        "coarse",
        {near_refs + 2: 0, near_refs + 8: 2},
    )(*near, from_first, from_second, state, gk, gj, gi, tables, coarse, x)
    sums = lax.all_to_all(payload, "mem", split_axis=0, concat_axis=0, tiled=True)
    half = array(members // 2, 6 * cap + BLK, LANES)
    state, lift, unknowns, *sent, x = call(
        functools.partial(lift_kernel, members, cap),
        [VMEM] * 9 + [ANY],
        [states, array(3 * BLK, LANES), array(BLK, LANES), half, half, array(80, LANES), array(80, LANES), field],
        [VMEM] * 7 + [ANY],
        [],
        "lift",
        {1: 0, 9: 7},
    )(sums, state, eff, inverse, gk, gj, gi, tables, chosen, x)
    state, x, (near, from_first, from_second) = steps(state, sent, x, lift, unknowns)
    state, velocity = inside(state, x, final=True)
    residual = call(
        gathered(last_kernel, members, cap),
        [VMEM] * (near_refs + 7),
        [field],
        [HBM],
        ghost_scratch + field_scratch,
        "last",
    )(*near, from_first, from_second, state, gk, gj, gi, tables)[0]
    return velocity, residual


def solution(mesh):
    in_specs = (
        P(None, ("grp", "mem"), None),
        P(("grp", "mem"), None),
        P(("grp", "mem")),
        P(("grp", "mem"), None),
        P(("grp", "mem"), None),
        P(("grp", "mem"), None),
        P(("grp", "mem"), None),
        P("grp", "mem", None),
    )
    out_specs = (P(None, ("grp", "mem"), None), P(None, ("grp", "mem"), None))
    return jax.shard_map(local, mesh=mesh, in_specs=in_specs, out_specs=out_specs, check_vma=False)
```

time: 104 us -> 88 us (0.85)
  local copies, waits for them, and re-layouts: 10.9 us -> 0.03 us
  starting transfers between devices: 35.4 us -> 41.1 us
  blocking collectives: 12.5 us -> 7.22 us
  waiting for transfers between devices: 24.8 us -> 20.6 us
  Pallas kernels: 18.2 us -> 16 us
  other arithmetic: 0 us -> 1.69 us
    ppermute x0 -> x36, starting transfers between devices: none -> 34.1 us  [the longest x24 21.7 us: swap(): return lax.ppermute(a, 'mem', [(m, m ^ bits) for m in range(members)])]
    all_to_all x7 -> x1, starting transfers between devices: 25.9 us -> 5.18 us  [exchange(): lax.all_to_all(payload, 'mem', split_axis=0, concat_axis=0, tiled=True)]
    ppermute x0 -> x36, waiting for transfers between devices: none -> 15.1 us  [the longest x24 7.8 us: swap(): return lax.ppermute(a, 'mem', [(m, m ^ bits) for m in range(members)])]
    all_to_all x7 -> x1, waiting for transfers between devices: 16.4 us -> 3.63 us  [exchange(): lax.all_to_all(payload, 'mem', split_axis=0, concat_axis=0, tiled=True)]
    unnamed x42 -> x12, local copies, waits for them, and re-layouts: 10.1 us -> 0.03 us
    ppermute x7 -> x1, starting transfers between devices: 8.71 us -> 1.58 us  [exchange(): first = lax.ppermute(first, ('grp', 'mem'), first_route)]
    ppermute x7 -> x1, waiting for transfers between devices: 8.43 us -> 1.85 us  [exchange(): first = lax.ppermute(first, ('grp', 'mem'), first_route)]
    all_to_all x1, blocking collectives: 12.5 us -> 7.22 us  [local(): lax.all_to_all(payload, 'mem', split_axis=0, concat_axis=0, tiled=True)]
  transfers between devices with their start and end apart: 21 -> 39, of which waited for: 12 -> 14; matrix products, arithmetic and copies ran while one was open for 0% -> 0% of each run, Pallas kernels for 4% -> 5%
where the time goes in v2:
time: 88 us; the launch traced here: 87.7 us
  starting transfers between devices  41.1 us (47%)
  waiting for transfers between devices  20.6 us (23%)
  Pallas kernels  16 us (18%)
  blocking collectives  7.22 us (8%)
  other arithmetic  1.69 us (2%)
  between operations  1.14 us (1%)
    ppermute x24, starting transfers between devices, swap(): return lax.ppermute(a, 'mem', [(m, m ^ bits) for m in range(members)])  21.7 us
    ppermute x6, starting transfers between devices, spread(): first = lax.ppermute(first, ('grp', 'mem'), first_route)  12.4 us
    ppermute x24, waiting for transfers between devices, swap(): return lax.ppermute(a, 'mem', [(m, m ^ bits) for m in range(members)])  7.8 us
    ppermute x6, waiting for transfers between devices, spread(): first = lax.ppermute(first, ('grp', 'mem'), first_route)  7.29 us
    all_to_all x1, blocking collectives, local(): lax.all_to_all(payload, 'mem', split_axis=0, concat_axis=0, tiled=True)  7.22 us
    pallas_call x4, Pallas kernels, outside(): call(gathered(outside_kernel, members, cap, old, new, unknowns is not Non...  5.53 us
    all_to_all x1, starting transfers between devices, exchange(): lax.all_to_all(payload, 'mem', split_axis=0, concat_axis=0, tiled=True)  5.18 us
    pallas_call x6, Pallas kernels, inside(): call(functools.partial(inside_kernel, x is None, members if lift else 0,...  4.79 us
  transfers between devices with their start and end apart: 39, of which 14 were waited for; matrix products, arithmetic and copies ran while one was open for 0% of the time, Pallas kernels for 5%

profile of v2, /device:TPU:0, one launch (start us, length us, event | category | flops | bytes accessed | tf_op | source)
XLA Modules:
  0.0 87.7 jit_solution(3579803657751081095)
XLA Ops:
  3.7 5.2 %all-to-all-start = ((f32[8,72,128]{2,1,0:T(8,128)}), f32[8,72,128]{2,1,0:T(8,128)S(1)}, u32[]{:S(2)}, u32[]{:S(2)}) async-start(f32[8,72,128]{2,1,0:T(8,128)} %get-tuple-element.84), calls=%async_computation | async-start | bytes 589824 | tf_op jit(solution)/shard_map/all_to_all | solution.py:666
  8.8 1.6 %collective-permute-start = (f32[16,128]{1,0:T(8,128)S(1)}, f32[16,128]{1,0:T(8,128)S(1)}, u32[]{:S(2)}, u32[]{:S(2)}) collective-permute-start(f32[16,128]{1,0:T(8,128)S(1)} %get-tuple-element.85), channel_id=1, source_target_pairs={{0,8},{1,9},{2,10},{3,11},{4,12},{5,13},{6,14},{7,15},{8,0},{9,1},... | collective-permute-start | bytes 24584 | tf_op jit(solution)/shard_map/ppermute | solution.py:667
  10.6 1.8 %collective-permute-done.from_first = f32[16,128]{1,0:T(8,128)S(1)} collective-permute-done((f32[16,128]{1,0:T(8,128)S(1)}, f32[16,128]{1,0:T(8,128)S(1)}, u32[]{:S(2)}, u32[]{:S(2)}) %collective-permute-start) | collective-permute-done | bytes 8224 | tf_op jit(solution)/shard_map/ppermute | solution.py:667
  12.5 3.6 %all-to-all-done.near = f32[8,72,128]{2,1,0:T(8,128)S(1)} async-done(((f32[8,72,128]{2,1,0:T(8,128)}), f32[8,72,128]{2,1,0:T(8,128)S(1)}, u32[]{:S(2)}, u32[]{:S(2)}) %all-to-all-start) | async-done | bytes 294944 | tf_op jit(solution)/shard_map/all_to_all | solution.py:666
  19.6 2.4 %collective-permute-start.5 = (f32[2,48,128]{2,1,0:T(8,128)S(1)}, f32[2,48,128]{2,1,0:T(8,128)S(1)}, u32[]{:S(2)}, u32[]{:S(2)}) collective-permute-start(f32[2,48,128]{2,1,0:T(8,128)S(1)} %get-tuple-element.92), channel_id=1, source_target_pairs={{0,6},{1,7},{2,4},{3,5},{4,2},{5,3},{6,0},{7,1},{8,14},{9,15},{10,... | collective-permute-start | bytes 147464 | tf_op jit(solution)/shard_map/ppermute | solution.py:672
  22.0 1.6 %collective-permute-start.6 = (f32[48,128]{1,0:T(8,128)S(1)}, f32[48,128]{1,0:T(8,128)S(1)}, u32[]{:S(2)}, u32[]{:S(2)}) collective-permute-start(f32[48,128]{1,0:T(8,128)S(1)} %get-tuple-element.93), channel_id=1, source_target_pairs={{0,8},{1,9},{2,10},{3,11},{4,12},{5,13},{6,14},{7,15},{8,0},{9,1},... | collective-permute-start | bytes 73736 | tf_op jit(solution)/shard_map/ppermute | solution.py:675
  24.2 1.5 %collective-permute-done.6.refs_5_ = f32[48,128]{1,0:T(8,128)S(1)} collective-permute-done((f32[48,128]{1,0:T(8,128)S(1)}, f32[48,128]{1,0:T(8,128)S(1)}, u32[]{:S(2)}, u32[]{:S(2)}) %collective-permute-start.6) | collective-permute-done | bytes 24608 | tf_op jit(solution)/shard_map/ppermute | solution.py:675
  25.8 1.3 %outside.4 = (f32[6,8,4096]{2,1,0:T(8,128)S(1)}, f32[4,48,128]{2,1,0:T(8,128)S(1)}, f32[4,48,128]{2,1,0:T(8,128)S(1)}, f32[48,128]{1,0:T(8,128)S(1)}, f32[48,128]{1,0:T(8,128)S(1)}, /*index=5*/f32[3,8,4096]{2,1,0:T(8,128)S(1)}) custom-call(f32[4,48,128]{2,1,0:T(8,128)S(1)} %get-tuple-element.88.mine.refs_0_, ...), custom_call_target="tpu_custom_call", output_to_operand_aliasing={{0}: (7, {}), {5}: (14, {})} | custom-call | flops 2000000 | bytes 2000000 | tf_op jit(solution)/shard_map/outside/pallas_call | solution.py:736
  30.3 1.8 %collective-permute-start.11 = (f32[2,48,128]{2,1,0:T(8,128)S(1)}, f32[2,48,128]{2,1,0:T(8,128)S(1)}, u32[]{:S(2)}, u32[]{:S(2)}) collective-permute-start(f32[2,48,128]{2,1,0:T(8,128)S(1)} %get-tuple-element.109), channel_id=1, source_target_pairs={{0,6},{1,7},{2,4},{3,5},{4,2},{5,3},{6,0},{7,1},{8,14},{9,15},{10,... | collective-permute-start | bytes 147464 | tf_op jit(solution)/shard_map/ppermute | solution.py:672
  32.1 2.7 %collective-permute-start.12 = (f32[48,128]{1,0:T(8,128)S(1)}, f32[48,128]{1,0:T(8,128)S(1)}, u32[]{:S(2)}, u32[]{:S(2)}) collective-permute-start(f32[48,128]{1,0:T(8,128)S(1)} %get-tuple-element.110), channel_id=1, source_target_pairs={{0,8},{1,9},{2,10},{3,11},{4,12},{5,13},{6,14},{7,15},{8,0},{9,1},... | collective-permute-start | bytes 73736 | tf_op jit(solution)/shard_map/ppermute | solution.py:675
  40.5 2.4 %collective-permute-start.17 = (f32[2,48,128]{2,1,0:T(8,128)S(1)}, f32[2,48,128]{2,1,0:T(8,128)S(1)}, u32[]{:S(2)}, u32[]{:S(2)}) collective-permute-start(f32[2,48,128]{2,1,0:T(8,128)S(1)} %get-tuple-element.120), channel_id=1, source_target_pairs={{0,6},{1,7},{2,4},{3,5},{4,2},{5,3},{6,0},{7,1},{8,14},{9,15},{10,... | collective-permute-start | bytes 147464 | tf_op jit(solution)/shard_map/ppermute | solution.py:672
  42.9 2.0 %collective-permute-start.18 = (f32[48,128]{1,0:T(8,128)S(1)}, f32[48,128]{1,0:T(8,128)S(1)}, u32[]{:S(2)}, u32[]{:S(2)}) collective-permute-start(f32[48,128]{1,0:T(8,128)S(1)} %get-tuple-element.121), channel_id=1, source_target_pairs={{0,8},{1,9},{2,10},{3,11},{4,12},{5,13},{6,14},{7,15},{8,0},{9,1},... | collective-permute-start | bytes 73736 | tf_op jit(solution)/shard_map/ppermute | solution.py:675
  46.7 1.6 %coarse.1 = (f32[6,8,4096]{2,1,0:T(8,128)S(1)}, f32[8,8,128]{2,1,0:T(8,128)S(1)}, f32[3,8,4096]{2,1,0:T(8,128)S(1)}) custom-call(f32[4,48,128]{2,1,0:T(8,128)S(1)} %get-tuple-element.116.mine.refs_0_, f32[4,48,128]{2,1,0:T(8,128)S(1)} %collective-permute-done.14.got.refs_1_, ...), custom_call_target="tpu_custom_call", output_to_operand_aliasing={{0}: (7, {}), {2}: (13, {})} | custom-call | flops 2000000 | bytes 2000000 | tf_op jit(solution)/shard_map/coarse/pallas_call | solution.py:765
  48.3 7.2 %all_to_all.10.arrived = f32[8,8,128]{2,1,0:T(8,128)S(1)} all-to-all(f32[8,8,128]{2,1,0:T(8,128)S(1)} %get-tuple-element.128), channel_id=1, replica_groups=mesh['grp'=4,'mem'=8] {'mem'}, dimensions={0} | all-to-all | bytes 65536 | tf_op jit(solution)/shard_map/all_to_all | solution.py:774
  58.8 2.4 %collective-permute-start.23 = (f32[2,56,128]{2,1,0:T(8,128)S(1)}, f32[2,56,128]{2,1,0:T(8,128)S(1)}, u32[]{:S(2)}, u32[]{:S(2)}) collective-permute-start(f32[2,56,128]{2,1,0:T(8,128)S(1)} %get-tuple-element.135), channel_id=1, source_target_pairs={{0,6},{1,7},{2,4},{3,5},{4,2},{5,3},{6,0},{7,1},{8,14},{9,15},{10,... | collective-permute-start | bytes 172040 | tf_op jit(solution)/shard_map/ppermute | solution.py:672
  61.1 2.0 %collective-permute-start.24 = (f32[80,128]{1,0:T(8,128)S(1)}, f32[80,128]{1,0:T(8,128)S(1)}, u32[]{:S(2)}, u32[]{:S(2)}) collective-permute-start(f32[80,128]{1,0:T(8,128)S(1)} %get-tuple-element.136), channel_id=1, source_target_pairs={{0,8},{1,9},{2,10},{3,11},{4,12},{5,13},{6,14},{7,15},{8,0},{9,1},... | collective-permute-start | bytes 122888 | tf_op jit(solution)/shard_map/ppermute | solution.py:675
  63.1 2.0 %collective-permute-done.24.refs_5_ = f32[80,128]{1,0:T(8,128)S(1)} collective-permute-done((f32[80,128]{1,0:T(8,128)S(1)}, f32[80,128]{1,0:T(8,128)S(1)}, u32[]{:S(2)}, u32[]{:S(2)}) %collective-permute-start.24) | collective-permute-done | bytes 40992 | tf_op jit(solution)/shard_map/ppermute | solution.py:675
  65.9 1.6 %outside.6 = (f32[6,8,4096]{2,1,0:T(8,128)S(1)}, f32[4,48,128]{2,1,0:T(8,128)S(1)}, f32[4,48,128]{2,1,0:T(8,128)S(1)}, f32[48,128]{1,0:T(8,128)S(1)}, f32[48,128]{1,0:T(8,128)S(1)}, /*index=5*/f32[3,8,4096]{2,1,0:T(8,128)S(1)}) custom-call(f32[4,56,128]{2,1,0:T(8,128)S(1)} %get-tuple-element.131.mine.refs_0_, ...), custom_call_target="tpu_custom_call", output_to_operand_aliasing={{0}: (7, {}), {5}: (14, {})} | custom-call | flops 2000000 | bytes 2000000 | tf_op jit(solution)/shard_map/outside/pallas_call | solution.py:736
  70.0 2.4 %collective-permute-start.29 = (f32[2,48,128]{2,1,0:T(8,128)S(1)}, f32[2,48,128]{2,1,0:T(8,128)S(1)}, u32[]{:S(2)}, u32[]{:S(2)}) collective-permute-start(f32[2,48,128]{2,1,0:T(8,128)S(1)} %get-tuple-element.148), channel_id=1, source_target_pairs={{0,6},{1,7},{2,4},{3,5},{4,2},{5,3},{6,0},{7,1},{8,14},{9,15},{10,... | collective-permute-start | bytes 147464 | tf_op jit(solution)/shard_map/ppermute | solution.py:672
  72.4 2.0 %collective-permute-start.30 = (f32[48,128]{1,0:T(8,128)S(1)}, f32[48,128]{1,0:T(8,128)S(1)}, u32[]{:S(2)}, u32[]{:S(2)}) collective-permute-start(f32[48,128]{1,0:T(8,128)S(1)} %get-tuple-element.149), channel_id=1, source_target_pairs={{0,8},{1,9},{2,10},{3,11},{4,12},{5,13},{6,14},{7,15},{8,0},{9,1},... | collective-permute-start | bytes 73736 | tf_op jit(solution)/shard_map/ppermute | solution.py:675
  76.2 1.3 %outside.7 = (f32[6,8,4096]{2,1,0:T(8,128)S(1)}, f32[4,48,128]{2,1,0:T(8,128)S(1)}, f32[4,48,128]{2,1,0:T(8,128)S(1)}, f32[48,128]{1,0:T(8,128)S(1)}, f32[48,128]{1,0:T(8,128)S(1)}, /*index=5*/f32[3,8,4096]{2,1,0:T(8,128)S(1)}) custom-call(f32[4,48,128]{2,1,0:T(8,128)S(1)} %get-tuple-element.144.mine.refs_0_, ...), custom_call_target="tpu_custom_call", output_to_operand_aliasing={{0}: (7, {}), {5}: (14, {})} | custom-call | flops 2000000 | bytes 2000000 | tf_op jit(solution)/shard_map/outside/pallas_call | solution.py:736
  80.7 1.8 %collective-permute-start.35 = (f32[2,48,128]{2,1,0:T(8,128)S(1)}, f32[2,48,128]{2,1,0:T(8,128)S(1)}, u32[]{:S(2)}, u32[]{:S(2)}) collective-permute-start(f32[2,48,128]{2,1,0:T(8,128)S(1)} %get-tuple-element.162), channel_id=1, source_target_pairs={{0,6},{1,7},{2,4},{3,5},{4,2},{5,3},{6,0},{7,1},{8,14},{9,15},{10,... | collective-permute-start | bytes 147464 | tf_op jit(solution)/shard_map/ppermute | solution.py:672
  82.5 2.0 %collective-permute-start.36 = (f32[48,128]{1,0:T(8,128)S(1)}, f32[48,128]{1,0:T(8,128)S(1)}, u32[]{:S(2)}, u32[]{:S(2)}) collective-permute-start(f32[48,128]{1,0:T(8,128)S(1)} %get-tuple-element.163), channel_id=1, source_target_pairs={{0,8},{1,9},{2,10},{3,11},{4,12},{5,13},{6,14},{7,15},{8,0},{9,1},... | collective-permute-start | bytes 73736 | tf_op jit(solution)/shard_map/ppermute | solution.py:675
  84.5 1.4 %inside.11 = (f32[6,8,4096]{2,1,0:T(8,128)S(1)}, f32[3,8,4096]{2,1,0:T(8,128)}) custom-call(f32[6,8,4096]{2,1,0:T(8,128)S(1)} %get-tuple-element.155.refs_0_, f32[5,8,4096]{2,1,0:T(8,128)S(1)} %get-tuple-element.96.refs_1_, f32[8,4096]{1,0:T(8,128)S(1)} %get-tuple-element.97.refs_2_, ...), custom_call_target="tpu_custom_call", output_to_operand_aliasing={{0}: (0, {})} | custom-call | flops 2000000 | bytes 2000000 | tf_op jit(solution)/shard_map/inside/pallas_call | solution.py:724
  (90 shorter events, 31.0 us)
Async XLA Ops:
  3.7 12.5 %all-to-all-start = ((f32[8,72,128]{2,1,0:T(8,128)}), f32[8,72,128]{2,1,0:T(8,128)S(1)}, u32[]{:S(2)}, u32[]{:S(2)}) async-start(f32[8,72,128]{2,1,0:T(8,128)} %get-tuple-element.84), calls=%async_computation | async-start | bytes 589824 | tf_op jit(solution)/shard_map/all_to_all | solution.py:666
  18.4 7.4 %collective-permute-start.3 = (f32[2,48,128]{2,1,0:T(8,128)S(1)}, f32[2,48,128]{2,1,0:T(8,128)S(1)}, u32[]{:S(2)}, u32[]{:S(2)}) collective-permute-start(f32[2,48,128]{2,1,0:T(8,128)S(1)} %get-tuple-element.90), channel_id=1, source_target_pairs={{0,2},{1,3},{2,0},{3,1},{4,6},{5,7},{6,4},{7,5},{8,10},{9,11},{10,... | collective-permute-start | bytes 147464 | tf_op jit(solution)/shard_map/ppermute | solution.py:672
  19.0 6.8 %collective-permute-start.4 = (f32[2,48,128]{2,1,0:T(8,128)S(1)}, f32[2,48,128]{2,1,0:T(8,128)S(1)}, u32[]{:S(2)}, u32[]{:S(2)}) collective-permute-start(f32[2,48,128]{2,1,0:T(8,128)S(1)} %get-tuple-element.91), channel_id=1, source_target_pairs={{0,4},{1,5},{2,6},{3,7},{4,0},{5,1},{6,2},{7,3},{8,12},{9,13},{10,... | collective-permute-start | bytes 147464 | tf_op jit(solution)/shard_map/ppermute | solution.py:672
  19.6 6.2 %collective-permute-start.5 = (f32[2,48,128]{2,1,0:T(8,128)S(1)}, f32[2,48,128]{2,1,0:T(8,128)S(1)}, u32[]{:S(2)}, u32[]{:S(2)}) collective-permute-start(f32[2,48,128]{2,1,0:T(8,128)S(1)} %get-tuple-element.92), channel_id=1, source_target_pairs={{0,6},{1,7},{2,4},{3,5},{4,2},{5,3},{6,0},{7,1},{8,14},{9,15},{10,... | collective-permute-start | bytes 147464 | tf_op jit(solution)/shard_map/ppermute | solution.py:672
  28.5 8.1 %collective-permute-start.9 = (f32[2,48,128]{2,1,0:T(8,128)S(1)}, f32[2,48,128]{2,1,0:T(8,128)S(1)}, u32[]{:S(2)}, u32[]{:S(2)}) collective-permute-start(f32[2,48,128]{2,1,0:T(8,128)S(1)} %get-tuple-element.107), channel_id=1, source_target_pairs={{0,2},{1,3},{2,0},{3,1},{4,6},{5,7},{6,4},{7,5},{8,10},{9,11},{10,... | collective-permute-start | bytes 147464 | tf_op jit(solution)/shard_map/ppermute | solution.py:672
  29.2 7.4 %collective-permute-start.10 = (f32[2,48,128]{2,1,0:T(8,128)S(1)}, f32[2,48,128]{2,1,0:T(8,128)S(1)}, u32[]{:S(2)}, u32[]{:S(2)}) collective-permute-start(f32[2,48,128]{2,1,0:T(8,128)S(1)} %get-tuple-element.108), channel_id=1, source_target_pairs={{0,4},{1,5},{2,6},{3,7},{4,0},{5,1},{6,2},{7,3},{8,12},{9,13},{10,... | collective-permute-start | bytes 147464 | tf_op jit(solution)/shard_map/ppermute | solution.py:672
  30.3 6.3 %collective-permute-start.11 = (f32[2,48,128]{2,1,0:T(8,128)S(1)}, f32[2,48,128]{2,1,0:T(8,128)S(1)}, u32[]{:S(2)}, u32[]{:S(2)}) collective-permute-start(f32[2,48,128]{2,1,0:T(8,128)S(1)} %get-tuple-element.109), channel_id=1, source_target_pairs={{0,6},{1,7},{2,4},{3,5},{4,2},{5,3},{6,0},{7,1},{8,14},{9,15},{10,... | collective-permute-start | bytes 147464 | tf_op jit(solution)/shard_map/ppermute | solution.py:672
  32.1 4.5 %collective-permute-start.12 = (f32[48,128]{1,0:T(8,128)S(1)}, f32[48,128]{1,0:T(8,128)S(1)}, u32[]{:S(2)}, u32[]{:S(2)}) collective-permute-start(f32[48,128]{1,0:T(8,128)S(1)} %get-tuple-element.110), channel_id=1, source_target_pairs={{0,8},{1,9},{2,10},{3,11},{4,12},{5,13},{6,14},{7,15},{8,0},{9,1},... | collective-permute-start | bytes 73736 | tf_op jit(solution)/shard_map/ppermute | solution.py:675
  39.3 7.4 %collective-permute-start.15 = (f32[2,48,128]{2,1,0:T(8,128)S(1)}, f32[2,48,128]{2,1,0:T(8,128)S(1)}, u32[]{:S(2)}, u32[]{:S(2)}) collective-permute-start(f32[2,48,128]{2,1,0:T(8,128)S(1)} %get-tuple-element.118), channel_id=1, source_target_pairs={{0,2},{1,3},{2,0},{3,1},{4,6},{5,7},{6,4},{7,5},{8,10},{9,11},{10,... | collective-permute-start | bytes 147464 | tf_op jit(solution)/shard_map/ppermute | solution.py:672
  39.9 6.8 %collective-permute-start.16 = (f32[2,48,128]{2,1,0:T(8,128)S(1)}, f32[2,48,128]{2,1,0:T(8,128)S(1)}, u32[]{:S(2)}, u32[]{:S(2)}) collective-permute-start(f32[2,48,128]{2,1,0:T(8,128)S(1)} %get-tuple-element.119), channel_id=1, source_target_pairs={{0,4},{1,5},{2,6},{3,7},{4,0},{5,1},{6,2},{7,3},{8,12},{9,13},{10,... | collective-permute-start | bytes 147464 | tf_op jit(solution)/shard_map/ppermute | solution.py:672
  40.5 6.2 %collective-permute-start.17 = (f32[2,48,128]{2,1,0:T(8,128)S(1)}, f32[2,48,128]{2,1,0:T(8,128)S(1)}, u32[]{:S(2)}, u32[]{:S(2)}) collective-permute-start(f32[2,48,128]{2,1,0:T(8,128)S(1)} %get-tuple-element.120), channel_id=1, source_target_pairs={{0,6},{1,7},{2,4},{3,5},{4,2},{5,3},{6,0},{7,1},{8,14},{9,15},{10,... | collective-permute-start | bytes 147464 | tf_op jit(solution)/shard_map/ppermute | solution.py:672
  42.9 3.8 %collective-permute-start.18 = (f32[48,128]{1,0:T(8,128)S(1)}, f32[48,128]{1,0:T(8,128)S(1)}, u32[]{:S(2)}, u32[]{:S(2)}) collective-permute-start(f32[48,128]{1,0:T(8,128)S(1)} %get-tuple-element.121), channel_id=1, source_target_pairs={{0,8},{1,9},{2,10},{3,11},{4,12},{5,13},{6,14},{7,15},{8,0},{9,1},... | collective-permute-start | bytes 73736 | tf_op jit(solution)/shard_map/ppermute | solution.py:675
  57.6 8.3 %collective-permute-start.21 = (f32[2,56,128]{2,1,0:T(8,128)S(1)}, f32[2,56,128]{2,1,0:T(8,128)S(1)}, u32[]{:S(2)}, u32[]{:S(2)}) collective-permute-start(f32[2,56,128]{2,1,0:T(8,128)S(1)} %get-tuple-element.133), channel_id=1, source_target_pairs={{0,2},{1,3},{2,0},{3,1},{4,6},{5,7},{6,4},{7,5},{8,10},{9,11},{10,... | collective-permute-start | bytes 172040 | tf_op jit(solution)/shard_map/ppermute | solution.py:672
  58.2 7.6 %collective-permute-start.22 = (f32[2,56,128]{2,1,0:T(8,128)S(1)}, f32[2,56,128]{2,1,0:T(8,128)S(1)}, u32[]{:S(2)}, u32[]{:S(2)}) collective-permute-start(f32[2,56,128]{2,1,0:T(8,128)S(1)} %get-tuple-element.134), channel_id=1, source_target_pairs={{0,4},{1,5},{2,6},{3,7},{4,0},{5,1},{6,2},{7,3},{8,12},{9,13},{10,... | collective-permute-start | bytes 172040 | tf_op jit(solution)/shard_map/ppermute | solution.py:672
  58.8 7.1 %collective-permute-start.23 = (f32[2,56,128]{2,1,0:T(8,128)S(1)}, f32[2,56,128]{2,1,0:T(8,128)S(1)}, u32[]{:S(2)}, u32[]{:S(2)}) collective-permute-start(f32[2,56,128]{2,1,0:T(8,128)S(1)} %get-tuple-element.135), channel_id=1, source_target_pairs={{0,6},{1,7},{2,4},{3,5},{4,2},{5,3},{6,0},{7,1},{8,14},{9,15},{10,... | collective-permute-start | bytes 172040 | tf_op jit(solution)/shard_map/ppermute | solution.py:672
  61.1 4.0 %collective-permute-start.24 = (f32[80,128]{1,0:T(8,128)S(1)}, f32[80,128]{1,0:T(8,128)S(1)}, u32[]{:S(2)}, u32[]{:S(2)}) collective-permute-start(f32[80,128]{1,0:T(8,128)S(1)} %get-tuple-element.136), channel_id=1, source_target_pairs={{0,8},{1,9},{2,10},{3,11},{4,12},{5,13},{6,14},{7,15},{8,0},{9,1},... | collective-permute-start | bytes 122888 | tf_op jit(solution)/shard_map/ppermute | solution.py:675
  68.8 7.4 %collective-permute-start.27 = (f32[2,48,128]{2,1,0:T(8,128)S(1)}, f32[2,48,128]{2,1,0:T(8,128)S(1)}, u32[]{:S(2)}, u32[]{:S(2)}) collective-permute-start(f32[2,48,128]{2,1,0:T(8,128)S(1)} %get-tuple-element.146), channel_id=1, source_target_pairs={{0,2},{1,3},{2,0},{3,1},{4,6},{5,7},{6,4},{7,5},{8,10},{9,11},{10,... | collective-permute-start | bytes 147464 | tf_op jit(solution)/shard_map/ppermute | solution.py:672
  69.5 6.8 %collective-permute-start.28 = (f32[2,48,128]{2,1,0:T(8,128)S(1)}, f32[2,48,128]{2,1,0:T(8,128)S(1)}, u32[]{:S(2)}, u32[]{:S(2)}) collective-permute-start(f32[2,48,128]{2,1,0:T(8,128)S(1)} %get-tuple-element.147), channel_id=1, source_target_pairs={{0,4},{1,5},{2,6},{3,7},{4,0},{5,1},{6,2},{7,3},{8,12},{9,13},{10,... | collective-permute-start | bytes 147464 | tf_op jit(solution)/shard_map/ppermute | solution.py:672
  70.0 6.2 %collective-permute-start.29 = (f32[2,48,128]{2,1,0:T(8,128)S(1)}, f32[2,48,128]{2,1,0:T(8,128)S(1)}, u32[]{:S(2)}, u32[]{:S(2)}) collective-permute-start(f32[2,48,128]{2,1,0:T(8,128)S(1)} %get-tuple-element.148), channel_id=1, source_target_pairs={{0,6},{1,7},{2,4},{3,5},{4,2},{5,3},{6,0},{7,1},{8,14},{9,15},{10,... | collective-permute-start | bytes 147464 | tf_op jit(solution)/shard_map/ppermute | solution.py:672
  72.4 3.8 %collective-permute-start.30 = (f32[48,128]{1,0:T(8,128)S(1)}, f32[48,128]{1,0:T(8,128)S(1)}, u32[]{:S(2)}, u32[]{:S(2)}) collective-permute-start(f32[48,128]{1,0:T(8,128)S(1)} %get-tuple-element.149), channel_id=1, source_target_pairs={{0,8},{1,9},{2,10},{3,11},{4,12},{5,13},{6,14},{7,15},{8,0},{9,1},... | collective-permute-start | bytes 73736 | tf_op jit(solution)/shard_map/ppermute | solution.py:675
  78.9 7.4 %collective-permute-start.33 = (f32[2,48,128]{2,1,0:T(8,128)S(1)}, f32[2,48,128]{2,1,0:T(8,128)S(1)}, u32[]{:S(2)}, u32[]{:S(2)}) collective-permute-start(f32[2,48,128]{2,1,0:T(8,128)S(1)} %get-tuple-element.160), channel_id=1, source_target_pairs={{0,2},{1,3},{2,0},{3,1},{4,6},{5,7},{6,4},{7,5},{8,10},{9,11},{10,... | collective-permute-start | bytes 147464 | tf_op jit(solution)/shard_map/ppermute | solution.py:672
  79.6 6.8 %collective-permute-start.34 = (f32[2,48,128]{2,1,0:T(8,128)S(1)}, f32[2,48,128]{2,1,0:T(8,128)S(1)}, u32[]{:S(2)}, u32[]{:S(2)}) collective-permute-start(f32[2,48,128]{2,1,0:T(8,128)S(1)} %get-tuple-element.161), channel_id=1, source_target_pairs={{0,4},{1,5},{2,6},{3,7},{4,0},{5,1},{6,2},{7,3},{8,12},{9,13},{10,... | collective-permute-start | bytes 147464 | tf_op jit(solution)/shard_map/ppermute | solution.py:672
  80.7 5.6 %collective-permute-start.35 = (f32[2,48,128]{2,1,0:T(8,128)S(1)}, f32[2,48,128]{2,1,0:T(8,128)S(1)}, u32[]{:S(2)}, u32[]{:S(2)}) collective-permute-start(f32[2,48,128]{2,1,0:T(8,128)S(1)} %get-tuple-element.162), channel_id=1, source_target_pairs={{0,6},{1,7},{2,4},{3,5},{4,2},{5,3},{6,0},{7,1},{8,14},{9,15},{10,... | collective-permute-start | bytes 147464 | tf_op jit(solution)/shard_map/ppermute | solution.py:672
  82.5 3.8 %collective-permute-start.36 = (f32[48,128]{1,0:T(8,128)S(1)}, f32[48,128]{1,0:T(8,128)S(1)}, u32[]{:S(2)}, u32[]{:S(2)}) collective-permute-start(f32[48,128]{1,0:T(8,128)S(1)} %get-tuple-element.163), channel_id=1, source_target_pairs={{0,8},{1,9},{2,10},{3,11},{4,12},{5,13},{6,14},{7,15},{8,0},{9,1},... | collective-permute-start | bytes 73736 | tf_op jit(solution)/shard_map/ppermute | solution.py:675
  (21 other events, 48.5 us)

commit v3 on v2

--- a/solution.py
+++ b/solution.py
@@ -210,8 +210,8 @@
 
 def prepare_kernel(
     members, groups, cap, eff, owner_hbm, block_hbm, plane_hbm, hanging_hbm, coarse_rows,
-    payload, first, second, tables,
-    face_owner, face_block, plane_block, hanging, staged, sems, out_sem,
+    mine, other, first, second, tables,
+    face_owner, face_block, plane_block, hanging, special, sems,
 ):
     copies = [
         pltpu.make_async_copy(source, target, sems.at[n])
@@ -282,7 +282,7 @@
         for f in range(4):
             for p in range(2):
                 at = (f * 2 + p) * BLK
-                staged[n, at : at + BLK, :] = packed[f][p]
+                (mine, other)[n % 2][n // 2, at : at + BLK, :] = packed[f][p]
         request = lane_sum(jnp.where(lane64 == n * cap + sub64 % cap, wanted, 0.0))
         last = splat(request)
         at, off = divmod(n * columns, LANES)
@@ -293,10 +293,9 @@
                 more = roll(coarse_tile(rows, at + 1), v * columns - off)
                 part = jnp.where(lane < v * columns + LANES - off, part, more)
             last = jnp.where((lane >= v * columns) & (lane < (v + 1) * columns), part, last)
-        staged[n, 8 * BLK : 9 * BLK, :] = last
-    copy = pltpu.make_async_copy(staged, payload, out_sem)
-    copy.start()
-    copy.wait()
+        special[member ^ n, :, :] = last
+    for n in range(members):
+        (mine, other)[n % 2][n // 2, 8 * BLK : 9 * BLK, :] = special[n, :, :]
 
 
 def weights_kernel(
@@ -307,16 +306,15 @@
     k, g = lane & 15, lane >> 4
     table = Table(tables)
     for n in range(members):
-        last = near[n, 8 * BLK : 9 * BLK, :]
-        coarse[n * BLK : (n + 1) * BLK, :] = last
-        asked = near[lax.axis_index("mem") ^ n, 8 * BLK : 9 * BLK, :]
-        chosen[n * BLK : (n + 1) * BLK, :] = splat(asked[:, LANES - 1 :]).astype(jnp.int32)
+        last = sent_by(near, n, slice(8 * BLK, 9 * BLK))
+        chosen[n * BLK : (n + 1) * BLK, :] = splat(last[:, LANES - 1 :]).astype(jnp.int32)
+        coarse[lax.axis_index("mem") ^ n, :, :] = last
 
     def near_tile(m, d, n):
         at = ((d ^ 1) * 2 + n) * BLK
-        return near[m, at : at + BLK, :], table(Table.BLOCK + d)
-
-    ghost = gather_ghosts(near_tile, members, Table.OWNER, from_first, from_second, table, ghosts, lane, 2)
+        return sent_by(near, m, slice(at, at + BLK)), table(Table.BLOCK + d)
+
+    ghost = gather_ghosts(near_tile, members, Table.APART, from_first, from_second, table, ghosts, lane, 2)
     values = [eff[:, tile(m)] for m in range(TILES)]
     start = [[], [], []]
     for m in range(TILES):
@@ -493,7 +491,7 @@
     rows = [jnp.zeros((BLK, LANES), F32) for _ in range(wide)]
     for n in range(members):
         for v in range(3):
-            have = jnp.where(lane < columns, roll(coarse[n * BLK : (n + 1) * BLK, :], -v * columns), 0.0)
+            have = jnp.where(lane < columns, roll(coarse[n, :, :], -v * columns), 0.0)
             part = splat(lane_sum(have * own))
             place = n * columns + v * BLK
             for t in range(place // LANES, (place + BLK - 1) // LANES + 1):
@@ -662,12 +660,6 @@
             else:
                 second_route.append((q * members + m, (q + 1 if q % 2 else q - 1) * members + m))
 
-    def exchange(payload, first, second):
-        near = lax.all_to_all(payload, "mem", split_axis=0, concat_axis=0, tiled=True)
-        first = lax.ppermute(first, ("grp", "mem"), first_route)
-        second = lax.ppermute(second, ("grp", "mem"), second_route)
-        return near, first, second
-
     def swap(a, bits):
         return lax.ppermute(a, "mem", [(m, m ^ bits) for m in range(members)])
 
@@ -682,21 +674,22 @@
         return [mine, got] + [swap(a, 2 * n + 2) for n, a in enumerate(sent)], first, second
 
     per = 9 * BLK
+    half = array(members // 2, per, LANES)
     eff = viscosity * jnp.exp2(-refinement.astype(F32))[:, None]
-    payload, first, second, tables = call(
+    mine, other, first, second, tables = call(
         functools.partial(prepare_kernel, members, groups, cap),
         [VMEM] + [HBM] * 4 + [VMEM],
-        [array(members, per, LANES), array(16, LANES), array(16, LANES), ints(Table.SIZE * BLK, LANES)],
-        [HBM, VMEM, VMEM, VMEM],
+        [half, half, array(16, LANES), array(16, LANES), ints(Table.SIZE * BLK, LANES)],
+        [VMEM] * 5,
         [
-            pltpu.VMEM((1, 4 * BLK), jnp.int32), pltpu.VMEM((4, BLK), jnp.int32), pltpu.VMEM((2, BLK), jnp.int32),
-            pltpu.VMEM((BLK, 6), jnp.int32), scratch(members, per, LANES),
-            pltpu.SemaphoreType.DMA((4,)), pltpu.SemaphoreType.DMA,
+            pltpu.VMEM((1, 4 * BLK), jnp.int32), pltpu.VMEM((4, BLK), jnp.int32),
+            pltpu.VMEM((2, BLK), jnp.int32), pltpu.VMEM((BLK, 6), jnp.int32), scratch(members, BLK, LANES),
+            pltpu.SemaphoreType.DMA((4,)),
         ],
         "prepare",
         moved=0,
-    )(eff, face_owner.T, face_block.T, plane_block.T, hanging, coarse_solver[0])
-    arrived, from_first, from_second = exchange(payload, first, second)
+    )(eff, face_owner.T, face_block.T, plane_block.T, hanging, jnp.pad(coarse_solver[0], ((0, 0), (0, -coarse_solver.shape[2] % LANES))))
+    near, from_first, from_second = spread(mine, other, first, second)
 
     half = array(members // 2, 6 * cap, LANES)
     sent_out = [half, half, array(48, LANES), array(48, LANES)]
@@ -707,15 +700,15 @@
         return lambda *refs: body(*fixed, refs[:near_refs], *refs[near_refs:])
 
     state, mine, other, first, second, wi, gk, gj, gi, diagonal, inverse, chosen, coarse = call(
-        functools.partial(weights_kernel, members, cap),
-        [VMEM] * 6,
+        gathered(weights_kernel, members, cap),
+        [VMEM] * (near_refs + 5),
         [states] + sent_out
         + [array(5, BLK, CELLS), scalar_field, scalar_field, array(BLK, 4 * LANES), scalar_field, scalar_field]
-        + [ints(members * BLK, LANES), array(members * BLK, LANES)],
+        + [ints(members * BLK, LANES), array(members, BLK, LANES)],
         [VMEM] * 13,
         [scratch(3, 6 * 16, LANES)],
         "weights",
-    )(arrived, from_first, from_second, eff, forcing, tables)
+    )(*near, from_first, from_second, eff, forcing, tables)
 
     field_scratch = [scratch(3, BLK, CELLS), pltpu.SemaphoreType.DMA((3,))]
 

time: 88 us -> 86.9 us (0.988)
  waiting for transfers between devices: 20.6 us -> 19.3 us
    all_to_all x1 -> x0, starting transfers between devices: 5.18 us -> none  [exchange(): lax.all_to_all(payload, 'mem', split_axis=0, concat_axis=0, tiled=True)]
    ppermute x24 -> x28, starting transfers between devices: 21.7 us -> 26.7 us  [swap(): return lax.ppermute(a, 'mem', [(m, m ^ bits) for m in range(members)])]
    all_to_all x1 -> x0, waiting for transfers between devices: 3.63 us -> none  [exchange(): lax.all_to_all(payload, 'mem', split_axis=0, concat_axis=0, tiled=True)]
    ppermute x24 -> x28, waiting for transfers between devices: 7.8 us -> 10.4 us  [swap(): return lax.ppermute(a, 'mem', [(m, m ^ bits) for m in range(members)])]
    ppermute x6 -> x7, starting transfers between devices: 12.4 us -> 14.4 us  [spread(): first = lax.ppermute(first, ('grp', 'mem'), first_route)]
    ppermute x2 -> x0, waiting for transfers between devices: 1.85 us -> none  [the longest x1 1.85 us: exchange(): first = lax.ppermute(first, ('grp', 'mem'), first_route)]
    ppermute x2 -> x0, starting transfers between devices: 1.8 us -> none  [the longest x1 1.58 us: exchange(): first = lax.ppermute(first, ('grp', 'mem'), first_route)]
    ppermute x6 -> x7, waiting for transfers between devices: 7.29 us -> 8.9 us  [spread(): first = lax.ppermute(first, ('grp', 'mem'), first_route)]
  transfers between devices with their start and end apart: 39 -> 42, of which waited for: 14 -> 15; matrix products, arithmetic and copies ran while one was open for 0% -> 0% of each run, Pallas kernels for 5% -> 6%
where the time goes in v3:
time: 86.9 us; the launch traced here: 86.6 us
  starting transfers between devices  41.2 us (47%)
  waiting for transfers between devices  19.3 us (22%)
  Pallas kernels  15.3 us (18%)
  blocking collectives  7.28 us (8%)
  other arithmetic  1.67 us (2%)
  between operations  1.15 us (1%)
    ppermute x28, starting transfers between devices, swap(): return lax.ppermute(a, 'mem', [(m, m ^ bits) for m in range(members)])  26.7 us
    ppermute x7, starting transfers between devices, spread(): first = lax.ppermute(first, ('grp', 'mem'), first_route)  14.4 us
    ppermute x28, waiting for transfers between devices, swap(): return lax.ppermute(a, 'mem', [(m, m ^ bits) for m in range(members)])  10.4 us
    ppermute x7, waiting for transfers between devices, spread(): first = lax.ppermute(first, ('grp', 'mem'), first_route)  8.9 us
    all_to_all x1, blocking collectives, local(): lax.all_to_all(payload, 'mem', split_axis=0, concat_axis=0, tiled=True)  7.28 us
    pallas_call x4, Pallas kernels, outside(): call(gathered(outside_kernel, members, cap, old, new, unknowns is not Non...  5.55 us
    pallas_call x6, Pallas kernels, inside(): call(functools.partial(inside_kernel, x is None, members if lift else 0,...  4.77 us
  transfers between devices with their start and end apart: 42, of which 15 were waited for; matrix products, arithmetic and copies ran while one was open for 0% of the time, Pallas kernels for 6%

profile of v3, /device:TPU:0, one launch (start us, length us, event | category | flops | bytes accessed | tf_op | source)
XLA Modules:
  0.0 86.6 jit_solution(8792432420222355529)
XLA Ops:
  5.3 2.9 %collective-permute-start.1 = (f32[2,72,128]{2,1,0:T(8,128)S(1)}, f32[2,72,128]{2,1,0:T(8,128)S(1)}, u32[]{:S(2)}, u32[]{:S(2)}) collective-permute-start(f32[2,72,128]{2,1,0:T(8,128)S(1)} %get-tuple-element.90), channel_id=1, source_target_pairs={{0,2},{1,3},{2,0},{3,1},{4,6},{5,7},{6,4},{7,5},{8,10},{9,11},{10,... | collective-permute-start | bytes 221192 | tf_op jit(solution)/shard_map/ppermute | solution.py:664
  8.2 1.5 %collective-permute-start.2 = (f32[2,72,128]{2,1,0:T(8,128)S(1)}, f32[2,72,128]{2,1,0:T(8,128)S(1)}, u32[]{:S(2)}, u32[]{:S(2)}) collective-permute-start(f32[2,72,128]{2,1,0:T(8,128)S(1)} %get-tuple-element.91), channel_id=1, source_target_pairs={{0,4},{1,5},{2,6},{3,7},{4,0},{5,1},{6,2},{7,3},{8,12},{9,13},{10,... | collective-permute-start | bytes 221192 | tf_op jit(solution)/shard_map/ppermute | solution.py:664
  9.7 2.0 %collective-permute-start.4 = (f32[16,128]{1,0:T(8,128)S(1)}, f32[16,128]{1,0:T(8,128)S(1)}, u32[]{:S(2)}, u32[]{:S(2)}) collective-permute-start(f32[16,128]{1,0:T(8,128)S(1)} %get-tuple-element.93), channel_id=1, source_target_pairs={{0,8},{1,9},{2,10},{3,11},{4,12},{5,13},{6,14},{7,15},{8,0},{9,1},... | collective-permute-start | bytes 24584 | tf_op jit(solution)/shard_map/ppermute | solution.py:667
  11.7 1.6 %collective-permute-done.4.refs_5_ = f32[16,128]{1,0:T(8,128)S(1)} collective-permute-done((f32[16,128]{1,0:T(8,128)S(1)}, f32[16,128]{1,0:T(8,128)S(1)}, u32[]{:S(2)}, u32[]{:S(2)}) %collective-permute-start.4) | collective-permute-done | bytes 8224 | tf_op jit(solution)/shard_map/ppermute | solution.py:667
  13.4 1.6 %collective-permute-done.3.refs_4_ = f32[2,72,128]{2,1,0:T(8,128)S(1)} collective-permute-done((f32[2,72,128]{2,1,0:T(8,128)S(1)}, f32[2,72,128]{2,1,0:T(8,128)S(1)}, u32[]{:S(2)}, u32[]{:S(2)}) %collective-permute-start.3) | collective-permute-done | bytes 73760 | tf_op jit(solution)/shard_map/ppermute | solution.py:664
  17.8 1.4 %collective-permute-start.8 = (f32[2,48,128]{2,1,0:T(8,128)S(1)}, f32[2,48,128]{2,1,0:T(8,128)S(1)}, u32[]{:S(2)}, u32[]{:S(2)}) collective-permute-start(f32[2,48,128]{2,1,0:T(8,128)S(1)} %get-tuple-element.99), channel_id=1, source_target_pairs={{0,4},{1,5},{2,6},{3,7},{4,0},{5,1},{6,2},{7,3},{8,12},{9,13},{10,... | collective-permute-start | bytes 147464 | tf_op jit(solution)/shard_map/ppermute | solution.py:664
  19.2 1.6 %collective-permute-start.9 = (f32[2,48,128]{2,1,0:T(8,128)S(1)}, f32[2,48,128]{2,1,0:T(8,128)S(1)}, u32[]{:S(2)}, u32[]{:S(2)}) collective-permute-start(f32[2,48,128]{2,1,0:T(8,128)S(1)} %get-tuple-element.100), channel_id=1, source_target_pairs={{0,6},{1,7},{2,4},{3,5},{4,2},{5,3},{6,0},{7,1},{8,14},{9,15},{10,... | collective-permute-start | bytes 147464 | tf_op jit(solution)/shard_map/ppermute | solution.py:664
  20.8 1.6 %collective-permute-start.10 = (f32[48,128]{1,0:T(8,128)S(1)}, f32[48,128]{1,0:T(8,128)S(1)}, u32[]{:S(2)}, u32[]{:S(2)}) collective-permute-start(f32[48,128]{1,0:T(8,128)S(1)} %get-tuple-element.101), channel_id=1, source_target_pairs={{0,8},{1,9},{2,10},{3,11},{4,12},{5,13},{6,14},{7,15},{8,0},{9,1},... | collective-permute-start | bytes 73736 | tf_op jit(solution)/shard_map/ppermute | solution.py:667
  23.1 1.5 %collective-permute-done.10.refs_5_ = f32[48,128]{1,0:T(8,128)S(1)} collective-permute-done((f32[48,128]{1,0:T(8,128)S(1)}, f32[48,128]{1,0:T(8,128)S(1)}, u32[]{:S(2)}, u32[]{:S(2)}) %collective-permute-start.10) | collective-permute-done | bytes 24608 | tf_op jit(solution)/shard_map/ppermute | solution.py:667
  28.5 1.5 %collective-permute-start.14 = (f32[2,48,128]{2,1,0:T(8,128)S(1)}, f32[2,48,128]{2,1,0:T(8,128)S(1)}, u32[]{:S(2)}, u32[]{:S(2)}) collective-permute-start(f32[2,48,128]{2,1,0:T(8,128)S(1)} %get-tuple-element.116), channel_id=1, source_target_pairs={{0,4},{1,5},{2,6},{3,7},{4,0},{5,1},{6,2},{7,3},{8,12},{9,13},{10,... | collective-permute-start | bytes 147464 | tf_op jit(solution)/shard_map/ppermute | solution.py:664
  30.9 2.7 %collective-permute-start.16 = (f32[48,128]{1,0:T(8,128)S(1)}, f32[48,128]{1,0:T(8,128)S(1)}, u32[]{:S(2)}, u32[]{:S(2)}) collective-permute-start(f32[48,128]{1,0:T(8,128)S(1)} %get-tuple-element.118), channel_id=1, source_target_pairs={{0,8},{1,9},{2,10},{3,11},{4,12},{5,13},{6,14},{7,15},{8,0},{9,1},... | collective-permute-start | bytes 73736 | tf_op jit(solution)/shard_map/ppermute | solution.py:667
  38.7 1.4 %collective-permute-start.20 = (f32[2,48,128]{2,1,0:T(8,128)S(1)}, f32[2,48,128]{2,1,0:T(8,128)S(1)}, u32[]{:S(2)}, u32[]{:S(2)}) collective-permute-start(f32[2,48,128]{2,1,0:T(8,128)S(1)} %get-tuple-element.127), channel_id=1, source_target_pairs={{0,4},{1,5},{2,6},{3,7},{4,0},{5,1},{6,2},{7,3},{8,12},{9,13},{10,... | collective-permute-start | bytes 147464 | tf_op jit(solution)/shard_map/ppermute | solution.py:664
  40.1 1.6 %collective-permute-start.21 = (f32[2,48,128]{2,1,0:T(8,128)S(1)}, f32[2,48,128]{2,1,0:T(8,128)S(1)}, u32[]{:S(2)}, u32[]{:S(2)}) collective-permute-start(f32[2,48,128]{2,1,0:T(8,128)S(1)} %get-tuple-element.128), channel_id=1, source_target_pairs={{0,6},{1,7},{2,4},{3,5},{4,2},{5,3},{6,0},{7,1},{8,14},{9,15},{10,... | collective-permute-start | bytes 147464 | tf_op jit(solution)/shard_map/ppermute | solution.py:664
  41.7 2.0 %collective-permute-start.22 = (f32[48,128]{1,0:T(8,128)S(1)}, f32[48,128]{1,0:T(8,128)S(1)}, u32[]{:S(2)}, u32[]{:S(2)}) collective-permute-start(f32[48,128]{1,0:T(8,128)S(1)} %get-tuple-element.129), channel_id=1, source_target_pairs={{0,8},{1,9},{2,10},{3,11},{4,12},{5,13},{6,14},{7,15},{8,0},{9,1},... | collective-permute-start | bytes 73736 | tf_op jit(solution)/shard_map/ppermute | solution.py:667
  45.5 1.6 %coarse.1 = (f32[6,8,4096]{2,1,0:T(8,128)S(1)}, f32[8,8,128]{2,1,0:T(8,128)S(1)}, f32[3,8,4096]{2,1,0:T(8,128)S(1)}) custom-call(f32[4,48,128]{2,1,0:T(8,128)S(1)} %get-tuple-element.124.mine.refs_0_, f32[4,48,128]{2,1,0:T(8,128)S(1)} %collective-permute-done.18.got.refs_1_, ...), custom_call_target="tpu_custom_call", output_to_operand_aliasing={{0}: (7, {}), {2}: (13, {})} | custom-call | flops 2000000 | bytes 2000000 | tf_op jit(solution)/shard_map/coarse/pallas_call | solution.py:758
  47.1 7.3 %all_to_all.5.arrived = f32[8,8,128]{2,1,0:T(8,128)S(1)} all-to-all(f32[8,8,128]{2,1,0:T(8,128)S(1)} %get-tuple-element.136), channel_id=1, replica_groups=mesh['grp'=4,'mem'=8] {'mem'}, dimensions={0} | all-to-all | bytes 65536 | tf_op jit(solution)/shard_map/all_to_all | solution.py:767
  57.6 2.4 %collective-permute-start.27 = (f32[2,56,128]{2,1,0:T(8,128)S(1)}, f32[2,56,128]{2,1,0:T(8,128)S(1)}, u32[]{:S(2)}, u32[]{:S(2)}) collective-permute-start(f32[2,56,128]{2,1,0:T(8,128)S(1)} %get-tuple-element.143), channel_id=1, source_target_pairs={{0,6},{1,7},{2,4},{3,5},{4,2},{5,3},{6,0},{7,1},{8,14},{9,15},{10,... | collective-permute-start | bytes 172040 | tf_op jit(solution)/shard_map/ppermute | solution.py:664
  60.0 2.0 %collective-permute-start.28 = (f32[80,128]{1,0:T(8,128)S(1)}, f32[80,128]{1,0:T(8,128)S(1)}, u32[]{:S(2)}, u32[]{:S(2)}) collective-permute-start(f32[80,128]{1,0:T(8,128)S(1)} %get-tuple-element.144), channel_id=1, source_target_pairs={{0,8},{1,9},{2,10},{3,11},{4,12},{5,13},{6,14},{7,15},{8,0},{9,1},... | collective-permute-start | bytes 122888 | tf_op jit(solution)/shard_map/ppermute | solution.py:667
  62.0 2.0 %collective-permute-done.28.refs_5_ = f32[80,128]{1,0:T(8,128)S(1)} collective-permute-done((f32[80,128]{1,0:T(8,128)S(1)}, f32[80,128]{1,0:T(8,128)S(1)}, u32[]{:S(2)}, u32[]{:S(2)}) %collective-permute-start.28) | collective-permute-done | bytes 40992 | tf_op jit(solution)/shard_map/ppermute | solution.py:667
  64.7 1.6 %outside.6 = (f32[6,8,4096]{2,1,0:T(8,128)S(1)}, f32[4,48,128]{2,1,0:T(8,128)S(1)}, f32[4,48,128]{2,1,0:T(8,128)S(1)}, f32[48,128]{1,0:T(8,128)S(1)}, f32[48,128]{1,0:T(8,128)S(1)}, /*index=5*/f32[3,8,4096]{2,1,0:T(8,128)S(1)}) custom-call(f32[4,56,128]{2,1,0:T(8,128)S(1)} %get-tuple-element.139.mine.refs_0_, ...), custom_call_target="tpu_custom_call", output_to_operand_aliasing={{0}: (7, {}), {5}: (14, {})} | custom-call | flops 2000000 | bytes 2000000 | tf_op jit(solution)/shard_map/outside/pallas_call | solution.py:729
  68.9 2.4 %collective-permute-start.33 = (f32[2,48,128]{2,1,0:T(8,128)S(1)}, f32[2,48,128]{2,1,0:T(8,128)S(1)}, u32[]{:S(2)}, u32[]{:S(2)}) collective-permute-start(f32[2,48,128]{2,1,0:T(8,128)S(1)} %get-tuple-element.156), channel_id=1, source_target_pairs={{0,6},{1,7},{2,4},{3,5},{4,2},{5,3},{6,0},{7,1},{8,14},{9,15},{10,... | collective-permute-start | bytes 147464 | tf_op jit(solution)/shard_map/ppermute | solution.py:664
  71.3 2.0 %collective-permute-start.34 = (f32[48,128]{1,0:T(8,128)S(1)}, f32[48,128]{1,0:T(8,128)S(1)}, u32[]{:S(2)}, u32[]{:S(2)}) collective-permute-start(f32[48,128]{1,0:T(8,128)S(1)} %get-tuple-element.157), channel_id=1, source_target_pairs={{0,8},{1,9},{2,10},{3,11},{4,12},{5,13},{6,14},{7,15},{8,0},{9,1},... | collective-permute-start | bytes 73736 | tf_op jit(solution)/shard_map/ppermute | solution.py:667
  79.6 1.8 %collective-permute-start.39 = (f32[2,48,128]{2,1,0:T(8,128)S(1)}, f32[2,48,128]{2,1,0:T(8,128)S(1)}, u32[]{:S(2)}, u32[]{:S(2)}) collective-permute-start(f32[2,48,128]{2,1,0:T(8,128)S(1)} %get-tuple-element.170), channel_id=1, source_target_pairs={{0,6},{1,7},{2,4},{3,5},{4,2},{5,3},{6,0},{7,1},{8,14},{9,15},{10,... | collective-permute-start | bytes 147464 | tf_op jit(solution)/shard_map/ppermute | solution.py:664
  81.4 2.0 %collective-permute-start.40 = (f32[48,128]{1,0:T(8,128)S(1)}, f32[48,128]{1,0:T(8,128)S(1)}, u32[]{:S(2)}, u32[]{:S(2)}) collective-permute-start(f32[48,128]{1,0:T(8,128)S(1)} %get-tuple-element.171), channel_id=1, source_target_pairs={{0,8},{1,9},{2,10},{3,11},{4,12},{5,13},{6,14},{7,15},{8,0},{9,1},... | collective-permute-start | bytes 73736 | tf_op jit(solution)/shard_map/ppermute | solution.py:667
  (96 shorter events, 35.5 us)
Async XLA Ops:
  5.3 8.1 %collective-permute-start.1 = (f32[2,72,128]{2,1,0:T(8,128)S(1)}, f32[2,72,128]{2,1,0:T(8,128)S(1)}, u32[]{:S(2)}, u32[]{:S(2)}) collective-permute-start(f32[2,72,128]{2,1,0:T(8,128)S(1)} %get-tuple-element.90), channel_id=1, source_target_pairs={{0,2},{1,3},{2,0},{3,1},{4,6},{5,7},{6,4},{7,5},{8,10},{9,11},{10,... | collective-permute-start | bytes 221192 | tf_op jit(solution)/shard_map/ppermute | solution.py:664
  8.2 5.2 %collective-permute-start.2 = (f32[2,72,128]{2,1,0:T(8,128)S(1)}, f32[2,72,128]{2,1,0:T(8,128)S(1)}, u32[]{:S(2)}, u32[]{:S(2)}) collective-permute-start(f32[2,72,128]{2,1,0:T(8,128)S(1)} %get-tuple-element.91), channel_id=1, source_target_pairs={{0,4},{1,5},{2,6},{3,7},{4,0},{5,1},{6,2},{7,3},{8,12},{9,13},{10,... | collective-permute-start | bytes 221192 | tf_op jit(solution)/shard_map/ppermute | solution.py:664
  9.7 5.3 %collective-permute-start.3 = (f32[2,72,128]{2,1,0:T(8,128)S(1)}, f32[2,72,128]{2,1,0:T(8,128)S(1)}, u32[]{:S(2)}, u32[]{:S(2)}) collective-permute-start(f32[2,72,128]{2,1,0:T(8,128)S(1)} %get-tuple-element.92), channel_id=1, source_target_pairs={{0,6},{1,7},{2,4},{3,5},{4,2},{5,3},{6,0},{7,1},{8,14},{9,15},{10,... | collective-permute-start | bytes 221192 | tf_op jit(solution)/shard_map/ppermute | solution.py:664
  17.2 7.4 %collective-permute-start.7 = (f32[2,48,128]{2,1,0:T(8,128)S(1)}, f32[2,48,128]{2,1,0:T(8,128)S(1)}, u32[]{:S(2)}, u32[]{:S(2)}) collective-permute-start(f32[2,48,128]{2,1,0:T(8,128)S(1)} %get-tuple-element.98), channel_id=1, source_target_pairs={{0,2},{1,3},{2,0},{3,1},{4,6},{5,7},{6,4},{7,5},{8,10},{9,11},{10,... | collective-permute-start | bytes 147464 | tf_op jit(solution)/shard_map/ppermute | solution.py:664
  17.8 6.8 %collective-permute-start.8 = (f32[2,48,128]{2,1,0:T(8,128)S(1)}, f32[2,48,128]{2,1,0:T(8,128)S(1)}, u32[]{:S(2)}, u32[]{:S(2)}) collective-permute-start(f32[2,48,128]{2,1,0:T(8,128)S(1)} %get-tuple-element.99), channel_id=1, source_target_pairs={{0,4},{1,5},{2,6},{3,7},{4,0},{5,1},{6,2},{7,3},{8,12},{9,13},{10,... | collective-permute-start | bytes 147464 | tf_op jit(solution)/shard_map/ppermute | solution.py:664
  19.2 5.4 %collective-permute-start.9 = (f32[2,48,128]{2,1,0:T(8,128)S(1)}, f32[2,48,128]{2,1,0:T(8,128)S(1)}, u32[]{:S(2)}, u32[]{:S(2)}) collective-permute-start(f32[2,48,128]{2,1,0:T(8,128)S(1)} %get-tuple-element.100), channel_id=1, source_target_pairs={{0,6},{1,7},{2,4},{3,5},{4,2},{5,3},{6,0},{7,1},{8,14},{9,15},{10,... | collective-permute-start | bytes 147464 | tf_op jit(solution)/shard_map/ppermute | solution.py:664
  27.3 8.1 %collective-permute-start.13 = (f32[2,48,128]{2,1,0:T(8,128)S(1)}, f32[2,48,128]{2,1,0:T(8,128)S(1)}, u32[]{:S(2)}, u32[]{:S(2)}) collective-permute-start(f32[2,48,128]{2,1,0:T(8,128)S(1)} %get-tuple-element.115), channel_id=1, source_target_pairs={{0,2},{1,3},{2,0},{3,1},{4,6},{5,7},{6,4},{7,5},{8,10},{9,11},{10,... | collective-permute-start | bytes 147464 | tf_op jit(solution)/shard_map/ppermute | solution.py:664
  28.5 6.9 %collective-permute-start.14 = (f32[2,48,128]{2,1,0:T(8,128)S(1)}, f32[2,48,128]{2,1,0:T(8,128)S(1)}, u32[]{:S(2)}, u32[]{:S(2)}) collective-permute-start(f32[2,48,128]{2,1,0:T(8,128)S(1)} %get-tuple-element.116), channel_id=1, source_target_pairs={{0,4},{1,5},{2,6},{3,7},{4,0},{5,1},{6,2},{7,3},{8,12},{9,13},{10,... | collective-permute-start | bytes 147464 | tf_op jit(solution)/shard_map/ppermute | solution.py:664
  30.0 5.4 %collective-permute-start.15 = (f32[2,48,128]{2,1,0:T(8,128)S(1)}, f32[2,48,128]{2,1,0:T(8,128)S(1)}, u32[]{:S(2)}, u32[]{:S(2)}) collective-permute-start(f32[2,48,128]{2,1,0:T(8,128)S(1)} %get-tuple-element.117), channel_id=1, source_target_pairs={{0,6},{1,7},{2,4},{3,5},{4,2},{5,3},{6,0},{7,1},{8,14},{9,15},{10,... | collective-permute-start | bytes 147464 | tf_op jit(solution)/shard_map/ppermute | solution.py:664
  30.9 4.5 %collective-permute-start.16 = (f32[48,128]{1,0:T(8,128)S(1)}, f32[48,128]{1,0:T(8,128)S(1)}, u32[]{:S(2)}, u32[]{:S(2)}) collective-permute-start(f32[48,128]{1,0:T(8,128)S(1)} %get-tuple-element.118), channel_id=1, source_target_pairs={{0,8},{1,9},{2,10},{3,11},{4,12},{5,13},{6,14},{7,15},{8,0},{9,1},... | collective-permute-start | bytes 73736 | tf_op jit(solution)/shard_map/ppermute | solution.py:667
  38.1 7.4 %collective-permute-start.19 = (f32[2,48,128]{2,1,0:T(8,128)S(1)}, f32[2,48,128]{2,1,0:T(8,128)S(1)}, u32[]{:S(2)}, u32[]{:S(2)}) collective-permute-start(f32[2,48,128]{2,1,0:T(8,128)S(1)} %get-tuple-element.126), channel_id=1, source_target_pairs={{0,2},{1,3},{2,0},{3,1},{4,6},{5,7},{6,4},{7,5},{8,10},{9,11},{10,... | collective-permute-start | bytes 147464 | tf_op jit(solution)/shard_map/ppermute | solution.py:664
  38.7 6.8 %collective-permute-start.20 = (f32[2,48,128]{2,1,0:T(8,128)S(1)}, f32[2,48,128]{2,1,0:T(8,128)S(1)}, u32[]{:S(2)}, u32[]{:S(2)}) collective-permute-start(f32[2,48,128]{2,1,0:T(8,128)S(1)} %get-tuple-element.127), channel_id=1, source_target_pairs={{0,4},{1,5},{2,6},{3,7},{4,0},{5,1},{6,2},{7,3},{8,12},{9,13},{10,... | collective-permute-start | bytes 147464 | tf_op jit(solution)/shard_map/ppermute | solution.py:664
  40.1 5.4 %collective-permute-start.21 = (f32[2,48,128]{2,1,0:T(8,128)S(1)}, f32[2,48,128]{2,1,0:T(8,128)S(1)}, u32[]{:S(2)}, u32[]{:S(2)}) collective-permute-start(f32[2,48,128]{2,1,0:T(8,128)S(1)} %get-tuple-element.128), channel_id=1, source_target_pairs={{0,6},{1,7},{2,4},{3,5},{4,2},{5,3},{6,0},{7,1},{8,14},{9,15},{10,... | collective-permute-start | bytes 147464 | tf_op jit(solution)/shard_map/ppermute | solution.py:664
  56.5 8.3 %collective-permute-start.25 = (f32[2,56,128]{2,1,0:T(8,128)S(1)}, f32[2,56,128]{2,1,0:T(8,128)S(1)}, u32[]{:S(2)}, u32[]{:S(2)}) collective-permute-start(f32[2,56,128]{2,1,0:T(8,128)S(1)} %get-tuple-element.141), channel_id=1, source_target_pairs={{0,2},{1,3},{2,0},{3,1},{4,6},{5,7},{6,4},{7,5},{8,10},{9,11},{10,... | collective-permute-start | bytes 172040 | tf_op jit(solution)/shard_map/ppermute | solution.py:664
  57.1 7.6 %collective-permute-start.26 = (f32[2,56,128]{2,1,0:T(8,128)S(1)}, f32[2,56,128]{2,1,0:T(8,128)S(1)}, u32[]{:S(2)}, u32[]{:S(2)}) collective-permute-start(f32[2,56,128]{2,1,0:T(8,128)S(1)} %get-tuple-element.142), channel_id=1, source_target_pairs={{0,4},{1,5},{2,6},{3,7},{4,0},{5,1},{6,2},{7,3},{8,12},{9,13},{10,... | collective-permute-start | bytes 172040 | tf_op jit(solution)/shard_map/ppermute | solution.py:664
  57.6 7.1 %collective-permute-start.27 = (f32[2,56,128]{2,1,0:T(8,128)S(1)}, f32[2,56,128]{2,1,0:T(8,128)S(1)}, u32[]{:S(2)}, u32[]{:S(2)}) collective-permute-start(f32[2,56,128]{2,1,0:T(8,128)S(1)} %get-tuple-element.143), channel_id=1, source_target_pairs={{0,6},{1,7},{2,4},{3,5},{4,2},{5,3},{6,0},{7,1},{8,14},{9,15},{10,... | collective-permute-start | bytes 172040 | tf_op jit(solution)/shard_map/ppermute | solution.py:664
  60.0 4.0 %collective-permute-start.28 = (f32[80,128]{1,0:T(8,128)S(1)}, f32[80,128]{1,0:T(8,128)S(1)}, u32[]{:S(2)}, u32[]{:S(2)}) collective-permute-start(f32[80,128]{1,0:T(8,128)S(1)} %get-tuple-element.144), channel_id=1, source_target_pairs={{0,8},{1,9},{2,10},{3,11},{4,12},{5,13},{6,14},{7,15},{8,0},{9,1},... | collective-permute-start | bytes 122888 | tf_op jit(solution)/shard_map/ppermute | solution.py:667
  67.7 7.4 %collective-permute-start.31 = (f32[2,48,128]{2,1,0:T(8,128)S(1)}, f32[2,48,128]{2,1,0:T(8,128)S(1)}, u32[]{:S(2)}, u32[]{:S(2)}) collective-permute-start(f32[2,48,128]{2,1,0:T(8,128)S(1)} %get-tuple-element.154), channel_id=1, source_target_pairs={{0,2},{1,3},{2,0},{3,1},{4,6},{5,7},{6,4},{7,5},{8,10},{9,11},{10,... | collective-permute-start | bytes 147464 | tf_op jit(solution)/shard_map/ppermute | solution.py:664
  68.4 6.8 %collective-permute-start.32 = (f32[2,48,128]{2,1,0:T(8,128)S(1)}, f32[2,48,128]{2,1,0:T(8,128)S(1)}, u32[]{:S(2)}, u32[]{:S(2)}) collective-permute-start(f32[2,48,128]{2,1,0:T(8,128)S(1)} %get-tuple-element.155), channel_id=1, source_target_pairs={{0,4},{1,5},{2,6},{3,7},{4,0},{5,1},{6,2},{7,3},{8,12},{9,13},{10,... | collective-permute-start | bytes 147464 | tf_op jit(solution)/shard_map/ppermute | solution.py:664
  68.9 6.2 %collective-permute-start.33 = (f32[2,48,128]{2,1,0:T(8,128)S(1)}, f32[2,48,128]{2,1,0:T(8,128)S(1)}, u32[]{:S(2)}, u32[]{:S(2)}) collective-permute-start(f32[2,48,128]{2,1,0:T(8,128)S(1)} %get-tuple-element.156), channel_id=1, source_target_pairs={{0,6},{1,7},{2,4},{3,5},{4,2},{5,3},{6,0},{7,1},{8,14},{9,15},{10,... | collective-permute-start | bytes 147464 | tf_op jit(solution)/shard_map/ppermute | solution.py:664
  71.3 3.8 %collective-permute-start.34 = (f32[48,128]{1,0:T(8,128)S(1)}, f32[48,128]{1,0:T(8,128)S(1)}, u32[]{:S(2)}, u32[]{:S(2)}) collective-permute-start(f32[48,128]{1,0:T(8,128)S(1)} %get-tuple-element.157), channel_id=1, source_target_pairs={{0,8},{1,9},{2,10},{3,11},{4,12},{5,13},{6,14},{7,15},{8,0},{9,1},... | collective-permute-start | bytes 73736 | tf_op jit(solution)/shard_map/ppermute | solution.py:667
  77.8 7.4 %collective-permute-start.37 = (f32[2,48,128]{2,1,0:T(8,128)S(1)}, f32[2,48,128]{2,1,0:T(8,128)S(1)}, u32[]{:S(2)}, u32[]{:S(2)}) collective-permute-start(f32[2,48,128]{2,1,0:T(8,128)S(1)} %get-tuple-element.168), channel_id=1, source_target_pairs={{0,2},{1,3},{2,0},{3,1},{4,6},{5,7},{6,4},{7,5},{8,10},{9,11},{10,... | collective-permute-start | bytes 147464 | tf_op jit(solution)/shard_map/ppermute | solution.py:664
  78.5 6.8 %collective-permute-start.38 = (f32[2,48,128]{2,1,0:T(8,128)S(1)}, f32[2,48,128]{2,1,0:T(8,128)S(1)}, u32[]{:S(2)}, u32[]{:S(2)}) collective-permute-start(f32[2,48,128]{2,1,0:T(8,128)S(1)} %get-tuple-element.169), channel_id=1, source_target_pairs={{0,4},{1,5},{2,6},{3,7},{4,0},{5,1},{6,2},{7,3},{8,12},{9,13},{10,... | collective-permute-start | bytes 147464 | tf_op jit(solution)/shard_map/ppermute | solution.py:664
  79.6 5.6 %collective-permute-start.39 = (f32[2,48,128]{2,1,0:T(8,128)S(1)}, f32[2,48,128]{2,1,0:T(8,128)S(1)}, u32[]{:S(2)}, u32[]{:S(2)}) collective-permute-start(f32[2,48,128]{2,1,0:T(8,128)S(1)} %get-tuple-element.170), channel_id=1, source_target_pairs={{0,6},{1,7},{2,4},{3,5},{4,2},{5,3},{6,0},{7,1},{8,14},{9,15},{10,... | collective-permute-start | bytes 147464 | tf_op jit(solution)/shard_map/ppermute | solution.py:664
  (23 other events, 61.6 us)

commit v4 on v3

--- a/solution.py
+++ b/solution.py
@@ -105,9 +105,9 @@
         return self.ref[n * BLK : (n + 1) * BLK, :]
 
 
-def gather_ghosts(near_tile, members, who, first, second, table, ghosts, lane, rows, amend=None):
+def gather_ghosts(near_tile, members, who, first, second, table, ghosts, lane, rows, amend=None, faces=range(6)):
     even = table(Table.EVEN) == 1
-    for d in range(6):
+    for d in faces:
         for n in range(rows):
             if d < 4:
                 v = None
@@ -127,21 +127,21 @@
             at = (d * rows + n) * BLK
             ghosts[0, at : at + BLK, :] = v
     for stage in range(2):
-        for d in range(6):
+        for d in faces:
             bit = 16 if stage else (2 if d < 2 else 1)
             low = (lane & bit) == 0
             for n in range(rows):
                 at = (d * rows + n) * BLK
                 v = ghosts[stage, at : at + BLK, :]
                 ghosts[stage + 1, at : at + BLK, :] = v + jnp.where(low, roll(v, -bit), roll(v, bit))
-    result = []
-    for d in range(6):
+    result = {}
+    for d in faces:
         hang = table(Table.HANG + d) == 1
         tiles = []
         for n in range(rows):
             at = (d * rows + n) * BLK
             tiles.append(jnp.where(hang, ghosts[2, at : at + BLK, :] * 0.25, ghosts[0, at : at + BLK, :]))
-        result.append(tiles)
+        result[d] = tiles
     return result
 
 
@@ -150,13 +150,13 @@
     return near[bit][0, rows, :] if pair == 0 else near[1 + pair][bit, rows, :]
 
 
-def step_ghosts(members, cap, near, first, second, table, ghosts, lane, amend=None):
+def step_ghosts(members, cap, near, first, second, table, ghosts, lane, amend=None, faces=range(6)):
     def near_tile(m, d, n):
         start = n * cap
         at = start // BLK * BLK
         return sent_by(near, m, slice(at, at + BLK)), table(Table.SLOT + d) + (start - at)
 
-    return gather_ghosts(near_tile, members, Table.APART, first, second, table, ghosts, lane, 6, amend)
+    return gather_ghosts(near_tile, members, Table.APART, first, second, table, ghosts, lane, 6, amend, faces)
 
 
 def look_up(rows, block, lane):
@@ -364,27 +364,28 @@
         pair[1, :, :] = got[n + 1, :, :]
 
 
-def inside_kernel(first_step, has_lift, final, *refs):
+def inside_kernel(first_step, lifted, final, members, *refs):
     refs = list(refs)
     state, wi, diagonal = refs[:3]
     refs = refs[3:]
+    lane = lane_id()
+    lift, fixed = None, {}
     x = None if first_step else refs.pop(0)
-    lift, fixed = None, {}
-    if has_lift:
+    if lifted:
         lift = refs.pop(0)
-        fixed = lift_inside(has_lift, refs[0], refs[1], state, *refs[2:5])
+        fixed = lift_inside(members, refs[0], refs[1], state, *refs[2:5])
         refs = refs[5:]
     out, new_x = refs[:2]
     if final:
         staged, sems = refs[2:]
-    g = lane_id() >> 4
+    g = lane >> 4
     copies = []
 
     def get(row, m):
         return fixed[row, m] if (row, m) in fixed else state[row, :, tile(m)]
 
     for c in range(3):
-        up = None if not has_lift else lift[c * BLK : (c + 1) * BLK, :]
+        up = lift[c * BLK : (c + 1) * BLK, :] if lifted else None
         for m in range(TILES):
             i, h = divmod(m, 2)
             s = get(S + c, m)
@@ -404,7 +405,7 @@
                 acc = acc + wi[4, :, tile(m + 2)] * get(S + c, m + 2)
             out[R + c, :, tile(m)] = acc
             total = s if first_step else x[c, :, tile(m)] + s
-            if has_lift:
+            if lifted:
                 total = total + up
             if final:
                 staged[c, :, tile(m)] = total
@@ -420,11 +421,14 @@
         copy.wait()
 
 
-def add_ghosts(c, m, value, ghost, gk, gj, gi, lane):
-    i, h = divmod(m, 2)
+def add_side(c, m, value, ghost, gk, gj, lane):
     pair = slice(2 * c, 2 * c + 2)
     value = value + gk[:, tile(m)] * unpack_k(ghost[0][pair], ghost[1][pair], lane, m)
-    value = value + gj[:, tile(m)] * unpack_j(ghost[2][pair], ghost[3][pair], m)
+    return value + gj[:, tile(m)] * unpack_j(ghost[2][pair], ghost[3][pair], m)
+
+
+def add_ends(c, m, value, ghost, gi):
+    i, h = divmod(m, 2)
     if i == 0:
         value = value + gi[:, tile(h)] * ghost[4][2 * c + h]
     if i == EDGE - 1:
@@ -432,19 +436,38 @@
     return value
 
 
-def outside_kernel(members, cap, old, new, has_lift, near, from_first, from_second, state, *refs):
-    inverse, gk, gj, gi, tables, chosen, x = refs[:7]
+def side_kernel(members, cap, near, state, gk, gj, tables, out, ghosts):
+    lane = lane_id()
+    ghost = step_ghosts(members, cap, near, None, None, Table(tables), ghosts, lane, None, range(4))
+    for c in range(3):
+        for batch in BATCHES:
+            done = [(m, add_side(c, m, state[R + c, :, tile(m)], ghost, gk, gj, lane)) for m in batch]
+            for m, r in done:
+                out[R + c, :, tile(m)] = r
+    out[S : S + 3, :, :] = state[S : S + 3, :, :]
+
+
+def outside_kernel(
+    members, cap, old, new, from_first, from_second, state, inverse, gi, tables, chosen, x, *refs,
+):
     out, mine, other, first, second, same_x, ghosts = refs[-7:]
     lane = lane_id()
     table = Table(tables)
-    amend = lift_outside(members, cap, near, from_first, from_second, refs[7], tables) if has_lift else None
-    ghost = step_ghosts(members, cap, near, from_first, from_second, table, ghosts, lane, amend)
+    lifted = len(refs) > 7
+    if lifted:
+        near, (unknowns, gk, gj) = refs[:-10], refs[-10:-7]
+        amend = lift_outside(members, cap, near, from_first, from_second, unknowns, tables)
+        ghost = step_ghosts(members, cap, near, from_first, from_second, table, ghosts, lane, amend)
+    else:
+        ghost = step_ghosts(members, cap, None, from_first, from_second, table, ghosts, lane, None, (4, 5))
     for c in range(3):
         values = []
         for batch in BATCHES:
             done = []
             for m in batch:
-                r = add_ghosts(c, m, state[R + c, :, tile(m)], ghost, gk, gj, gi, lane)
+                r = add_ends(c, m, state[R + c, :, tile(m)], ghost, gi)
+                if lifted:
+                    r = add_side(c, m, r, ghost, gk, gj, lane)
                 done.append((m, r, old * state[S + c, :, tile(m)] + new * (r * inverse[:, tile(m)])))
             for m, r, s in done:
                 out[R + c, :, tile(m)] = r
@@ -454,31 +477,32 @@
 
 
 def last_kernel(
-    members, cap, near, from_first, from_second, state, gk, gj, gi, tables, new_residual, ghosts, staged, sems,
+    members, cap, near, from_first, from_second, state, gk, gj, gi, tables, residual, ghosts, staged, sems,
 ):
     lane = lane_id()
     ghost = step_ghosts(members, cap, near, from_first, from_second, Table(tables), ghosts, lane)
     copies = []
     for c in range(3):
         for m in range(TILES):
-            staged[c, :, tile(m)] = add_ghosts(c, m, state[R + c, :, tile(m)], ghost, gk, gj, gi, lane)
-        copies.append(pltpu.make_async_copy(staged.at[c], new_residual.at[c], sems.at[c]))
+            r = add_ends(c, m, state[R + c, :, tile(m)], ghost, gi)
+            staged[c, :, tile(m)] = add_side(c, m, r, ghost, gk, gj, lane)
+        copies.append(pltpu.make_async_copy(staged.at[c], residual.at[c], sems.at[c]))
         copies[c].start()
     for copy in copies:
         copy.wait()
 
 
 def coarse_kernel(
-    members, cap, near, from_first, from_second, state, gk, gj, gi, tables, coarse, x,
+    members, cap, from_first, from_second, state, gi, tables, coarse, x,
     out_state, payload, same_x, ghosts,
 ):
     lane, sub = lane_id(), sub_id()
-    ghost = step_ghosts(members, cap, near, from_first, from_second, Table(tables), ghosts, lane)
+    ghost = step_ghosts(members, cap, None, from_first, from_second, Table(tables), ghosts, lane, None, (4, 5))
     placed = jnp.zeros((BLK, LANES), F32)
     for c in range(3):
         sums = [None] * 4
         for batch in BATCHES:
-            done = [(m, add_ghosts(c, m, state[R + c, :, tile(m)], ghost, gk, gj, gi, lane)) for m in batch]
+            done = [(m, add_ends(c, m, state[R + c, :, tile(m)], ghost, gi)) for m in batch]
             for m, r in done:
                 out_state[R + c, :, tile(m)] = r
                 sums[m % 4] = r if sums[m % 4] is None else sums[m % 4] + r
@@ -715,7 +739,7 @@
     def inside(state, x=None, lift=(), final=False):
         operands = [state, wi, diagonal] + ([] if x is None else [x]) + list(lift)
         return call(
-            functools.partial(inside_kernel, x is None, members if lift else 0, final),
+            functools.partial(inside_kernel, x is None, bool(lift), final, members),
             [VMEM] * len(operands),
             [states, field],
             [VMEM, HBM if final else VMEM],
@@ -724,17 +748,27 @@
             {0: 0} if x is None or final else {0: 0, 3: 1},
         )(*operands)
 
-    def outside(near, from_first, from_second, state, x, old, new, unknowns=None):
-        more = [] if unknowns is None else [unknowns]
+    def side(near, state):
         return call(
-            gathered(outside_kernel, members, cap, old, new, unknowns is not None),
-            [VMEM] * (near_refs + 9) + [ANY] + [VMEM] * len(more),
+            gathered(side_kernel, members, cap),
+            [VMEM] * (near_refs + 4),
+            [states],
+            [VMEM],
+            ghost_scratch,
+            "side",
+            {near_refs: 0},
+        )(*near, state, gk, gj, tables)[0]
+
+    def outside(from_first, from_second, state, x, old, new, more=()):
+        return call(
+            functools.partial(outside_kernel, members, cap, old, new),
+            [VMEM] * 7 + [ANY] + [VMEM] * len(more),
             [states] + sent_out + [field],
             [VMEM] * 5 + [ANY],
             ghost_scratch,
             "outside",
-            {near_refs + 2: 0, near_refs + 9: 5},
-        )(*near, from_first, from_second, state, inverse, gk, gj, gi, tables, chosen, x, *more)
+            {2: 0, 7: 5},
+        )(from_first, from_second, state, inverse, gi, tables, chosen, x, *more)
 
     rho = 1.0 / SIGMA
     factors = []
@@ -746,24 +780,28 @@
     def steps(state, sent, x, lift=None, unknowns=None):
         for n, (old, new) in enumerate(factors):
             near, from_first, from_second = spread(*sent)
-            more = (lift, from_first, from_second, inverse, gi, tables) if n == 0 and lift is not None else ()
-            state, x = inside(state, x, more)
-            state, *sent, x = outside(
-                near, from_first, from_second, state, x, old, new, unknowns if n == 0 else None
-            )
+            more = ()
+            if n == 0 and lift is not None:
+                state, x = inside(state, x, (lift, from_first, from_second, inverse, gi, tables))
+                more = (*near, unknowns, gk, gj)
+            else:
+                state, x = inside(state, x)
+                state = side(near, state)
+            state, *sent, x = outside(from_first, from_second, state, x, old, new, more)
         return state, x, spread(*sent)
 
     state, x, (near, from_first, from_second) = steps(state, (mine, other, first, second), None)
     state, x = inside(state, x)
+    state = side(near, state)
     state, payload, x = call(
-        gathered(coarse_kernel, members, cap),
-        [VMEM] * (near_refs + 8) + [ANY],
+        functools.partial(coarse_kernel, members, cap),
+        [VMEM] * 6 + [ANY],
         [states, array(members, BLK, LANES), field],
         [VMEM, VMEM, ANY],
         ghost_scratch,
         "coarse",
-        {near_refs + 2: 0, near_refs + 8: 2},
-    )(*near, from_first, from_second, state, gk, gj, gi, tables, coarse, x)
+        {2: 0, 6: 2},
+    )(from_first, from_second, state, gi, tables, coarse, x)
     sums = lax.all_to_all(payload, "mem", split_axis=0, concat_axis=0, tiled=True)
     half = array(members // 2, 6 * cap + BLK, LANES)
     state, lift, unknowns, *sent, x = call(

time: 86.9 us -> 84.5 us (0.972)
  waiting for transfers between devices: 19.3 us -> 16.8 us
  Pallas kernels: 15.3 us -> 14.3 us
    ppermute x7, waiting for transfers between devices: 8.9 us -> 4.54 us  [spread(): first = lax.ppermute(first, ('grp', 'mem'), first_route)]
    ppermute x28, waiting for transfers between devices: 10.4 us -> 12.3 us  [swap(): return lax.ppermute(a, 'mem', [(m, m ^ bits) for m in range(members)])]
    pallas_call x11 -> x15, Pallas kernels: 11.9 us -> 10.9 us  [the longest x6 4.77 us: inside(): call(functools.partial(inside_kernel, x is None, bool(lift), final, membe...]
  transfers between devices with their start and end apart: 42 -> 42, of which waited for: 15 -> 15; matrix products, arithmetic and copies ran while one was open for 0% -> 0% of each run, Pallas kernels for 6% -> 9%
where the time goes in v4:
time: 84.5 us; the launch traced here: 84.2 us
  starting transfers between devices  41.7 us (49%)
  waiting for transfers between devices  16.8 us (20%)
  Pallas kernels  14.3 us (17%)
  blocking collectives  7.71 us (9%)
  other arithmetic  1.67 us (2%)
  between operations  1.2 us (1%)
    ppermute x28, starting transfers between devices, swap(): return lax.ppermute(a, 'mem', [(m, m ^ bits) for m in range(members)])  26.8 us
    ppermute x7, starting transfers between devices, spread(): first = lax.ppermute(first, ('grp', 'mem'), first_route)  14.9 us
    ppermute x28, waiting for transfers between devices, swap(): return lax.ppermute(a, 'mem', [(m, m ^ bits) for m in range(members)])  12.3 us
    all_to_all x1, blocking collectives, local(): lax.all_to_all(payload, 'mem', split_axis=0, concat_axis=0, tiled=True)  7.71 us
    pallas_call x6, Pallas kernels, inside(): call(functools.partial(inside_kernel, x is None, bool(lift), final, membe...  4.77 us
    ppermute x7, waiting for transfers between devices, spread(): first = lax.ppermute(first, ('grp', 'mem'), first_route)  4.54 us
    pallas_call x4, Pallas kernels, outside(): call(functools.partial(outside_kernel, members, cap, old, new), [VMEM] *...  3.3 us
    pallas_call x4, Pallas kernels, side(): call(gathered(side_kernel, members, cap), [VMEM] * (near_refs + 4), [stat...  2.46 us
  transfers between devices with their start and end apart: 42, of which 15 were waited for; matrix products, arithmetic and copies ran while one was open for 0% of the time, Pallas kernels for 9%

profile of v4, /device:TPU:0, one launch (start us, length us, event | category | flops | bytes accessed | tf_op | source)
XLA Modules:
  0.0 84.2 jit_solution(13439290407064046759)
XLA Ops:
  5.3 2.9 %collective-permute-start.1 = (f32[2,72,128]{2,1,0:T(8,128)S(1)}, f32[2,72,128]{2,1,0:T(8,128)S(1)}, u32[]{:S(2)}, u32[]{:S(2)}) collective-permute-start(f32[2,72,128]{2,1,0:T(8,128)S(1)} %get-tuple-element.90), channel_id=1, source_target_pairs={{0,2},{1,3},{2,0},{3,1},{4,6},{5,7},{6,4},{7,5},{8,10},{9,11},{10,... | collective-permute-start | bytes 221192 | tf_op jit(solution)/shard_map/ppermute | solution.py:688
  8.2 1.5 %collective-permute-start.2 = (f32[2,72,128]{2,1,0:T(8,128)S(1)}, f32[2,72,128]{2,1,0:T(8,128)S(1)}, u32[]{:S(2)}, u32[]{:S(2)}) collective-permute-start(f32[2,72,128]{2,1,0:T(8,128)S(1)} %get-tuple-element.91), channel_id=1, source_target_pairs={{0,4},{1,5},{2,6},{3,7},{4,0},{5,1},{6,2},{7,3},{8,12},{9,13},{10,... | collective-permute-start | bytes 221192 | tf_op jit(solution)/shard_map/ppermute | solution.py:688
  9.7 2.0 %collective-permute-start.4 = (f32[16,128]{1,0:T(8,128)S(1)}, f32[16,128]{1,0:T(8,128)S(1)}, u32[]{:S(2)}, u32[]{:S(2)}) collective-permute-start(f32[16,128]{1,0:T(8,128)S(1)} %get-tuple-element.93), channel_id=1, source_target_pairs={{0,8},{1,9},{2,10},{3,11},{4,12},{5,13},{6,14},{7,15},{8,0},{9,1},... | collective-permute-start | bytes 24584 | tf_op jit(solution)/shard_map/ppermute | solution.py:691
  11.7 1.6 %collective-permute-done.4.refs_5_ = f32[16,128]{1,0:T(8,128)S(1)} collective-permute-done((f32[16,128]{1,0:T(8,128)S(1)}, f32[16,128]{1,0:T(8,128)S(1)}, u32[]{:S(2)}, u32[]{:S(2)}) %collective-permute-start.4) | collective-permute-done | bytes 8224 | tf_op jit(solution)/shard_map/ppermute | solution.py:691
  13.4 1.6 %collective-permute-done.3.refs_4_ = f32[2,72,128]{2,1,0:T(8,128)S(1)} collective-permute-done((f32[2,72,128]{2,1,0:T(8,128)S(1)}, f32[2,72,128]{2,1,0:T(8,128)S(1)}, u32[]{:S(2)}, u32[]{:S(2)}) %collective-permute-start.3) | collective-permute-done | bytes 73760 | tf_op jit(solution)/shard_map/ppermute | solution.py:688
  17.8 1.4 %collective-permute-start.10 = (f32[2,48,128]{2,1,0:T(8,128)S(1)}, f32[2,48,128]{2,1,0:T(8,128)S(1)}, u32[]{:S(2)}, u32[]{:S(2)}) collective-permute-start(f32[2,48,128]{2,1,0:T(8,128)S(1)} %get-tuple-element.101), channel_id=1, source_target_pairs={{0,4},{1,5},{2,6},{3,7},{4,0},{5,1},{6,2},{7,3},{8,12},{9,13},{10,... | collective-permute-start | bytes 147464 | tf_op jit(solution)/shard_map/ppermute | solution.py:688
  19.2 1.6 %collective-permute-start.11 = (f32[2,48,128]{2,1,0:T(8,128)S(1)}, f32[2,48,128]{2,1,0:T(8,128)S(1)}, u32[]{:S(2)}, u32[]{:S(2)}) collective-permute-start(f32[2,48,128]{2,1,0:T(8,128)S(1)} %get-tuple-element.102), channel_id=1, source_target_pairs={{0,6},{1,7},{2,4},{3,5},{4,2},{5,3},{6,0},{7,1},{8,14},{9,15},{10,... | collective-permute-start | bytes 147464 | tf_op jit(solution)/shard_map/ppermute | solution.py:688
  20.8 1.6 %collective-permute-start.6 = (f32[48,128]{1,0:T(8,128)S(1)}, f32[48,128]{1,0:T(8,128)S(1)}, u32[]{:S(2)}, u32[]{:S(2)}) collective-permute-start(f32[48,128]{1,0:T(8,128)S(1)} %get-tuple-element.96), channel_id=1, source_target_pairs={{0,8},{1,9},{2,10},{3,11},{4,12},{5,13},{6,14},{7,15},{8,0},{9,1},... | collective-permute-start | bytes 73736 | tf_op jit(solution)/shard_map/ppermute | solution.py:691
  27.7 1.5 %collective-permute-start.16 = (f32[2,48,128]{2,1,0:T(8,128)S(1)}, f32[2,48,128]{2,1,0:T(8,128)S(1)}, u32[]{:S(2)}, u32[]{:S(2)}) collective-permute-start(f32[2,48,128]{2,1,0:T(8,128)S(1)} %get-tuple-element.118), channel_id=1, source_target_pairs={{0,4},{1,5},{2,6},{3,7},{4,0},{5,1},{6,2},{7,3},{8,12},{9,13},{10,... | collective-permute-start | bytes 147464 | tf_op jit(solution)/shard_map/ppermute | solution.py:688
  30.4 2.7 %collective-permute-start.12 = (f32[48,128]{1,0:T(8,128)S(1)}, f32[48,128]{1,0:T(8,128)S(1)}, u32[]{:S(2)}, u32[]{:S(2)}) collective-permute-start(f32[48,128]{1,0:T(8,128)S(1)} %get-tuple-element.113), channel_id=1, source_target_pairs={{0,8},{1,9},{2,10},{3,11},{4,12},{5,13},{6,14},{7,15},{8,0},{9,1},... | collective-permute-start | bytes 73736 | tf_op jit(solution)/shard_map/ppermute | solution.py:691
  38.6 1.8 %collective-permute-start.23 = (f32[2,48,128]{2,1,0:T(8,128)S(1)}, f32[2,48,128]{2,1,0:T(8,128)S(1)}, u32[]{:S(2)}, u32[]{:S(2)}) collective-permute-start(f32[2,48,128]{2,1,0:T(8,128)S(1)} %get-tuple-element.130), channel_id=1, source_target_pairs={{0,6},{1,7},{2,4},{3,5},{4,2},{5,3},{6,0},{7,1},{8,14},{9,15},{10,... | collective-permute-start | bytes 147464 | tf_op jit(solution)/shard_map/ppermute | solution.py:688
  40.4 2.0 %collective-permute-start.18 = (f32[48,128]{1,0:T(8,128)S(1)}, f32[48,128]{1,0:T(8,128)S(1)}, u32[]{:S(2)}, u32[]{:S(2)}) collective-permute-start(f32[48,128]{1,0:T(8,128)S(1)} %get-tuple-element.124), channel_id=1, source_target_pairs={{0,8},{1,9},{2,10},{3,11},{4,12},{5,13},{6,14},{7,15},{8,0},{9,1},... | collective-permute-start | bytes 73736 | tf_op jit(solution)/shard_map/ppermute | solution.py:691
  44.7 7.7 %all_to_all.5.arrived = f32[8,8,128]{2,1,0:T(8,128)S(1)} all-to-all(f32[8,8,128]{2,1,0:T(8,128)S(1)} %get-tuple-element.136), channel_id=1, replica_groups=mesh['grp'=4,'mem'=8] {'mem'}, dimensions={0} | all-to-all | bytes 65536 | tf_op jit(solution)/shard_map/all_to_all | solution.py:805
  53.1 1.3 %collective-permute-done.26.got.refs_1_ = f32[4,56,128]{2,1,0:T(8,128)S(1)} collective-permute-done((f32[4,56,128]{2,1,0:T(8,128)S(1)}, f32[4,56,128]{2,1,0:T(8,128)S(1)}, u32[]{:S(2)}, u32[]{:S(2)}) %collective-permute-start.26) | collective-permute-done | bytes 114720 | tf_op jit(solution)/shard_map/ppermute | solution.py:688
  55.6 2.4 %collective-permute-start.29 = (f32[2,56,128]{2,1,0:T(8,128)S(1)}, f32[2,56,128]{2,1,0:T(8,128)S(1)}, u32[]{:S(2)}, u32[]{:S(2)}) collective-permute-start(f32[2,56,128]{2,1,0:T(8,128)S(1)} %get-tuple-element.150), channel_id=1, source_target_pairs={{0,6},{1,7},{2,4},{3,5},{4,2},{5,3},{6,0},{7,1},{8,14},{9,15},{10,... | collective-permute-start | bytes 172040 | tf_op jit(solution)/shard_map/ppermute | solution.py:688
  57.9 2.2 %collective-permute-start.24 = (f32[80,128]{1,0:T(8,128)S(1)}, f32[80,128]{1,0:T(8,128)S(1)}, u32[]{:S(2)}, u32[]{:S(2)}) collective-permute-start(f32[80,128]{1,0:T(8,128)S(1)} %get-tuple-element.139), channel_id=1, source_target_pairs={{0,8},{1,9},{2,10},{3,11},{4,12},{5,13},{6,14},{7,15},{8,0},{9,1},... | collective-permute-start | bytes 122888 | tf_op jit(solution)/shard_map/ppermute | solution.py:691
  60.1 2.0 %collective-permute-done.24.refs_5_.from_first = f32[80,128]{1,0:T(8,128)S(1)} collective-permute-done((f32[80,128]{1,0:T(8,128)S(1)}, f32[80,128]{1,0:T(8,128)S(1)}, u32[]{:S(2)}, u32[]{:S(2)}) %collective-permute-start.24) | collective-permute-done | bytes 40992 | tf_op jit(solution)/shard_map/ppermute | solution.py:691
  62.9 1.6 %outside.6 = (f32[6,8,4096]{2,1,0:T(8,128)S(1)}, f32[4,48,128]{2,1,0:T(8,128)S(1)}, f32[4,48,128]{2,1,0:T(8,128)S(1)}, f32[48,128]{1,0:T(8,128)S(1)}, f32[48,128]{1,0:T(8,128)S(1)}, /*index=5*/f32[3,8,4096]{2,1,0:T(8,128)S(1)}) custom-call(f32[80,128]{1,0:T(8,128)S(1)} %collective-permute-done.24.refs_5_.from_first, ...), custom_call_target="tpu_custom_call", output_to_operand_aliasing={{0}: (2, {}), {5}: (7, {})} | custom-call | flops 2000000 | bytes 2000000 | tf_op jit(solution)/shard_map/outside/pallas_call | solution.py:763
  67.0 2.4 %collective-permute-start.35 = (f32[2,48,128]{2,1,0:T(8,128)S(1)}, f32[2,48,128]{2,1,0:T(8,128)S(1)}, u32[]{:S(2)}, u32[]{:S(2)}) collective-permute-start(f32[2,48,128]{2,1,0:T(8,128)S(1)} %get-tuple-element.158), channel_id=1, source_target_pairs={{0,6},{1,7},{2,4},{3,5},{4,2},{5,3},{6,0},{7,1},{8,14},{9,15},{10,... | collective-permute-start | bytes 147464 | tf_op jit(solution)/shard_map/ppermute | solution.py:688
  69.4 2.3 %collective-permute-start.30 = (f32[48,128]{1,0:T(8,128)S(1)}, f32[48,128]{1,0:T(8,128)S(1)}, u32[]{:S(2)}, u32[]{:S(2)}) collective-permute-start(f32[48,128]{1,0:T(8,128)S(1)} %get-tuple-element.152), channel_id=1, source_target_pairs={{0,8},{1,9},{2,10},{3,11},{4,12},{5,13},{6,14},{7,15},{8,0},{9,1},... | collective-permute-start | bytes 73736 | tf_op jit(solution)/shard_map/ppermute | solution.py:691
  76.1 1.5 %collective-permute-start.38 = (f32[2,48,128]{2,1,0:T(8,128)S(1)}, f32[2,48,128]{2,1,0:T(8,128)S(1)}, u32[]{:S(2)}, u32[]{:S(2)}) collective-permute-start(f32[2,48,128]{2,1,0:T(8,128)S(1)} %get-tuple-element.169), channel_id=1, source_target_pairs={{0,4},{1,5},{2,6},{3,7},{4,0},{5,1},{6,2},{7,3},{8,12},{9,13},{10,... | collective-permute-start | bytes 147464 | tf_op jit(solution)/shard_map/ppermute | solution.py:688
  77.6 1.4 %collective-permute-start.39 = (f32[2,48,128]{2,1,0:T(8,128)S(1)}, f32[2,48,128]{2,1,0:T(8,128)S(1)}, u32[]{:S(2)}, u32[]{:S(2)}) collective-permute-start(f32[2,48,128]{2,1,0:T(8,128)S(1)} %get-tuple-element.170), channel_id=1, source_target_pairs={{0,6},{1,7},{2,4},{3,5},{4,2},{5,3},{6,0},{7,1},{8,14},{9,15},{10,... | collective-permute-start | bytes 147464 | tf_op jit(solution)/shard_map/ppermute | solution.py:688
  79.0 2.0 %collective-permute-start.40 = (f32[48,128]{1,0:T(8,128)S(1)}, f32[48,128]{1,0:T(8,128)S(1)}, u32[]{:S(2)}, u32[]{:S(2)}) collective-permute-start(f32[48,128]{1,0:T(8,128)S(1)} %get-tuple-element.171), channel_id=1, source_target_pairs={{0,8},{1,9},{2,10},{3,11},{4,12},{5,13},{6,14},{7,15},{8,0},{9,1},... | collective-permute-start | bytes 73736 | tf_op jit(solution)/shard_map/ppermute | solution.py:691
  81.0 1.4 %inside.11 = (f32[6,8,4096]{2,1,0:T(8,128)S(1)}, f32[3,8,4096]{2,1,0:T(8,128)}) custom-call(f32[6,8,4096]{2,1,0:T(8,128)S(1)} %get-tuple-element.163.refs_0_, f32[5,8,4096]{2,1,0:T(8,128)S(1)} %get-tuple-element.104.refs_1_, f32[8,4096]{1,0:T(8,128)S(1)} %get-tuple-element.105.refs_2_, ...), custom_call_target="tpu_custom_call", output_to_operand_aliasing={{0}: (0, {})} | custom-call | flops 2000000 | bytes 2000000 | tf_op jit(solution)/shard_map/inside/pallas_call | solution.py:741
  (100 shorter events, 32.7 us)
Async XLA Ops:
  5.3 8.1 %collective-permute-start.1 = (f32[2,72,128]{2,1,0:T(8,128)S(1)}, f32[2,72,128]{2,1,0:T(8,128)S(1)}, u32[]{:S(2)}, u32[]{:S(2)}) collective-permute-start(f32[2,72,128]{2,1,0:T(8,128)S(1)} %get-tuple-element.90), channel_id=1, source_target_pairs={{0,2},{1,3},{2,0},{3,1},{4,6},{5,7},{6,4},{7,5},{8,10},{9,11},{10,... | collective-permute-start | bytes 221192 | tf_op jit(solution)/shard_map/ppermute | solution.py:688
  8.2 5.2 %collective-permute-start.2 = (f32[2,72,128]{2,1,0:T(8,128)S(1)}, f32[2,72,128]{2,1,0:T(8,128)S(1)}, u32[]{:S(2)}, u32[]{:S(2)}) collective-permute-start(f32[2,72,128]{2,1,0:T(8,128)S(1)} %get-tuple-element.91), channel_id=1, source_target_pairs={{0,4},{1,5},{2,6},{3,7},{4,0},{5,1},{6,2},{7,3},{8,12},{9,13},{10,... | collective-permute-start | bytes 221192 | tf_op jit(solution)/shard_map/ppermute | solution.py:688
  9.7 5.3 %collective-permute-start.3 = (f32[2,72,128]{2,1,0:T(8,128)S(1)}, f32[2,72,128]{2,1,0:T(8,128)S(1)}, u32[]{:S(2)}, u32[]{:S(2)}) collective-permute-start(f32[2,72,128]{2,1,0:T(8,128)S(1)} %get-tuple-element.92), channel_id=1, source_target_pairs={{0,6},{1,7},{2,4},{3,5},{4,2},{5,3},{6,0},{7,1},{8,14},{9,15},{10,... | collective-permute-start | bytes 221192 | tf_op jit(solution)/shard_map/ppermute | solution.py:688
  17.2 5.9 %collective-permute-start.9 = (f32[2,48,128]{2,1,0:T(8,128)S(1)}, f32[2,48,128]{2,1,0:T(8,128)S(1)}, u32[]{:S(2)}, u32[]{:S(2)}) collective-permute-start(f32[2,48,128]{2,1,0:T(8,128)S(1)} %get-tuple-element.100), channel_id=1, source_target_pairs={{0,2},{1,3},{2,0},{3,1},{4,6},{5,7},{6,4},{7,5},{8,10},{9,11},{10,... | collective-permute-start | bytes 147464 | tf_op jit(solution)/shard_map/ppermute | solution.py:688
  17.8 5.3 %collective-permute-start.10 = (f32[2,48,128]{2,1,0:T(8,128)S(1)}, f32[2,48,128]{2,1,0:T(8,128)S(1)}, u32[]{:S(2)}, u32[]{:S(2)}) collective-permute-start(f32[2,48,128]{2,1,0:T(8,128)S(1)} %get-tuple-element.101), channel_id=1, source_target_pairs={{0,4},{1,5},{2,6},{3,7},{4,0},{5,1},{6,2},{7,3},{8,12},{9,13},{10,... | collective-permute-start | bytes 147464 | tf_op jit(solution)/shard_map/ppermute | solution.py:688
  19.2 5.0 %collective-permute-start.11 = (f32[2,48,128]{2,1,0:T(8,128)S(1)}, f32[2,48,128]{2,1,0:T(8,128)S(1)}, u32[]{:S(2)}, u32[]{:S(2)}) collective-permute-start(f32[2,48,128]{2,1,0:T(8,128)S(1)} %get-tuple-element.102), channel_id=1, source_target_pairs={{0,6},{1,7},{2,4},{3,5},{4,2},{5,3},{6,0},{7,1},{8,14},{9,15},{10,... | collective-permute-start | bytes 147464 | tf_op jit(solution)/shard_map/ppermute | solution.py:688
  26.8 6.9 %collective-permute-start.15 = (f32[2,48,128]{2,1,0:T(8,128)S(1)}, f32[2,48,128]{2,1,0:T(8,128)S(1)}, u32[]{:S(2)}, u32[]{:S(2)}) collective-permute-start(f32[2,48,128]{2,1,0:T(8,128)S(1)} %get-tuple-element.117), channel_id=1, source_target_pairs={{0,2},{1,3},{2,0},{3,1},{4,6},{5,7},{6,4},{7,5},{8,10},{9,11},{10,... | collective-permute-start | bytes 147464 | tf_op jit(solution)/shard_map/ppermute | solution.py:688
  27.7 6.0 %collective-permute-start.16 = (f32[2,48,128]{2,1,0:T(8,128)S(1)}, f32[2,48,128]{2,1,0:T(8,128)S(1)}, u32[]{:S(2)}, u32[]{:S(2)}) collective-permute-start(f32[2,48,128]{2,1,0:T(8,128)S(1)} %get-tuple-element.118), channel_id=1, source_target_pairs={{0,4},{1,5},{2,6},{3,7},{4,0},{5,1},{6,2},{7,3},{8,12},{9,13},{10,... | collective-permute-start | bytes 147464 | tf_op jit(solution)/shard_map/ppermute | solution.py:688
  29.2 5.0 %collective-permute-start.17 = (f32[2,48,128]{2,1,0:T(8,128)S(1)}, f32[2,48,128]{2,1,0:T(8,128)S(1)}, u32[]{:S(2)}, u32[]{:S(2)}) collective-permute-start(f32[2,48,128]{2,1,0:T(8,128)S(1)} %get-tuple-element.119), channel_id=1, source_target_pairs={{0,6},{1,7},{2,4},{3,5},{4,2},{5,3},{6,0},{7,1},{8,14},{9,15},{10,... | collective-permute-start | bytes 147464 | tf_op jit(solution)/shard_map/ppermute | solution.py:688
  30.4 4.5 %collective-permute-start.12 = (f32[48,128]{1,0:T(8,128)S(1)}, f32[48,128]{1,0:T(8,128)S(1)}, u32[]{:S(2)}, u32[]{:S(2)}) collective-permute-start(f32[48,128]{1,0:T(8,128)S(1)} %get-tuple-element.113), channel_id=1, source_target_pairs={{0,8},{1,9},{2,10},{3,11},{4,12},{5,13},{6,14},{7,15},{8,0},{9,1},... | collective-permute-start | bytes 73736 | tf_op jit(solution)/shard_map/ppermute | solution.py:691
  36.8 6.3 %collective-permute-start.21 = (f32[2,48,128]{2,1,0:T(8,128)S(1)}, f32[2,48,128]{2,1,0:T(8,128)S(1)}, u32[]{:S(2)}, u32[]{:S(2)}) collective-permute-start(f32[2,48,128]{2,1,0:T(8,128)S(1)} %get-tuple-element.128), channel_id=1, source_target_pairs={{0,2},{1,3},{2,0},{3,1},{4,6},{5,7},{6,4},{7,5},{8,10},{9,11},{10,... | collective-permute-start | bytes 147464 | tf_op jit(solution)/shard_map/ppermute | solution.py:688
  37.4 5.7 %collective-permute-start.22 = (f32[2,48,128]{2,1,0:T(8,128)S(1)}, f32[2,48,128]{2,1,0:T(8,128)S(1)}, u32[]{:S(2)}, u32[]{:S(2)}) collective-permute-start(f32[2,48,128]{2,1,0:T(8,128)S(1)} %get-tuple-element.129), channel_id=1, source_target_pairs={{0,4},{1,5},{2,6},{3,7},{4,0},{5,1},{6,2},{7,3},{8,12},{9,13},{10,... | collective-permute-start | bytes 147464 | tf_op jit(solution)/shard_map/ppermute | solution.py:688
  38.6 5.0 %collective-permute-start.23 = (f32[2,48,128]{2,1,0:T(8,128)S(1)}, f32[2,48,128]{2,1,0:T(8,128)S(1)}, u32[]{:S(2)}, u32[]{:S(2)}) collective-permute-start(f32[2,48,128]{2,1,0:T(8,128)S(1)} %get-tuple-element.130), channel_id=1, source_target_pairs={{0,6},{1,7},{2,4},{3,5},{4,2},{5,3},{6,0},{7,1},{8,14},{9,15},{10,... | collective-permute-start | bytes 147464 | tf_op jit(solution)/shard_map/ppermute | solution.py:688
  54.4 8.4 %collective-permute-start.27 = (f32[2,56,128]{2,1,0:T(8,128)S(1)}, f32[2,56,128]{2,1,0:T(8,128)S(1)}, u32[]{:S(2)}, u32[]{:S(2)}) collective-permute-start(f32[2,56,128]{2,1,0:T(8,128)S(1)} %get-tuple-element.148), channel_id=1, source_target_pairs={{0,2},{1,3},{2,0},{3,1},{4,6},{5,7},{6,4},{7,5},{8,10},{9,11},{10,... | collective-permute-start | bytes 172040 | tf_op jit(solution)/shard_map/ppermute | solution.py:688
  55.0 7.8 %collective-permute-start.28 = (f32[2,56,128]{2,1,0:T(8,128)S(1)}, f32[2,56,128]{2,1,0:T(8,128)S(1)}, u32[]{:S(2)}, u32[]{:S(2)}) collective-permute-start(f32[2,56,128]{2,1,0:T(8,128)S(1)} %get-tuple-element.149), channel_id=1, source_target_pairs={{0,4},{1,5},{2,6},{3,7},{4,0},{5,1},{6,2},{7,3},{8,12},{9,13},{10,... | collective-permute-start | bytes 172040 | tf_op jit(solution)/shard_map/ppermute | solution.py:688
  55.6 7.3 %collective-permute-start.29 = (f32[2,56,128]{2,1,0:T(8,128)S(1)}, f32[2,56,128]{2,1,0:T(8,128)S(1)}, u32[]{:S(2)}, u32[]{:S(2)}) collective-permute-start(f32[2,56,128]{2,1,0:T(8,128)S(1)} %get-tuple-element.150), channel_id=1, source_target_pairs={{0,6},{1,7},{2,4},{3,5},{4,2},{5,3},{6,0},{7,1},{8,14},{9,15},{10,... | collective-permute-start | bytes 172040 | tf_op jit(solution)/shard_map/ppermute | solution.py:688
  57.9 4.2 %collective-permute-start.24 = (f32[80,128]{1,0:T(8,128)S(1)}, f32[80,128]{1,0:T(8,128)S(1)}, u32[]{:S(2)}, u32[]{:S(2)}) collective-permute-start(f32[80,128]{1,0:T(8,128)S(1)} %get-tuple-element.139), channel_id=1, source_target_pairs={{0,8},{1,9},{2,10},{3,11},{4,12},{5,13},{6,14},{7,15},{8,0},{9,1},... | collective-permute-start | bytes 122888 | tf_op jit(solution)/shard_map/ppermute | solution.py:691
  65.8 6.5 %collective-permute-start.33 = (f32[2,48,128]{2,1,0:T(8,128)S(1)}, f32[2,48,128]{2,1,0:T(8,128)S(1)}, u32[]{:S(2)}, u32[]{:S(2)}) collective-permute-start(f32[2,48,128]{2,1,0:T(8,128)S(1)} %get-tuple-element.156), channel_id=1, source_target_pairs={{0,2},{1,3},{2,0},{3,1},{4,6},{5,7},{6,4},{7,5},{8,10},{9,11},{10,... | collective-permute-start | bytes 147464 | tf_op jit(solution)/shard_map/ppermute | solution.py:688
  66.4 5.9 %collective-permute-start.34 = (f32[2,48,128]{2,1,0:T(8,128)S(1)}, f32[2,48,128]{2,1,0:T(8,128)S(1)}, u32[]{:S(2)}, u32[]{:S(2)}) collective-permute-start(f32[2,48,128]{2,1,0:T(8,128)S(1)} %get-tuple-element.157), channel_id=1, source_target_pairs={{0,4},{1,5},{2,6},{3,7},{4,0},{5,1},{6,2},{7,3},{8,12},{9,13},{10,... | collective-permute-start | bytes 147464 | tf_op jit(solution)/shard_map/ppermute | solution.py:688
  67.0 5.4 %collective-permute-start.35 = (f32[2,48,128]{2,1,0:T(8,128)S(1)}, f32[2,48,128]{2,1,0:T(8,128)S(1)}, u32[]{:S(2)}, u32[]{:S(2)}) collective-permute-start(f32[2,48,128]{2,1,0:T(8,128)S(1)} %get-tuple-element.158), channel_id=1, source_target_pairs={{0,6},{1,7},{2,4},{3,5},{4,2},{5,3},{6,0},{7,1},{8,14},{9,15},{10,... | collective-permute-start | bytes 147464 | tf_op jit(solution)/shard_map/ppermute | solution.py:688
  69.4 4.1 %collective-permute-start.30 = (f32[48,128]{1,0:T(8,128)S(1)}, f32[48,128]{1,0:T(8,128)S(1)}, u32[]{:S(2)}, u32[]{:S(2)}) collective-permute-start(f32[48,128]{1,0:T(8,128)S(1)} %get-tuple-element.152), channel_id=1, source_target_pairs={{0,8},{1,9},{2,10},{3,11},{4,12},{5,13},{6,14},{7,15},{8,0},{9,1},... | collective-permute-start | bytes 73736 | tf_op jit(solution)/shard_map/ppermute | solution.py:691
  75.4 7.4 %collective-permute-start.37 = (f32[2,48,128]{2,1,0:T(8,128)S(1)}, f32[2,48,128]{2,1,0:T(8,128)S(1)}, u32[]{:S(2)}, u32[]{:S(2)}) collective-permute-start(f32[2,48,128]{2,1,0:T(8,128)S(1)} %get-tuple-element.168), channel_id=1, source_target_pairs={{0,2},{1,3},{2,0},{3,1},{4,6},{5,7},{6,4},{7,5},{8,10},{9,11},{10,... | collective-permute-start | bytes 147464 | tf_op jit(solution)/shard_map/ppermute | solution.py:688
  76.1 6.7 %collective-permute-start.38 = (f32[2,48,128]{2,1,0:T(8,128)S(1)}, f32[2,48,128]{2,1,0:T(8,128)S(1)}, u32[]{:S(2)}, u32[]{:S(2)}) collective-permute-start(f32[2,48,128]{2,1,0:T(8,128)S(1)} %get-tuple-element.169), channel_id=1, source_target_pairs={{0,4},{1,5},{2,6},{3,7},{4,0},{5,1},{6,2},{7,3},{8,12},{9,13},{10,... | collective-permute-start | bytes 147464 | tf_op jit(solution)/shard_map/ppermute | solution.py:688
  77.6 5.2 %collective-permute-start.39 = (f32[2,48,128]{2,1,0:T(8,128)S(1)}, f32[2,48,128]{2,1,0:T(8,128)S(1)}, u32[]{:S(2)}, u32[]{:S(2)}) collective-permute-start(f32[2,48,128]{2,1,0:T(8,128)S(1)} %get-tuple-element.170), channel_id=1, source_target_pairs={{0,6},{1,7},{2,4},{3,5},{4,2},{5,3},{6,0},{7,1},{8,14},{9,15},{10,... | collective-permute-start | bytes 147464 | tf_op jit(solution)/shard_map/ppermute | solution.py:688
  (23 other events, 62.0 us)

commit v5 on v4

--- a/solution.py
+++ b/solution.py
@@ -364,6 +364,10 @@
         pair[1, :, :] = got[n + 1, :, :]
 
 
+def add_kernel(mine, got, total):
+    total[...] = mine[...] + got[...]
+
+
 def inside_kernel(first_step, lifted, final, members, *refs):
     refs = list(refs)
     state, wi, diagonal = refs[:3]
@@ -523,12 +527,11 @@
     out = jnp.zeros((BLK, LANES), F32)
     for t in range(wide):
         out = jnp.where(sub == t, jnp.sum(rows[t], axis=0, keepdims=True), out)
-    for n in range(members):
-        payload[n, :, :] = out
+    payload[...] = out
 
 
 def lift_kernel(
-    members, cap, arrived, state, eff, inverse, gk, gj, gi, tables, chosen, x,
+    members, cap, parts, state, eff, inverse, gk, gj, gi, tables, chosen, x,
     out, lift, unknowns, mine, other, first, second, same_x,
 ):
     lane, sub = lane_id(), sub_id()
@@ -536,9 +539,9 @@
     table = Table(tables)
     wide = -(-members * BLK * 3 // LANES)
     member = lax.axis_index("mem")
-    total = arrived[0, :, :]
-    for n in range(1, members):
-        total = total + arrived[n, :, :]
+    total = parts[0][...]
+    for part in parts[1:]:
+        total = total + part[...]
     unknowns[...] = total
     known = rows_of(total, wide)
     own = look_up(known, member * BLK + sub, lane)
@@ -699,6 +702,7 @@
 
     per = 9 * BLK
     half = array(members // 2, per, LANES)
+    solver_rows = jnp.pad(coarse_solver[0], ((0, 0), (0, -coarse_solver.shape[2] % LANES)))
     eff = viscosity * jnp.exp2(-refinement.astype(F32))[:, None]
     mine, other, first, second, tables = call(
         functools.partial(prepare_kernel, members, groups, cap),
@@ -712,7 +716,7 @@
         ],
         "prepare",
         moved=0,
-    )(eff, face_owner.T, face_block.T, plane_block.T, hanging, jnp.pad(coarse_solver[0], ((0, 0), (0, -coarse_solver.shape[2] % LANES))))
+    )(eff, face_owner.T, face_block.T, plane_block.T, hanging, solver_rows)
     near, from_first, from_second = spread(mine, other, first, second)
 
     half = array(members // 2, 6 * cap, LANES)
@@ -796,23 +800,24 @@
     state, payload, x = call(
         functools.partial(coarse_kernel, members, cap),
         [VMEM] * 6 + [ANY],
-        [states, array(members, BLK, LANES), field],
+        [states, array(BLK, LANES), field],
         [VMEM, VMEM, ANY],
         ghost_scratch,
         "coarse",
         {2: 0, 6: 2},
     )(from_first, from_second, state, gi, tables, coarse, x)
-    sums = lax.all_to_all(payload, "mem", split_axis=0, concat_axis=0, tiled=True)
+    pair = call(add_kernel, [VMEM] * 2, [array(BLK, LANES)], [VMEM], [], "add")(payload, swap(payload, 1))[0]
+    parts = [pair] + [swap(pair, 2 * n) for n in range(1, members // 2)]
     half = array(members // 2, 6 * cap + BLK, LANES)
     state, lift, unknowns, *sent, x = call(
-        functools.partial(lift_kernel, members, cap),
-        [VMEM] * 9 + [ANY],
+        lambda *refs: lift_kernel(members, cap, refs[: len(parts)], *refs[len(parts) :]),
+        [VMEM] * (len(parts) + 8) + [ANY],
         [states, array(3 * BLK, LANES), array(BLK, LANES), half, half, array(80, LANES), array(80, LANES), field],
         [VMEM] * 7 + [ANY],
         [],
         "lift",
-        {1: 0, 9: 7},
-    )(sums, state, eff, inverse, gk, gj, gi, tables, chosen, x)
+        {len(parts): 0, len(parts) + 8: 7},
+    )(*parts, state, eff, inverse, gk, gj, gi, tables, chosen, x)
     state, x, (near, from_first, from_second) = steps(state, sent, x, lift, unknowns)
     state, velocity = inside(state, x, final=True)
     residual = call(

time: 84.5 us -> 84.1 us (level)
  blocking collectives: 7.71 us -> 0 us
  starting transfers between devices: 41.7 us -> 45.6 us
  waiting for transfers between devices: 16.8 us -> 20.4 us
    all_to_all x1 -> x0, blocking collectives: 7.71 us -> none  [local(): lax.all_to_all(payload, 'mem', split_axis=0, concat_axis=0, tiled=True)]
    ppermute x28 -> x32, waiting for transfers between devices: 12.3 us -> 16.3 us  [swap(): return lax.ppermute(a, 'mem', [(m, m ^ bits) for m in range(members)])]
    ppermute x28 -> x32, starting transfers between devices: 26.8 us -> 30.4 us  [swap(): return lax.ppermute(a, 'mem', [(m, m ^ bits) for m in range(members)])]
  transfers between devices with their start and end apart: 42 -> 46, of which waited for: 15 -> 19; matrix products, arithmetic and copies ran while one was open for 0% -> 0% of each run, Pallas kernels for 9% -> 9%
where the time goes in v5:
time: 84.1 us; the launch traced here: 83.9 us
  starting transfers between devices  45.6 us (54%)
  waiting for transfers between devices  20.4 us (24%)
  Pallas kernels  14.3 us (17%)
  other arithmetic  1.67 us (2%)
  between operations  1.05 us (1%)
    ppermute x32, starting transfers between devices, swap(): return lax.ppermute(a, 'mem', [(m, m ^ bits) for m in range(members)])  30.4 us
    ppermute x32, waiting for transfers between devices, swap(): return lax.ppermute(a, 'mem', [(m, m ^ bits) for m in range(members)])  16.3 us
    ppermute x7, starting transfers between devices, spread(): first = lax.ppermute(first, ('grp', 'mem'), first_route)  15.2 us
    pallas_call x6, Pallas kernels, inside(): call(functools.partial(inside_kernel, x is None, bool(lift), final, membe...  4.77 us
    ppermute x7, waiting for transfers between devices, spread(): first = lax.ppermute(first, ('grp', 'mem'), first_route)  4.08 us
    pallas_call x4, Pallas kernels, outside(): call(functools.partial(outside_kernel, members, cap, old, new), [VMEM] *...  3.3 us
    pallas_call x4, Pallas kernels, side(): call(gathered(side_kernel, members, cap), [VMEM] * (near_refs + 4), [stat...  2.45 us
  transfers between devices with their start and end apart: 46, of which 19 were waited for; matrix products, arithmetic and copies ran while one was open for 0% of the time, Pallas kernels for 9%

profile of v5, /device:TPU:0, one launch (start us, length us, event | category | flops | bytes accessed | tf_op | source)
XLA Modules:
  0.0 83.9 jit_solution(12255859826434387436)
XLA Ops:
  5.3 2.9 %collective-permute-start.1 = (f32[2,72,128]{2,1,0:T(8,128)S(1)}, f32[2,72,128]{2,1,0:T(8,128)S(1)}, u32[]{:S(2)}, u32[]{:S(2)}) collective-permute-start(f32[2,72,128]{2,1,0:T(8,128)S(1)} %get-tuple-element.90), channel_id=1, source_target_pairs={{0,2},{1,3},{2,0},{3,1},{4,6},{5,7},{6,4},{7,5},{8,10},{9,11},{10,... | collective-permute-start | bytes 221192 | tf_op jit(solution)/shard_map/ppermute | solution.py:691
  8.2 1.5 %collective-permute-start.2 = (f32[2,72,128]{2,1,0:T(8,128)S(1)}, f32[2,72,128]{2,1,0:T(8,128)S(1)}, u32[]{:S(2)}, u32[]{:S(2)}) collective-permute-start(f32[2,72,128]{2,1,0:T(8,128)S(1)} %get-tuple-element.91), channel_id=1, source_target_pairs={{0,4},{1,5},{2,6},{3,7},{4,0},{5,1},{6,2},{7,3},{8,12},{9,13},{10,... | collective-permute-start | bytes 221192 | tf_op jit(solution)/shard_map/ppermute | solution.py:691
  9.7 2.0 %collective-permute-start.4 = (f32[16,128]{1,0:T(8,128)S(1)}, f32[16,128]{1,0:T(8,128)S(1)}, u32[]{:S(2)}, u32[]{:S(2)}) collective-permute-start(f32[16,128]{1,0:T(8,128)S(1)} %get-tuple-element.93), channel_id=1, source_target_pairs={{0,8},{1,9},{2,10},{3,11},{4,12},{5,13},{6,14},{7,15},{8,0},{9,1},... | collective-permute-start | bytes 24584 | tf_op jit(solution)/shard_map/ppermute | solution.py:694
  11.7 1.6 %collective-permute-done.4.refs_5_ = f32[16,128]{1,0:T(8,128)S(1)} collective-permute-done((f32[16,128]{1,0:T(8,128)S(1)}, f32[16,128]{1,0:T(8,128)S(1)}, u32[]{:S(2)}, u32[]{:S(2)}) %collective-permute-start.4) | collective-permute-done | bytes 8224 | tf_op jit(solution)/shard_map/ppermute | solution.py:694
  13.4 1.6 %collective-permute-done.3.refs_4_ = f32[2,72,128]{2,1,0:T(8,128)S(1)} collective-permute-done((f32[2,72,128]{2,1,0:T(8,128)S(1)}, f32[2,72,128]{2,1,0:T(8,128)S(1)}, u32[]{:S(2)}, u32[]{:S(2)}) %collective-permute-start.3) | collective-permute-done | bytes 73760 | tf_op jit(solution)/shard_map/ppermute | solution.py:691
  17.8 1.4 %collective-permute-start.10 = (f32[2,48,128]{2,1,0:T(8,128)S(1)}, f32[2,48,128]{2,1,0:T(8,128)S(1)}, u32[]{:S(2)}, u32[]{:S(2)}) collective-permute-start(f32[2,48,128]{2,1,0:T(8,128)S(1)} %get-tuple-element.101), channel_id=1, source_target_pairs={{0,4},{1,5},{2,6},{3,7},{4,0},{5,1},{6,2},{7,3},{8,12},{9,13},{10,... | collective-permute-start | bytes 147464 | tf_op jit(solution)/shard_map/ppermute | solution.py:691
  19.2 1.6 %collective-permute-start.11 = (f32[2,48,128]{2,1,0:T(8,128)S(1)}, f32[2,48,128]{2,1,0:T(8,128)S(1)}, u32[]{:S(2)}, u32[]{:S(2)}) collective-permute-start(f32[2,48,128]{2,1,0:T(8,128)S(1)} %get-tuple-element.102), channel_id=1, source_target_pairs={{0,6},{1,7},{2,4},{3,5},{4,2},{5,3},{6,0},{7,1},{8,14},{9,15},{10,... | collective-permute-start | bytes 147464 | tf_op jit(solution)/shard_map/ppermute | solution.py:691
  20.8 1.6 %collective-permute-start.6 = (f32[48,128]{1,0:T(8,128)S(1)}, f32[48,128]{1,0:T(8,128)S(1)}, u32[]{:S(2)}, u32[]{:S(2)}) collective-permute-start(f32[48,128]{1,0:T(8,128)S(1)} %get-tuple-element.96), channel_id=1, source_target_pairs={{0,8},{1,9},{2,10},{3,11},{4,12},{5,13},{6,14},{7,15},{8,0},{9,1},... | collective-permute-start | bytes 73736 | tf_op jit(solution)/shard_map/ppermute | solution.py:694
  27.7 1.5 %collective-permute-start.16 = (f32[2,48,128]{2,1,0:T(8,128)S(1)}, f32[2,48,128]{2,1,0:T(8,128)S(1)}, u32[]{:S(2)}, u32[]{:S(2)}) collective-permute-start(f32[2,48,128]{2,1,0:T(8,128)S(1)} %get-tuple-element.118), channel_id=1, source_target_pairs={{0,4},{1,5},{2,6},{3,7},{4,0},{5,1},{6,2},{7,3},{8,12},{9,13},{10,... | collective-permute-start | bytes 147464 | tf_op jit(solution)/shard_map/ppermute | solution.py:691
  30.4 2.7 %collective-permute-start.12 = (f32[48,128]{1,0:T(8,128)S(1)}, f32[48,128]{1,0:T(8,128)S(1)}, u32[]{:S(2)}, u32[]{:S(2)}) collective-permute-start(f32[48,128]{1,0:T(8,128)S(1)} %get-tuple-element.113), channel_id=1, source_target_pairs={{0,8},{1,9},{2,10},{3,11},{4,12},{5,13},{6,14},{7,15},{8,0},{9,1},... | collective-permute-start | bytes 73736 | tf_op jit(solution)/shard_map/ppermute | solution.py:694
  38.6 1.8 %collective-permute-start.23 = (f32[2,48,128]{2,1,0:T(8,128)S(1)}, f32[2,48,128]{2,1,0:T(8,128)S(1)}, u32[]{:S(2)}, u32[]{:S(2)}) collective-permute-start(f32[2,48,128]{2,1,0:T(8,128)S(1)} %get-tuple-element.130), channel_id=1, source_target_pairs={{0,6},{1,7},{2,4},{3,5},{4,2},{5,3},{6,0},{7,1},{8,14},{9,15},{10,... | collective-permute-start | bytes 147464 | tf_op jit(solution)/shard_map/ppermute | solution.py:691
  40.4 2.0 %collective-permute-start.18 = (f32[48,128]{1,0:T(8,128)S(1)}, f32[48,128]{1,0:T(8,128)S(1)}, u32[]{:S(2)}, u32[]{:S(2)}) collective-permute-start(f32[48,128]{1,0:T(8,128)S(1)} %get-tuple-element.124), channel_id=1, source_target_pairs={{0,8},{1,9},{2,10},{3,11},{4,12},{5,13},{6,14},{7,15},{8,0},{9,1},... | collective-permute-start | bytes 73736 | tf_op jit(solution)/shard_map/ppermute | solution.py:694
  45.9 1.8 %collective-permute-start.27 = (f32[8,128]{1,0:T(8,128)S(1)}, f32[8,128]{1,0:T(8,128)S(1)}, u32[]{:S(2)}, u32[]{:S(2)}) collective-permute-start(f32[8,128]{1,0:T(8,128)S(1)} %add.3.refs_0_), channel_id=1, source_target_pairs={{0,6},{1,7},{2,4},{3,5},{4,2},{5,3},{6,0},{7,1},{8,14},{9,15},{10,... | collective-permute-start | bytes 12296 | tf_op jit(solution)/shard_map/ppermute | solution.py:691
  52.5 1.3 %collective-permute-done.30.got.refs_1_ = f32[4,56,128]{2,1,0:T(8,128)S(1)} collective-permute-done((f32[4,56,128]{2,1,0:T(8,128)S(1)}, f32[4,56,128]{2,1,0:T(8,128)S(1)}, u32[]{:S(2)}, u32[]{:S(2)}) %collective-permute-start.30) | collective-permute-done | bytes 114720 | tf_op jit(solution)/shard_map/ppermute | solution.py:691
  55.9 1.4 %collective-permute-start.33 = (f32[2,56,128]{2,1,0:T(8,128)S(1)}, f32[2,56,128]{2,1,0:T(8,128)S(1)}, u32[]{:S(2)}, u32[]{:S(2)}) collective-permute-start(f32[2,56,128]{2,1,0:T(8,128)S(1)} %get-tuple-element.150), channel_id=1, source_target_pairs={{0,6},{1,7},{2,4},{3,5},{4,2},{5,3},{6,0},{7,1},{8,14},{9,15},{10,... | collective-permute-start | bytes 172040 | tf_op jit(solution)/shard_map/ppermute | solution.py:691
  57.4 2.4 %collective-permute-start.28 = (f32[80,128]{1,0:T(8,128)S(1)}, f32[80,128]{1,0:T(8,128)S(1)}, u32[]{:S(2)}, u32[]{:S(2)}) collective-permute-start(f32[80,128]{1,0:T(8,128)S(1)} %get-tuple-element.139), channel_id=1, source_target_pairs={{0,8},{1,9},{2,10},{3,11},{4,12},{5,13},{6,14},{7,15},{8,0},{9,1},... | collective-permute-start | bytes 122888 | tf_op jit(solution)/shard_map/ppermute | solution.py:694
  59.8 2.0 %collective-permute-done.28.refs_5_.from_first = f32[80,128]{1,0:T(8,128)S(1)} collective-permute-done((f32[80,128]{1,0:T(8,128)S(1)}, f32[80,128]{1,0:T(8,128)S(1)}, u32[]{:S(2)}, u32[]{:S(2)}) %collective-permute-start.28) | collective-permute-done | bytes 40992 | tf_op jit(solution)/shard_map/ppermute | solution.py:694
  62.5 1.6 %outside.6 = (f32[6,8,4096]{2,1,0:T(8,128)S(1)}, f32[4,48,128]{2,1,0:T(8,128)S(1)}, f32[4,48,128]{2,1,0:T(8,128)S(1)}, f32[48,128]{1,0:T(8,128)S(1)}, f32[48,128]{1,0:T(8,128)S(1)}, /*index=5*/f32[3,8,4096]{2,1,0:T(8,128)S(1)}) custom-call(f32[80,128]{1,0:T(8,128)S(1)} %collective-permute-done.28.refs_5_.from_first, ...), custom_call_target="tpu_custom_call", output_to_operand_aliasing={{0}: (2, {}), {5}: (7, {})} | custom-call | flops 2000000 | bytes 2000000 | tf_op jit(solution)/shard_map/outside/pallas_call | solution.py:767
  65.4 1.6 %collective-permute-start.37 = (f32[2,48,128]{2,1,0:T(8,128)S(1)}, f32[2,48,128]{2,1,0:T(8,128)S(1)}, u32[]{:S(2)}, u32[]{:S(2)}) collective-permute-start(f32[2,48,128]{2,1,0:T(8,128)S(1)} %get-tuple-element.156), channel_id=1, source_target_pairs={{0,2},{1,3},{2,0},{3,1},{4,6},{5,7},{6,4},{7,5},{8,10},{9,11},{10,... | collective-permute-start | bytes 147464 | tf_op jit(solution)/shard_map/ppermute | solution.py:691
  67.5 1.5 %collective-permute-start.39 = (f32[2,48,128]{2,1,0:T(8,128)S(1)}, f32[2,48,128]{2,1,0:T(8,128)S(1)}, u32[]{:S(2)}, u32[]{:S(2)}) collective-permute-start(f32[2,48,128]{2,1,0:T(8,128)S(1)} %get-tuple-element.158), channel_id=1, source_target_pairs={{0,6},{1,7},{2,4},{3,5},{4,2},{5,3},{6,0},{7,1},{8,14},{9,15},{10,... | collective-permute-start | bytes 147464 | tf_op jit(solution)/shard_map/ppermute | solution.py:691
  69.0 2.3 %collective-permute-start.34 = (f32[48,128]{1,0:T(8,128)S(1)}, f32[48,128]{1,0:T(8,128)S(1)}, u32[]{:S(2)}, u32[]{:S(2)}) collective-permute-start(f32[48,128]{1,0:T(8,128)S(1)} %get-tuple-element.152), channel_id=1, source_target_pairs={{0,8},{1,9},{2,10},{3,11},{4,12},{5,13},{6,14},{7,15},{8,0},{9,1},... | collective-permute-start | bytes 73736 | tf_op jit(solution)/shard_map/ppermute | solution.py:694
  77.2 1.4 %collective-permute-start.43 = (f32[2,48,128]{2,1,0:T(8,128)S(1)}, f32[2,48,128]{2,1,0:T(8,128)S(1)}, u32[]{:S(2)}, u32[]{:S(2)}) collective-permute-start(f32[2,48,128]{2,1,0:T(8,128)S(1)} %get-tuple-element.170), channel_id=1, source_target_pairs={{0,6},{1,7},{2,4},{3,5},{4,2},{5,3},{6,0},{7,1},{8,14},{9,15},{10,... | collective-permute-start | bytes 147464 | tf_op jit(solution)/shard_map/ppermute | solution.py:691
  78.7 2.2 %collective-permute-start.44 = (f32[48,128]{1,0:T(8,128)S(1)}, f32[48,128]{1,0:T(8,128)S(1)}, u32[]{:S(2)}, u32[]{:S(2)}) collective-permute-start(f32[48,128]{1,0:T(8,128)S(1)} %get-tuple-element.171), channel_id=1, source_target_pairs={{0,8},{1,9},{2,10},{3,11},{4,12},{5,13},{6,14},{7,15},{8,0},{9,1},... | collective-permute-start | bytes 73736 | tf_op jit(solution)/shard_map/ppermute | solution.py:694
  80.8 1.4 %inside.11 = (f32[6,8,4096]{2,1,0:T(8,128)S(1)}, f32[3,8,4096]{2,1,0:T(8,128)}) custom-call(f32[6,8,4096]{2,1,0:T(8,128)S(1)} %get-tuple-element.163.refs_0_, f32[5,8,4096]{2,1,0:T(8,128)S(1)} %get-tuple-element.104.refs_1_, f32[8,4096]{1,0:T(8,128)S(1)} %get-tuple-element.105.refs_2_, ...), custom_call_target="tpu_custom_call", output_to_operand_aliasing={{0}: (0, {})} | custom-call | flops 2000000 | bytes 2000000 | tf_op jit(solution)/shard_map/inside/pallas_call | solution.py:745
  (108 shorter events, 39.8 us)
Async XLA Ops:
  5.3 8.1 %collective-permute-start.1 = (f32[2,72,128]{2,1,0:T(8,128)S(1)}, f32[2,72,128]{2,1,0:T(8,128)S(1)}, u32[]{:S(2)}, u32[]{:S(2)}) collective-permute-start(f32[2,72,128]{2,1,0:T(8,128)S(1)} %get-tuple-element.90), channel_id=1, source_target_pairs={{0,2},{1,3},{2,0},{3,1},{4,6},{5,7},{6,4},{7,5},{8,10},{9,11},{10,... | collective-permute-start | bytes 221192 | tf_op jit(solution)/shard_map/ppermute | solution.py:691
  8.2 5.2 %collective-permute-start.2 = (f32[2,72,128]{2,1,0:T(8,128)S(1)}, f32[2,72,128]{2,1,0:T(8,128)S(1)}, u32[]{:S(2)}, u32[]{:S(2)}) collective-permute-start(f32[2,72,128]{2,1,0:T(8,128)S(1)} %get-tuple-element.91), channel_id=1, source_target_pairs={{0,4},{1,5},{2,6},{3,7},{4,0},{5,1},{6,2},{7,3},{8,12},{9,13},{10,... | collective-permute-start | bytes 221192 | tf_op jit(solution)/shard_map/ppermute | solution.py:691
  9.7 5.3 %collective-permute-start.3 = (f32[2,72,128]{2,1,0:T(8,128)S(1)}, f32[2,72,128]{2,1,0:T(8,128)S(1)}, u32[]{:S(2)}, u32[]{:S(2)}) collective-permute-start(f32[2,72,128]{2,1,0:T(8,128)S(1)} %get-tuple-element.92), channel_id=1, source_target_pairs={{0,6},{1,7},{2,4},{3,5},{4,2},{5,3},{6,0},{7,1},{8,14},{9,15},{10,... | collective-permute-start | bytes 221192 | tf_op jit(solution)/shard_map/ppermute | solution.py:691
  17.2 5.9 %collective-permute-start.9 = (f32[2,48,128]{2,1,0:T(8,128)S(1)}, f32[2,48,128]{2,1,0:T(8,128)S(1)}, u32[]{:S(2)}, u32[]{:S(2)}) collective-permute-start(f32[2,48,128]{2,1,0:T(8,128)S(1)} %get-tuple-element.100), channel_id=1, source_target_pairs={{0,2},{1,3},{2,0},{3,1},{4,6},{5,7},{6,4},{7,5},{8,10},{9,11},{10,... | collective-permute-start | bytes 147464 | tf_op jit(solution)/shard_map/ppermute | solution.py:691
  17.8 5.3 %collective-permute-start.10 = (f32[2,48,128]{2,1,0:T(8,128)S(1)}, f32[2,48,128]{2,1,0:T(8,128)S(1)}, u32[]{:S(2)}, u32[]{:S(2)}) collective-permute-start(f32[2,48,128]{2,1,0:T(8,128)S(1)} %get-tuple-element.101), channel_id=1, source_target_pairs={{0,4},{1,5},{2,6},{3,7},{4,0},{5,1},{6,2},{7,3},{8,12},{9,13},{10,... | collective-permute-start | bytes 147464 | tf_op jit(solution)/shard_map/ppermute | solution.py:691
  19.2 5.0 %collective-permute-start.11 = (f32[2,48,128]{2,1,0:T(8,128)S(1)}, f32[2,48,128]{2,1,0:T(8,128)S(1)}, u32[]{:S(2)}, u32[]{:S(2)}) collective-permute-start(f32[2,48,128]{2,1,0:T(8,128)S(1)} %get-tuple-element.102), channel_id=1, source_target_pairs={{0,6},{1,7},{2,4},{3,5},{4,2},{5,3},{6,0},{7,1},{8,14},{9,15},{10,... | collective-permute-start | bytes 147464 | tf_op jit(solution)/shard_map/ppermute | solution.py:691
  26.8 6.9 %collective-permute-start.15 = (f32[2,48,128]{2,1,0:T(8,128)S(1)}, f32[2,48,128]{2,1,0:T(8,128)S(1)}, u32[]{:S(2)}, u32[]{:S(2)}) collective-permute-start(f32[2,48,128]{2,1,0:T(8,128)S(1)} %get-tuple-element.117), channel_id=1, source_target_pairs={{0,2},{1,3},{2,0},{3,1},{4,6},{5,7},{6,4},{7,5},{8,10},{9,11},{10,... | collective-permute-start | bytes 147464 | tf_op jit(solution)/shard_map/ppermute | solution.py:691
  27.7 6.0 %collective-permute-start.16 = (f32[2,48,128]{2,1,0:T(8,128)S(1)}, f32[2,48,128]{2,1,0:T(8,128)S(1)}, u32[]{:S(2)}, u32[]{:S(2)}) collective-permute-start(f32[2,48,128]{2,1,0:T(8,128)S(1)} %get-tuple-element.118), channel_id=1, source_target_pairs={{0,4},{1,5},{2,6},{3,7},{4,0},{5,1},{6,2},{7,3},{8,12},{9,13},{10,... | collective-permute-start | bytes 147464 | tf_op jit(solution)/shard_map/ppermute | solution.py:691
  29.2 5.0 %collective-permute-start.17 = (f32[2,48,128]{2,1,0:T(8,128)S(1)}, f32[2,48,128]{2,1,0:T(8,128)S(1)}, u32[]{:S(2)}, u32[]{:S(2)}) collective-permute-start(f32[2,48,128]{2,1,0:T(8,128)S(1)} %get-tuple-element.119), channel_id=1, source_target_pairs={{0,6},{1,7},{2,4},{3,5},{4,2},{5,3},{6,0},{7,1},{8,14},{9,15},{10,... | collective-permute-start | bytes 147464 | tf_op jit(solution)/shard_map/ppermute | solution.py:691
  30.4 4.5 %collective-permute-start.12 = (f32[48,128]{1,0:T(8,128)S(1)}, f32[48,128]{1,0:T(8,128)S(1)}, u32[]{:S(2)}, u32[]{:S(2)}) collective-permute-start(f32[48,128]{1,0:T(8,128)S(1)} %get-tuple-element.113), channel_id=1, source_target_pairs={{0,8},{1,9},{2,10},{3,11},{4,12},{5,13},{6,14},{7,15},{8,0},{9,1},... | collective-permute-start | bytes 73736 | tf_op jit(solution)/shard_map/ppermute | solution.py:694
  36.8 6.3 %collective-permute-start.21 = (f32[2,48,128]{2,1,0:T(8,128)S(1)}, f32[2,48,128]{2,1,0:T(8,128)S(1)}, u32[]{:S(2)}, u32[]{:S(2)}) collective-permute-start(f32[2,48,128]{2,1,0:T(8,128)S(1)} %get-tuple-element.128), channel_id=1, source_target_pairs={{0,2},{1,3},{2,0},{3,1},{4,6},{5,7},{6,4},{7,5},{8,10},{9,11},{10,... | collective-permute-start | bytes 147464 | tf_op jit(solution)/shard_map/ppermute | solution.py:691
  37.4 5.7 %collective-permute-start.22 = (f32[2,48,128]{2,1,0:T(8,128)S(1)}, f32[2,48,128]{2,1,0:T(8,128)S(1)}, u32[]{:S(2)}, u32[]{:S(2)}) collective-permute-start(f32[2,48,128]{2,1,0:T(8,128)S(1)} %get-tuple-element.129), channel_id=1, source_target_pairs={{0,4},{1,5},{2,6},{3,7},{4,0},{5,1},{6,2},{7,3},{8,12},{9,13},{10,... | collective-permute-start | bytes 147464 | tf_op jit(solution)/shard_map/ppermute | solution.py:691
  38.6 5.0 %collective-permute-start.23 = (f32[2,48,128]{2,1,0:T(8,128)S(1)}, f32[2,48,128]{2,1,0:T(8,128)S(1)}, u32[]{:S(2)}, u32[]{:S(2)}) collective-permute-start(f32[2,48,128]{2,1,0:T(8,128)S(1)} %get-tuple-element.130), channel_id=1, source_target_pairs={{0,6},{1,7},{2,4},{3,5},{4,2},{5,3},{6,0},{7,1},{8,14},{9,15},{10,... | collective-permute-start | bytes 147464 | tf_op jit(solution)/shard_map/ppermute | solution.py:691
  45.9 4.5 %collective-permute-start.27 = (f32[8,128]{1,0:T(8,128)S(1)}, f32[8,128]{1,0:T(8,128)S(1)}, u32[]{:S(2)}, u32[]{:S(2)}) collective-permute-start(f32[8,128]{1,0:T(8,128)S(1)} %add.3.refs_0_), channel_id=1, source_target_pairs={{0,6},{1,7},{2,4},{3,5},{4,2},{5,3},{6,0},{7,1},{8,14},{9,15},{10,... | collective-permute-start | bytes 12296 | tf_op jit(solution)/shard_map/ppermute | solution.py:691
  53.8 8.6 %collective-permute-start.31 = (f32[2,56,128]{2,1,0:T(8,128)S(1)}, f32[2,56,128]{2,1,0:T(8,128)S(1)}, u32[]{:S(2)}, u32[]{:S(2)}) collective-permute-start(f32[2,56,128]{2,1,0:T(8,128)S(1)} %get-tuple-element.148), channel_id=1, source_target_pairs={{0,2},{1,3},{2,0},{3,1},{4,6},{5,7},{6,4},{7,5},{8,10},{9,11},{10,... | collective-permute-start | bytes 172040 | tf_op jit(solution)/shard_map/ppermute | solution.py:691
  55.1 7.4 %collective-permute-start.32 = (f32[2,56,128]{2,1,0:T(8,128)S(1)}, f32[2,56,128]{2,1,0:T(8,128)S(1)}, u32[]{:S(2)}, u32[]{:S(2)}) collective-permute-start(f32[2,56,128]{2,1,0:T(8,128)S(1)} %get-tuple-element.149), channel_id=1, source_target_pairs={{0,4},{1,5},{2,6},{3,7},{4,0},{5,1},{6,2},{7,3},{8,12},{9,13},{10,... | collective-permute-start | bytes 172040 | tf_op jit(solution)/shard_map/ppermute | solution.py:691
  55.9 6.5 %collective-permute-start.33 = (f32[2,56,128]{2,1,0:T(8,128)S(1)}, f32[2,56,128]{2,1,0:T(8,128)S(1)}, u32[]{:S(2)}, u32[]{:S(2)}) collective-permute-start(f32[2,56,128]{2,1,0:T(8,128)S(1)} %get-tuple-element.150), channel_id=1, source_target_pairs={{0,6},{1,7},{2,4},{3,5},{4,2},{5,3},{6,0},{7,1},{8,14},{9,15},{10,... | collective-permute-start | bytes 172040 | tf_op jit(solution)/shard_map/ppermute | solution.py:691
  57.4 4.4 %collective-permute-start.28 = (f32[80,128]{1,0:T(8,128)S(1)}, f32[80,128]{1,0:T(8,128)S(1)}, u32[]{:S(2)}, u32[]{:S(2)}) collective-permute-start(f32[80,128]{1,0:T(8,128)S(1)} %get-tuple-element.139), channel_id=1, source_target_pairs={{0,8},{1,9},{2,10},{3,11},{4,12},{5,13},{6,14},{7,15},{8,0},{9,1},... | collective-permute-start | bytes 122888 | tf_op jit(solution)/shard_map/ppermute | solution.py:694
  65.4 6.5 %collective-permute-start.37 = (f32[2,48,128]{2,1,0:T(8,128)S(1)}, f32[2,48,128]{2,1,0:T(8,128)S(1)}, u32[]{:S(2)}, u32[]{:S(2)}) collective-permute-start(f32[2,48,128]{2,1,0:T(8,128)S(1)} %get-tuple-element.156), channel_id=1, source_target_pairs={{0,2},{1,3},{2,0},{3,1},{4,6},{5,7},{6,4},{7,5},{8,10},{9,11},{10,... | collective-permute-start | bytes 147464 | tf_op jit(solution)/shard_map/ppermute | solution.py:691
  67.0 5.0 %collective-permute-start.38 = (f32[2,48,128]{2,1,0:T(8,128)S(1)}, f32[2,48,128]{2,1,0:T(8,128)S(1)}, u32[]{:S(2)}, u32[]{:S(2)}) collective-permute-start(f32[2,48,128]{2,1,0:T(8,128)S(1)} %get-tuple-element.157), channel_id=1, source_target_pairs={{0,4},{1,5},{2,6},{3,7},{4,0},{5,1},{6,2},{7,3},{8,12},{9,13},{10,... | collective-permute-start | bytes 147464 | tf_op jit(solution)/shard_map/ppermute | solution.py:691
  67.5 5.0 %collective-permute-start.39 = (f32[2,48,128]{2,1,0:T(8,128)S(1)}, f32[2,48,128]{2,1,0:T(8,128)S(1)}, u32[]{:S(2)}, u32[]{:S(2)}) collective-permute-start(f32[2,48,128]{2,1,0:T(8,128)S(1)} %get-tuple-element.158), channel_id=1, source_target_pairs={{0,6},{1,7},{2,4},{3,5},{4,2},{5,3},{6,0},{7,1},{8,14},{9,15},{10,... | collective-permute-start | bytes 147464 | tf_op jit(solution)/shard_map/ppermute | solution.py:691
  75.1 7.5 %collective-permute-start.41 = (f32[2,48,128]{2,1,0:T(8,128)S(1)}, f32[2,48,128]{2,1,0:T(8,128)S(1)}, u32[]{:S(2)}, u32[]{:S(2)}) collective-permute-start(f32[2,48,128]{2,1,0:T(8,128)S(1)} %get-tuple-element.168), channel_id=1, source_target_pairs={{0,2},{1,3},{2,0},{3,1},{4,6},{5,7},{6,4},{7,5},{8,10},{9,11},{10,... | collective-permute-start | bytes 147464 | tf_op jit(solution)/shard_map/ppermute | solution.py:691
  76.4 6.3 %collective-permute-start.42 = (f32[2,48,128]{2,1,0:T(8,128)S(1)}, f32[2,48,128]{2,1,0:T(8,128)S(1)}, u32[]{:S(2)}, u32[]{:S(2)}) collective-permute-start(f32[2,48,128]{2,1,0:T(8,128)S(1)} %get-tuple-element.169), channel_id=1, source_target_pairs={{0,4},{1,5},{2,6},{3,7},{4,0},{5,1},{6,2},{7,3},{8,12},{9,13},{10,... | collective-permute-start | bytes 147464 | tf_op jit(solution)/shard_map/ppermute | solution.py:691
  77.2 5.4 %collective-permute-start.43 = (f32[2,48,128]{2,1,0:T(8,128)S(1)}, f32[2,48,128]{2,1,0:T(8,128)S(1)}, u32[]{:S(2)}, u32[]{:S(2)}) collective-permute-start(f32[2,48,128]{2,1,0:T(8,128)S(1)} %get-tuple-element.170), channel_id=1, source_target_pairs={{0,6},{1,7},{2,4},{3,5},{4,2},{5,3},{6,0},{7,1},{8,14},{9,15},{10,... | collective-permute-start | bytes 147464 | tf_op jit(solution)/shard_map/ppermute | solution.py:691
  (27 other events, 74.8 us)

commit v6 on v5

--- a/solution.py
+++ b/solution.py
@@ -481,17 +481,18 @@
 
 
 def last_kernel(
-    members, cap, near, from_first, from_second, state, gk, gj, gi, tables, residual, ghosts, staged, sems,
+    members, cap, from_first, from_second, state, gi, tables, x, residual, velocity, ghosts, staged, sems,
 ):
     lane = lane_id()
-    ghost = step_ghosts(members, cap, near, from_first, from_second, Table(tables), ghosts, lane)
-    copies = []
+    out = pltpu.make_async_copy(x, velocity, sems.at[3])
+    out.start()
+    ghost = step_ghosts(members, cap, None, from_first, from_second, Table(tables), ghosts, lane, None, (4, 5))
+    copies = [out]
     for c in range(3):
         for m in range(TILES):
-            r = add_ends(c, m, state[R + c, :, tile(m)], ghost, gi)
-            staged[c, :, tile(m)] = add_side(c, m, r, ghost, gk, gj, lane)
+            staged[c, :, tile(m)] = add_ends(c, m, state[R + c, :, tile(m)], ghost, gi)
         copies.append(pltpu.make_async_copy(staged.at[c], residual.at[c], sems.at[c]))
-        copies[c].start()
+        copies[-1].start()
     for copy in copies:
         copy.wait()
 
@@ -819,15 +820,16 @@
         {len(parts): 0, len(parts) + 8: 7},
     )(*parts, state, eff, inverse, gk, gj, gi, tables, chosen, x)
     state, x, (near, from_first, from_second) = steps(state, sent, x, lift, unknowns)
-    state, velocity = inside(state, x, final=True)
-    residual = call(
-        gathered(last_kernel, members, cap),
-        [VMEM] * (near_refs + 7),
-        [field],
-        [HBM],
-        ghost_scratch + field_scratch,
+    state, x = inside(state, x)
+    state = side(near, state)
+    residual, velocity = call(
+        functools.partial(last_kernel, members, cap),
+        [VMEM] * 6,
+        [field, field],
+        [HBM, HBM],
+        ghost_scratch + [scratch(3, BLK, CELLS), pltpu.SemaphoreType.DMA((4,))],
         "last",
-    )(*near, from_first, from_second, state, gk, gj, gi, tables)[0]
+    )(from_first, from_second, state, gi, tables, x)
     return velocity, residual
 
 

time: 84.1 us -> 84 us (level)
    pallas_call x4 -> x5, Pallas kernels: 2.45 us -> 3.07 us  [side(): call(gathered(side_kernel, members, cap), [VMEM] * (near_refs + 4), [stat...]
where the time goes in v6:
time: 84 us; the launch traced here: 83.8 us
  starting transfers between devices  45.6 us (54%)
  waiting for transfers between devices  20.7 us (25%)
  Pallas kernels  13.9 us (17%)
  other arithmetic  1.67 us (2%)
  between operations  1.08 us (1%)
    ppermute x32, starting transfers between devices, swap(): return lax.ppermute(a, 'mem', [(m, m ^ bits) for m in range(members)])  30.4 us
    ppermute x32, waiting for transfers between devices, swap(): return lax.ppermute(a, 'mem', [(m, m ^ bits) for m in range(members)])  17 us
    ppermute x7, starting transfers between devices, spread(): first = lax.ppermute(first, ('grp', 'mem'), first_route)  15.2 us
    pallas_call x6, Pallas kernels, inside(): call(functools.partial(inside_kernel, x is None, bool(lift), final, membe...  4.08 us
    ppermute x7, waiting for transfers between devices, spread(): first = lax.ppermute(first, ('grp', 'mem'), first_route)  3.65 us
    pallas_call x4, Pallas kernels, outside(): call(functools.partial(outside_kernel, members, cap, old, new), [VMEM] *...  3.3 us
    pallas_call x5, Pallas kernels, side(): call(gathered(side_kernel, members, cap), [VMEM] * (near_refs + 4), [stat...  3.07 us
  transfers between devices with their start and end apart: 46, of which 19 were waited for; matrix products, arithmetic and copies ran while one was open for 0% of the time, Pallas kernels for 9%

profile of v6, /device:TPU:0, one launch (start us, length us, event | category | flops | bytes accessed | tf_op | source)
XLA Modules:
  0.0 83.8 jit_solution(3578596861644887915)
XLA Ops:
  5.3 2.9 %collective-permute-start.1 = (f32[2,72,128]{2,1,0:T(8,128)S(1)}, f32[2,72,128]{2,1,0:T(8,128)S(1)}, u32[]{:S(2)}, u32[]{:S(2)}) collective-permute-start(f32[2,72,128]{2,1,0:T(8,128)S(1)} %get-tuple-element.92), channel_id=1, source_target_pairs={{0,2},{1,3},{2,0},{3,1},{4,6},{5,7},{6,4},{7,5},{8,10},{9,11},{10,... | collective-permute-start | bytes 221192 | tf_op jit(solution)/shard_map/ppermute | solution.py:692
  8.2 1.5 %collective-permute-start.2 = (f32[2,72,128]{2,1,0:T(8,128)S(1)}, f32[2,72,128]{2,1,0:T(8,128)S(1)}, u32[]{:S(2)}, u32[]{:S(2)}) collective-permute-start(f32[2,72,128]{2,1,0:T(8,128)S(1)} %get-tuple-element.93), channel_id=1, source_target_pairs={{0,4},{1,5},{2,6},{3,7},{4,0},{5,1},{6,2},{7,3},{8,12},{9,13},{10,... | collective-permute-start | bytes 221192 | tf_op jit(solution)/shard_map/ppermute | solution.py:692
  9.7 2.0 %collective-permute-start.4 = (f32[16,128]{1,0:T(8,128)S(1)}, f32[16,128]{1,0:T(8,128)S(1)}, u32[]{:S(2)}, u32[]{:S(2)}) collective-permute-start(f32[16,128]{1,0:T(8,128)S(1)} %get-tuple-element.95), channel_id=1, source_target_pairs={{0,8},{1,9},{2,10},{3,11},{4,12},{5,13},{6,14},{7,15},{8,0},{9,1},... | collective-permute-start | bytes 24584 | tf_op jit(solution)/shard_map/ppermute | solution.py:695
  11.7 1.6 %collective-permute-done.4.refs_5_ = f32[16,128]{1,0:T(8,128)S(1)} collective-permute-done((f32[16,128]{1,0:T(8,128)S(1)}, f32[16,128]{1,0:T(8,128)S(1)}, u32[]{:S(2)}, u32[]{:S(2)}) %collective-permute-start.4) | collective-permute-done | bytes 8224 | tf_op jit(solution)/shard_map/ppermute | solution.py:695
  13.4 1.6 %collective-permute-done.3.refs_4_ = f32[2,72,128]{2,1,0:T(8,128)S(1)} collective-permute-done((f32[2,72,128]{2,1,0:T(8,128)S(1)}, f32[2,72,128]{2,1,0:T(8,128)S(1)}, u32[]{:S(2)}, u32[]{:S(2)}) %collective-permute-start.3) | collective-permute-done | bytes 73760 | tf_op jit(solution)/shard_map/ppermute | solution.py:692
  15.9 1.3 %collective-permute-done.8.got.refs_1_ = f32[4,48,128]{2,1,0:T(8,128)S(1)} collective-permute-done((f32[4,48,128]{2,1,0:T(8,128)S(1)}, f32[4,48,128]{2,1,0:T(8,128)S(1)}, u32[]{:S(2)}, u32[]{:S(2)}) %collective-permute-start.8) | collective-permute-done | bytes 98336 | tf_op jit(solution)/shard_map/ppermute | solution.py:692
  17.8 1.4 %collective-permute-start.10 = (f32[2,48,128]{2,1,0:T(8,128)S(1)}, f32[2,48,128]{2,1,0:T(8,128)S(1)}, u32[]{:S(2)}, u32[]{:S(2)}) collective-permute-start(f32[2,48,128]{2,1,0:T(8,128)S(1)} %get-tuple-element.103), channel_id=1, source_target_pairs={{0,4},{1,5},{2,6},{3,7},{4,0},{5,1},{6,2},{7,3},{8,12},{9,13},{10,... | collective-permute-start | bytes 147464 | tf_op jit(solution)/shard_map/ppermute | solution.py:692
  19.2 1.6 %collective-permute-start.11 = (f32[2,48,128]{2,1,0:T(8,128)S(1)}, f32[2,48,128]{2,1,0:T(8,128)S(1)}, u32[]{:S(2)}, u32[]{:S(2)}) collective-permute-start(f32[2,48,128]{2,1,0:T(8,128)S(1)} %get-tuple-element.104), channel_id=1, source_target_pairs={{0,6},{1,7},{2,4},{3,5},{4,2},{5,3},{6,0},{7,1},{8,14},{9,15},{10,... | collective-permute-start | bytes 147464 | tf_op jit(solution)/shard_map/ppermute | solution.py:692
  20.8 1.6 %collective-permute-start.6 = (f32[48,128]{1,0:T(8,128)S(1)}, f32[48,128]{1,0:T(8,128)S(1)}, u32[]{:S(2)}, u32[]{:S(2)}) collective-permute-start(f32[48,128]{1,0:T(8,128)S(1)} %get-tuple-element.98), channel_id=1, source_target_pairs={{0,8},{1,9},{2,10},{3,11},{4,12},{5,13},{6,14},{7,15},{8,0},{9,1},... | collective-permute-start | bytes 73736 | tf_op jit(solution)/shard_map/ppermute | solution.py:695
  27.7 1.5 %collective-permute-start.16 = (f32[2,48,128]{2,1,0:T(8,128)S(1)}, f32[2,48,128]{2,1,0:T(8,128)S(1)}, u32[]{:S(2)}, u32[]{:S(2)}) collective-permute-start(f32[2,48,128]{2,1,0:T(8,128)S(1)} %get-tuple-element.120), channel_id=1, source_target_pairs={{0,4},{1,5},{2,6},{3,7},{4,0},{5,1},{6,2},{7,3},{8,12},{9,13},{10,... | collective-permute-start | bytes 147464 | tf_op jit(solution)/shard_map/ppermute | solution.py:692
  30.4 2.7 %collective-permute-start.12 = (f32[48,128]{1,0:T(8,128)S(1)}, f32[48,128]{1,0:T(8,128)S(1)}, u32[]{:S(2)}, u32[]{:S(2)}) collective-permute-start(f32[48,128]{1,0:T(8,128)S(1)} %get-tuple-element.115), channel_id=1, source_target_pairs={{0,8},{1,9},{2,10},{3,11},{4,12},{5,13},{6,14},{7,15},{8,0},{9,1},... | collective-permute-start | bytes 73736 | tf_op jit(solution)/shard_map/ppermute | solution.py:695
  38.6 1.8 %collective-permute-start.23 = (f32[2,48,128]{2,1,0:T(8,128)S(1)}, f32[2,48,128]{2,1,0:T(8,128)S(1)}, u32[]{:S(2)}, u32[]{:S(2)}) collective-permute-start(f32[2,48,128]{2,1,0:T(8,128)S(1)} %get-tuple-element.132), channel_id=1, source_target_pairs={{0,6},{1,7},{2,4},{3,5},{4,2},{5,3},{6,0},{7,1},{8,14},{9,15},{10,... | collective-permute-start | bytes 147464 | tf_op jit(solution)/shard_map/ppermute | solution.py:692
  40.4 2.0 %collective-permute-start.18 = (f32[48,128]{1,0:T(8,128)S(1)}, f32[48,128]{1,0:T(8,128)S(1)}, u32[]{:S(2)}, u32[]{:S(2)}) collective-permute-start(f32[48,128]{1,0:T(8,128)S(1)} %get-tuple-element.126), channel_id=1, source_target_pairs={{0,8},{1,9},{2,10},{3,11},{4,12},{5,13},{6,14},{7,15},{8,0},{9,1},... | collective-permute-start | bytes 73736 | tf_op jit(solution)/shard_map/ppermute | solution.py:695
  45.9 1.8 %collective-permute-start.27 = (f32[8,128]{1,0:T(8,128)S(1)}, f32[8,128]{1,0:T(8,128)S(1)}, u32[]{:S(2)}, u32[]{:S(2)}) collective-permute-start(f32[8,128]{1,0:T(8,128)S(1)} %add.3.refs_0_), channel_id=1, source_target_pairs={{0,6},{1,7},{2,4},{3,5},{4,2},{5,3},{6,0},{7,1},{8,14},{9,15},{10,... | collective-permute-start | bytes 12296 | tf_op jit(solution)/shard_map/ppermute | solution.py:692
  52.5 1.3 %collective-permute-done.30.got.refs_1_ = f32[4,56,128]{2,1,0:T(8,128)S(1)} collective-permute-done((f32[4,56,128]{2,1,0:T(8,128)S(1)}, f32[4,56,128]{2,1,0:T(8,128)S(1)}, u32[]{:S(2)}, u32[]{:S(2)}) %collective-permute-start.30) | collective-permute-done | bytes 114720 | tf_op jit(solution)/shard_map/ppermute | solution.py:692
  55.9 1.4 %collective-permute-start.33 = (f32[2,56,128]{2,1,0:T(8,128)S(1)}, f32[2,56,128]{2,1,0:T(8,128)S(1)}, u32[]{:S(2)}, u32[]{:S(2)}) collective-permute-start(f32[2,56,128]{2,1,0:T(8,128)S(1)} %get-tuple-element.152), channel_id=1, source_target_pairs={{0,6},{1,7},{2,4},{3,5},{4,2},{5,3},{6,0},{7,1},{8,14},{9,15},{10,... | collective-permute-start | bytes 172040 | tf_op jit(solution)/shard_map/ppermute | solution.py:692
  57.4 2.4 %collective-permute-start.28 = (f32[80,128]{1,0:T(8,128)S(1)}, f32[80,128]{1,0:T(8,128)S(1)}, u32[]{:S(2)}, u32[]{:S(2)}) collective-permute-start(f32[80,128]{1,0:T(8,128)S(1)} %get-tuple-element.141), channel_id=1, source_target_pairs={{0,8},{1,9},{2,10},{3,11},{4,12},{5,13},{6,14},{7,15},{8,0},{9,1},... | collective-permute-start | bytes 122888 | tf_op jit(solution)/shard_map/ppermute | solution.py:695
  59.8 2.0 %collective-permute-done.28.refs_5_.from_first = f32[80,128]{1,0:T(8,128)S(1)} collective-permute-done((f32[80,128]{1,0:T(8,128)S(1)}, f32[80,128]{1,0:T(8,128)S(1)}, u32[]{:S(2)}, u32[]{:S(2)}) %collective-permute-start.28) | collective-permute-done | bytes 40992 | tf_op jit(solution)/shard_map/ppermute | solution.py:695
  62.5 1.6 %outside.6 = (f32[6,8,4096]{2,1,0:T(8,128)S(1)}, f32[4,48,128]{2,1,0:T(8,128)S(1)}, f32[4,48,128]{2,1,0:T(8,128)S(1)}, f32[48,128]{1,0:T(8,128)S(1)}, f32[48,128]{1,0:T(8,128)S(1)}, /*index=5*/f32[3,8,4096]{2,1,0:T(8,128)S(1)}) custom-call(f32[80,128]{1,0:T(8,128)S(1)} %collective-permute-done.28.refs_5_.from_first, ...), custom_call_target="tpu_custom_call", output_to_operand_aliasing={{0}: (2, {}), {5}: (7, {})} | custom-call | flops 2000000 | bytes 2000000 | tf_op jit(solution)/shard_map/outside/pallas_call | solution.py:768
  65.4 1.6 %collective-permute-start.37 = (f32[2,48,128]{2,1,0:T(8,128)S(1)}, f32[2,48,128]{2,1,0:T(8,128)S(1)}, u32[]{:S(2)}, u32[]{:S(2)}) collective-permute-start(f32[2,48,128]{2,1,0:T(8,128)S(1)} %get-tuple-element.158), channel_id=1, source_target_pairs={{0,2},{1,3},{2,0},{3,1},{4,6},{5,7},{6,4},{7,5},{8,10},{9,11},{10,... | collective-permute-start | bytes 147464 | tf_op jit(solution)/shard_map/ppermute | solution.py:692
  67.5 1.5 %collective-permute-start.39 = (f32[2,48,128]{2,1,0:T(8,128)S(1)}, f32[2,48,128]{2,1,0:T(8,128)S(1)}, u32[]{:S(2)}, u32[]{:S(2)}) collective-permute-start(f32[2,48,128]{2,1,0:T(8,128)S(1)} %get-tuple-element.160), channel_id=1, source_target_pairs={{0,6},{1,7},{2,4},{3,5},{4,2},{5,3},{6,0},{7,1},{8,14},{9,15},{10,... | collective-permute-start | bytes 147464 | tf_op jit(solution)/shard_map/ppermute | solution.py:692
  69.0 2.3 %collective-permute-start.34 = (f32[48,128]{1,0:T(8,128)S(1)}, f32[48,128]{1,0:T(8,128)S(1)}, u32[]{:S(2)}, u32[]{:S(2)}) collective-permute-start(f32[48,128]{1,0:T(8,128)S(1)} %get-tuple-element.154), channel_id=1, source_target_pairs={{0,8},{1,9},{2,10},{3,11},{4,12},{5,13},{6,14},{7,15},{8,0},{9,1},... | collective-permute-start | bytes 73736 | tf_op jit(solution)/shard_map/ppermute | solution.py:695
  77.2 1.4 %collective-permute-start.45 = (f32[2,48,128]{2,1,0:T(8,128)S(1)}, f32[2,48,128]{2,1,0:T(8,128)S(1)}, u32[]{:S(2)}, u32[]{:S(2)}) collective-permute-start(f32[2,48,128]{2,1,0:T(8,128)S(1)} %get-tuple-element.171), channel_id=1, source_target_pairs={{0,6},{1,7},{2,4},{3,5},{4,2},{5,3},{6,0},{7,1},{8,14},{9,15},{10,... | collective-permute-start | bytes 147464 | tf_op jit(solution)/shard_map/ppermute | solution.py:692
  78.7 2.2 %collective-permute-start.40 = (f32[48,128]{1,0:T(8,128)S(1)}, f32[48,128]{1,0:T(8,128)S(1)}, u32[]{:S(2)}, u32[]{:S(2)}) collective-permute-start(f32[48,128]{1,0:T(8,128)S(1)} %get-tuple-element.165), channel_id=1, source_target_pairs={{0,8},{1,9},{2,10},{3,11},{4,12},{5,13},{6,14},{7,15},{8,0},{9,1},... | collective-permute-start | bytes 73736 | tf_op jit(solution)/shard_map/ppermute | solution.py:695
  (109 shorter events, 39.8 us)
Async XLA Ops:
  5.3 8.1 %collective-permute-start.1 = (f32[2,72,128]{2,1,0:T(8,128)S(1)}, f32[2,72,128]{2,1,0:T(8,128)S(1)}, u32[]{:S(2)}, u32[]{:S(2)}) collective-permute-start(f32[2,72,128]{2,1,0:T(8,128)S(1)} %get-tuple-element.92), channel_id=1, source_target_pairs={{0,2},{1,3},{2,0},{3,1},{4,6},{5,7},{6,4},{7,5},{8,10},{9,11},{10,... | collective-permute-start | bytes 221192 | tf_op jit(solution)/shard_map/ppermute | solution.py:692
  8.2 5.2 %collective-permute-start.2 = (f32[2,72,128]{2,1,0:T(8,128)S(1)}, f32[2,72,128]{2,1,0:T(8,128)S(1)}, u32[]{:S(2)}, u32[]{:S(2)}) collective-permute-start(f32[2,72,128]{2,1,0:T(8,128)S(1)} %get-tuple-element.93), channel_id=1, source_target_pairs={{0,4},{1,5},{2,6},{3,7},{4,0},{5,1},{6,2},{7,3},{8,12},{9,13},{10,... | collective-permute-start | bytes 221192 | tf_op jit(solution)/shard_map/ppermute | solution.py:692
  9.7 5.3 %collective-permute-start.3 = (f32[2,72,128]{2,1,0:T(8,128)S(1)}, f32[2,72,128]{2,1,0:T(8,128)S(1)}, u32[]{:S(2)}, u32[]{:S(2)}) collective-permute-start(f32[2,72,128]{2,1,0:T(8,128)S(1)} %get-tuple-element.94), channel_id=1, source_target_pairs={{0,6},{1,7},{2,4},{3,5},{4,2},{5,3},{6,0},{7,1},{8,14},{9,15},{10,... | collective-permute-start | bytes 221192 | tf_op jit(solution)/shard_map/ppermute | solution.py:692
  17.2 5.9 %collective-permute-start.9 = (f32[2,48,128]{2,1,0:T(8,128)S(1)}, f32[2,48,128]{2,1,0:T(8,128)S(1)}, u32[]{:S(2)}, u32[]{:S(2)}) collective-permute-start(f32[2,48,128]{2,1,0:T(8,128)S(1)} %get-tuple-element.102), channel_id=1, source_target_pairs={{0,2},{1,3},{2,0},{3,1},{4,6},{5,7},{6,4},{7,5},{8,10},{9,11},{10,... | collective-permute-start | bytes 147464 | tf_op jit(solution)/shard_map/ppermute | solution.py:692
  17.8 5.3 %collective-permute-start.10 = (f32[2,48,128]{2,1,0:T(8,128)S(1)}, f32[2,48,128]{2,1,0:T(8,128)S(1)}, u32[]{:S(2)}, u32[]{:S(2)}) collective-permute-start(f32[2,48,128]{2,1,0:T(8,128)S(1)} %get-tuple-element.103), channel_id=1, source_target_pairs={{0,4},{1,5},{2,6},{3,7},{4,0},{5,1},{6,2},{7,3},{8,12},{9,13},{10,... | collective-permute-start | bytes 147464 | tf_op jit(solution)/shard_map/ppermute | solution.py:692
  19.2 5.0 %collective-permute-start.11 = (f32[2,48,128]{2,1,0:T(8,128)S(1)}, f32[2,48,128]{2,1,0:T(8,128)S(1)}, u32[]{:S(2)}, u32[]{:S(2)}) collective-permute-start(f32[2,48,128]{2,1,0:T(8,128)S(1)} %get-tuple-element.104), channel_id=1, source_target_pairs={{0,6},{1,7},{2,4},{3,5},{4,2},{5,3},{6,0},{7,1},{8,14},{9,15},{10,... | collective-permute-start | bytes 147464 | tf_op jit(solution)/shard_map/ppermute | solution.py:692
  26.8 6.9 %collective-permute-start.15 = (f32[2,48,128]{2,1,0:T(8,128)S(1)}, f32[2,48,128]{2,1,0:T(8,128)S(1)}, u32[]{:S(2)}, u32[]{:S(2)}) collective-permute-start(f32[2,48,128]{2,1,0:T(8,128)S(1)} %get-tuple-element.119), channel_id=1, source_target_pairs={{0,2},{1,3},{2,0},{3,1},{4,6},{5,7},{6,4},{7,5},{8,10},{9,11},{10,... | collective-permute-start | bytes 147464 | tf_op jit(solution)/shard_map/ppermute | solution.py:692
  27.7 6.0 %collective-permute-start.16 = (f32[2,48,128]{2,1,0:T(8,128)S(1)}, f32[2,48,128]{2,1,0:T(8,128)S(1)}, u32[]{:S(2)}, u32[]{:S(2)}) collective-permute-start(f32[2,48,128]{2,1,0:T(8,128)S(1)} %get-tuple-element.120), channel_id=1, source_target_pairs={{0,4},{1,5},{2,6},{3,7},{4,0},{5,1},{6,2},{7,3},{8,12},{9,13},{10,... | collective-permute-start | bytes 147464 | tf_op jit(solution)/shard_map/ppermute | solution.py:692
  29.2 5.0 %collective-permute-start.17 = (f32[2,48,128]{2,1,0:T(8,128)S(1)}, f32[2,48,128]{2,1,0:T(8,128)S(1)}, u32[]{:S(2)}, u32[]{:S(2)}) collective-permute-start(f32[2,48,128]{2,1,0:T(8,128)S(1)} %get-tuple-element.121), channel_id=1, source_target_pairs={{0,6},{1,7},{2,4},{3,5},{4,2},{5,3},{6,0},{7,1},{8,14},{9,15},{10,... | collective-permute-start | bytes 147464 | tf_op jit(solution)/shard_map/ppermute | solution.py:692
  30.4 4.5 %collective-permute-start.12 = (f32[48,128]{1,0:T(8,128)S(1)}, f32[48,128]{1,0:T(8,128)S(1)}, u32[]{:S(2)}, u32[]{:S(2)}) collective-permute-start(f32[48,128]{1,0:T(8,128)S(1)} %get-tuple-element.115), channel_id=1, source_target_pairs={{0,8},{1,9},{2,10},{3,11},{4,12},{5,13},{6,14},{7,15},{8,0},{9,1},... | collective-permute-start | bytes 73736 | tf_op jit(solution)/shard_map/ppermute | solution.py:695
  36.8 6.3 %collective-permute-start.21 = (f32[2,48,128]{2,1,0:T(8,128)S(1)}, f32[2,48,128]{2,1,0:T(8,128)S(1)}, u32[]{:S(2)}, u32[]{:S(2)}) collective-permute-start(f32[2,48,128]{2,1,0:T(8,128)S(1)} %get-tuple-element.130), channel_id=1, source_target_pairs={{0,2},{1,3},{2,0},{3,1},{4,6},{5,7},{6,4},{7,5},{8,10},{9,11},{10,... | collective-permute-start | bytes 147464 | tf_op jit(solution)/shard_map/ppermute | solution.py:692
  37.4 5.7 %collective-permute-start.22 = (f32[2,48,128]{2,1,0:T(8,128)S(1)}, f32[2,48,128]{2,1,0:T(8,128)S(1)}, u32[]{:S(2)}, u32[]{:S(2)}) collective-permute-start(f32[2,48,128]{2,1,0:T(8,128)S(1)} %get-tuple-element.131), channel_id=1, source_target_pairs={{0,4},{1,5},{2,6},{3,7},{4,0},{5,1},{6,2},{7,3},{8,12},{9,13},{10,... | collective-permute-start | bytes 147464 | tf_op jit(solution)/shard_map/ppermute | solution.py:692
  38.6 5.0 %collective-permute-start.23 = (f32[2,48,128]{2,1,0:T(8,128)S(1)}, f32[2,48,128]{2,1,0:T(8,128)S(1)}, u32[]{:S(2)}, u32[]{:S(2)}) collective-permute-start(f32[2,48,128]{2,1,0:T(8,128)S(1)} %get-tuple-element.132), channel_id=1, source_target_pairs={{0,6},{1,7},{2,4},{3,5},{4,2},{5,3},{6,0},{7,1},{8,14},{9,15},{10,... | collective-permute-start | bytes 147464 | tf_op jit(solution)/shard_map/ppermute | solution.py:692
  45.9 4.5 %collective-permute-start.27 = (f32[8,128]{1,0:T(8,128)S(1)}, f32[8,128]{1,0:T(8,128)S(1)}, u32[]{:S(2)}, u32[]{:S(2)}) collective-permute-start(f32[8,128]{1,0:T(8,128)S(1)} %add.3.refs_0_), channel_id=1, source_target_pairs={{0,6},{1,7},{2,4},{3,5},{4,2},{5,3},{6,0},{7,1},{8,14},{9,15},{10,... | collective-permute-start | bytes 12296 | tf_op jit(solution)/shard_map/ppermute | solution.py:692
  53.8 8.6 %collective-permute-start.31 = (f32[2,56,128]{2,1,0:T(8,128)S(1)}, f32[2,56,128]{2,1,0:T(8,128)S(1)}, u32[]{:S(2)}, u32[]{:S(2)}) collective-permute-start(f32[2,56,128]{2,1,0:T(8,128)S(1)} %get-tuple-element.150), channel_id=1, source_target_pairs={{0,2},{1,3},{2,0},{3,1},{4,6},{5,7},{6,4},{7,5},{8,10},{9,11},{10,... | collective-permute-start | bytes 172040 | tf_op jit(solution)/shard_map/ppermute | solution.py:692
  55.1 7.4 %collective-permute-start.32 = (f32[2,56,128]{2,1,0:T(8,128)S(1)}, f32[2,56,128]{2,1,0:T(8,128)S(1)}, u32[]{:S(2)}, u32[]{:S(2)}) collective-permute-start(f32[2,56,128]{2,1,0:T(8,128)S(1)} %get-tuple-element.151), channel_id=1, source_target_pairs={{0,4},{1,5},{2,6},{3,7},{4,0},{5,1},{6,2},{7,3},{8,12},{9,13},{10,... | collective-permute-start | bytes 172040 | tf_op jit(solution)/shard_map/ppermute | solution.py:692
  55.9 6.5 %collective-permute-start.33 = (f32[2,56,128]{2,1,0:T(8,128)S(1)}, f32[2,56,128]{2,1,0:T(8,128)S(1)}, u32[]{:S(2)}, u32[]{:S(2)}) collective-permute-start(f32[2,56,128]{2,1,0:T(8,128)S(1)} %get-tuple-element.152), channel_id=1, source_target_pairs={{0,6},{1,7},{2,4},{3,5},{4,2},{5,3},{6,0},{7,1},{8,14},{9,15},{10,... | collective-permute-start | bytes 172040 | tf_op jit(solution)/shard_map/ppermute | solution.py:692
  57.4 4.4 %collective-permute-start.28 = (f32[80,128]{1,0:T(8,128)S(1)}, f32[80,128]{1,0:T(8,128)S(1)}, u32[]{:S(2)}, u32[]{:S(2)}) collective-permute-start(f32[80,128]{1,0:T(8,128)S(1)} %get-tuple-element.141), channel_id=1, source_target_pairs={{0,8},{1,9},{2,10},{3,11},{4,12},{5,13},{6,14},{7,15},{8,0},{9,1},... | collective-permute-start | bytes 122888 | tf_op jit(solution)/shard_map/ppermute | solution.py:695
  65.4 6.5 %collective-permute-start.37 = (f32[2,48,128]{2,1,0:T(8,128)S(1)}, f32[2,48,128]{2,1,0:T(8,128)S(1)}, u32[]{:S(2)}, u32[]{:S(2)}) collective-permute-start(f32[2,48,128]{2,1,0:T(8,128)S(1)} %get-tuple-element.158), channel_id=1, source_target_pairs={{0,2},{1,3},{2,0},{3,1},{4,6},{5,7},{6,4},{7,5},{8,10},{9,11},{10,... | collective-permute-start | bytes 147464 | tf_op jit(solution)/shard_map/ppermute | solution.py:692
  67.0 5.0 %collective-permute-start.38 = (f32[2,48,128]{2,1,0:T(8,128)S(1)}, f32[2,48,128]{2,1,0:T(8,128)S(1)}, u32[]{:S(2)}, u32[]{:S(2)}) collective-permute-start(f32[2,48,128]{2,1,0:T(8,128)S(1)} %get-tuple-element.159), channel_id=1, source_target_pairs={{0,4},{1,5},{2,6},{3,7},{4,0},{5,1},{6,2},{7,3},{8,12},{9,13},{10,... | collective-permute-start | bytes 147464 | tf_op jit(solution)/shard_map/ppermute | solution.py:692
  67.5 5.0 %collective-permute-start.39 = (f32[2,48,128]{2,1,0:T(8,128)S(1)}, f32[2,48,128]{2,1,0:T(8,128)S(1)}, u32[]{:S(2)}, u32[]{:S(2)}) collective-permute-start(f32[2,48,128]{2,1,0:T(8,128)S(1)} %get-tuple-element.160), channel_id=1, source_target_pairs={{0,6},{1,7},{2,4},{3,5},{4,2},{5,3},{6,0},{7,1},{8,14},{9,15},{10,... | collective-permute-start | bytes 147464 | tf_op jit(solution)/shard_map/ppermute | solution.py:692
  75.1 6.4 %collective-permute-start.43 = (f32[2,48,128]{2,1,0:T(8,128)S(1)}, f32[2,48,128]{2,1,0:T(8,128)S(1)}, u32[]{:S(2)}, u32[]{:S(2)}) collective-permute-start(f32[2,48,128]{2,1,0:T(8,128)S(1)} %get-tuple-element.169), channel_id=1, source_target_pairs={{0,2},{1,3},{2,0},{3,1},{4,6},{5,7},{6,4},{7,5},{8,10},{9,11},{10,... | collective-permute-start | bytes 147464 | tf_op jit(solution)/shard_map/ppermute | solution.py:692
  76.4 5.2 %collective-permute-start.44 = (f32[2,48,128]{2,1,0:T(8,128)S(1)}, f32[2,48,128]{2,1,0:T(8,128)S(1)}, u32[]{:S(2)}, u32[]{:S(2)}) collective-permute-start(f32[2,48,128]{2,1,0:T(8,128)S(1)} %get-tuple-element.170), channel_id=1, source_target_pairs={{0,4},{1,5},{2,6},{3,7},{4,0},{5,1},{6,2},{7,3},{8,12},{9,13},{10,... | collective-permute-start | bytes 147464 | tf_op jit(solution)/shard_map/ppermute | solution.py:692
  77.2 5.0 %collective-permute-start.45 = (f32[2,48,128]{2,1,0:T(8,128)S(1)}, f32[2,48,128]{2,1,0:T(8,128)S(1)}, u32[]{:S(2)}, u32[]{:S(2)}) collective-permute-start(f32[2,48,128]{2,1,0:T(8,128)S(1)} %get-tuple-element.171), channel_id=1, source_target_pairs={{0,6},{1,7},{2,4},{3,5},{4,2},{5,3},{6,0},{7,1},{8,14},{9,15},{10,... | collective-permute-start | bytes 147464 | tf_op jit(solution)/shard_map/ppermute | solution.py:692
  (27 other events, 75.2 us)
